TPU v7x, 512 devices: a whole 4x8x8 slice. The times are simulated.
512 devices in a mesh: section: 8 (over y), dp: 16 (over z, core), mp: 4 (over x).
Axes of the slice: x: 4, y: 8, z: 8, core: 2. Of those that a mesh axis runs over, the one named last changes fastest.
Arguments:
- activations: bfloat16 [8, 2, 2048, 8192], P('section', None, 'dp', 'mp'), may hold values from -6 to 6
- cotangent: bfloat16 [8, 2, 2048, 1024], P('section', None, 'dp', 'mp'), may hold values from -6 to 6
- base_weight: bfloat16 [8, 8192, 1024], P('section', 'mp', 'dp'), may hold values from -0.0625 to 0.0625
- adapter_down: bfloat16 [8, 32, 8192, 64], P('section', 'dp', 'mp'), may hold values from -0.0625 to 0.0625
- adapter_up: bfloat16 [8, 32, 64, 1024], P('section', 'dp', None, 'mp'), may hold values from -0.75 to 0.75
- slot_language: int32 [8, 32], P('section'), may hold values from 0 to 31, each once within a row
- block_language: int32 [8, 2, 16], P('section', None, 'dp'), may hold values from 0 to 32, as said below
Outputs:
- layer_out: bfloat16 [8, 2, 2048, 1024], P('section', None, 'dp', 'mp')
- input_gradient: bfloat16 [8, 2, 2048, 8192], P('section', None, 'dp', 'mp')
- grad_sum: float32 [8, 32, 64, 1024], P('section', 'dp', None, 'mp')
- grad_square: float32 [8, 32, 64, 1024], P('section', 'dp', None, 'mp')
Inputs may be any that keep to these rules, and one draw needn't show every extreme that they name: `block_language`: within each micro-batch of a section the ids never fall along the blocks; padding blocks (32) stand at the end, one or more in every micro-batch, and at least 8 blocks are live.
All inputs are finite; a program needn't handle non-finite values.
Results may differ from a plain program's by a relative error of at most 0.011.
Values may be sent and summed in bfloat16 or wider, within the bound.
No kernel may reach another device: no remote copies, remote signals or barrier semaphores. Data moves between devices by JAX's collectives and lax.ppermute only.
A program may use at most 64 MiB of HBM per device.

v0:
```python
import jax
import jax.numpy as jnp
from jax import lax
from jax.sharding import PartitionSpec as P

BLOCK_ROWS = 128


adapter_scale = 2.0


def passed_along(array, axis, by):
    devices = lax.axis_size(axis)
    return lax.ppermute(array, axis, [(i, (i + by) % devices) for i in range(devices)])


def shards(
    activations, cotangent, base_weight, adapter_down, adapter_up, slot_language, block_language
):
    arrived = passed_along(activations, "section", 1)[0]
    returned = passed_along(cotangent, "section", -1)[0]
    micro_count, tok_rows, width_portion = arrived.shape
    column_portion = returned.shape[2]
    row_count = micro_count * tok_rows
    number_blocks = row_count // BLOCK_ROWS
    slot_table = slot_language[0]
    lane_ids = jnp.arange(slot_table.shape[0], dtype=jnp.int32)
    block_langs = block_language[0].reshape(number_blocks)
    slot_match = slot_table[None, :] == block_langs[:, None]
    live_blocks = jnp.any(slot_match, axis=1)
    slot_index = jnp.sum(jnp.where(slot_match, lane_ids[None, :], 0), axis=1)
    whole_weight = lax.all_gather(base_weight[0], "dp", axis=1, tiled=True)
    flat_acts = arrived.reshape(row_count, width_portion)
    frozen_output = lax.psum_scatter(
        jnp.dot(flat_acts, whole_weight, preferred_element_type=jnp.float32).astype(jnp.bfloat16),
        "mp",
        scatter_dimension=1,
        tiled=True,
    ).astype(jnp.float32)
    all_cots = lax.all_gather(returned, "mp", axis=2, tiled=True).reshape(
        row_count, whole_weight.shape[1]
    )
    frozen_backward = lax.dot_general(
        all_cots, whole_weight, (((1,), (1,)), ((), ())), preferred_element_type=jnp.float32
    )
    acts_blocks = flat_acts.reshape(number_blocks, BLOCK_ROWS, width_portion)
    down_all, up_all = (
        lax.all_gather(adapter_down[0], "dp", axis=0, tiled=True),
        lax.all_gather(adapter_up[0], "dp", axis=0, tiled=True),
    )
    block_down_weight = down_all[slot_index]
    block_up_weight = up_all[slot_index]
    down_part = jnp.einsum(
        "nbd,ndr->nbr", acts_blocks, block_down_weight, preferred_element_type=jnp.float32
    )
    up_part = jnp.einsum(
        "nbk,nrk->nbr", returned, block_up_weight, preferred_element_type=jnp.float32
    )
    down_sum, up_sum = lax.psum((down_part, up_part), "mp")
    down_rank_weight = down_sum.astype(jnp.bfloat16)
    up_rank_weight = up_sum.astype(jnp.bfloat16)
    adapter_backward = (
        adapter_scale
        * jnp.einsum(
            "tks,tjs->tkj", up_rank_weight, block_down_weight, preferred_element_type=jnp.float32
        )
    ).astype(jnp.bfloat16)
    retain_mask = live_blocks[:, None, None]
    forward_pass = frozen_output.reshape(
        number_blocks, BLOCK_ROWS, column_portion
    ) + adapter_scale * jnp.einsum(
        "pqe,pec->pqc", down_rank_weight, block_up_weight, preferred_element_type=jnp.float32
    )
    layer_out = (
        jnp.where(retain_mask, forward_pass, 0.0)
        .astype(jnp.bfloat16)
        .reshape(1, micro_count, tok_rows, column_portion)
    )
    reverse_pass = frozen_backward.reshape(
        number_blocks, BLOCK_ROWS, width_portion
    ) + adapter_backward.astype(jnp.float32)
    input_gradient = (
        jnp.where(retain_mask, reverse_pass, 0.0)
        .astype(jnp.bfloat16)
        .reshape(1, micro_count, tok_rows, width_portion)
    )
    block_gradient = (
        adapter_scale
        / BLOCK_ROWS
        * jnp.einsum("sdi,sdj->sij", down_rank_weight, returned, preferred_element_type=jnp.float32)
    )
    local_grads = jnp.einsum(
        "nl,nrk->lrk",
        slot_match.astype(jnp.float32),
        block_gradient,
        precision=lax.Precision.HIGHEST,
    )
    owner_count = lax.axis_size("dp")
    grouped = local_grads.reshape(
        owner_count, local_grads.shape[0] // owner_count, local_grads.shape[1], local_grads.shape[2]
    )
    owner_view = lax.all_to_all(grouped, "dp", split_axis=0, concat_axis=0, tiled=True)
    grad_sum = jnp.sum(owner_view, axis=0)
    grad_square = jnp.sum(owner_view * owner_view, axis=0)
    return (layer_out, input_gradient, grad_sum[None], grad_square[None])


def solution(mesh):
    in_specs = (
        P("section", None, "dp", "mp"),
        P("section", None, "dp", "mp"),
        P("section", "mp", "dp"),
        P("section", "dp", "mp", None),
        P("section", "dp", None, "mp"),
        P("section", None),
        P("section", None, "dp"),
    )
    out_specs = (
        P("section", None, "dp", "mp"),
        P("section", None, "dp", "mp"),
        P("section", "dp", None, "mp"),
        P("section", "dp", None, "mp"),
    )
    return jax.shard_map(shards, mesh=mesh, in_specs=in_specs, out_specs=out_specs, check_vma=False)
```

profile of v0, /device:TPU:1, one launch (start us, length us, event | category | flops | bytes accessed | tf_op | source)
XLA Modules:
  0.0 223.7 jit_solution(13991410778048564114)
XLA Ops:
  7.2 0.7 all-gather.12.cloned.1.call-update
  7.9 0.7 all-gather.10.cloned.1.call-update
  8.7 0.7 all-gather.8.cloned.1.call-update
  9.4 4.0 %collective-permute-start = (bf16[1,2,128,2048]{3,2,1,0:T(8,128)(2,1)}, bf16[1,2,128,2048]{3,2,1,0:T(8,128)(2,1)S(1)}, u32[]{:S(2)}, u32[]{:S(2)}) collective-permute-start(bf16[1,2,128,2048]{3,2,1,0:T(8,128)(2,1)} %param.7), channel_id=1, source_target_pairs={{0,64},{64,128},{128,192},{192,256},{256,320},{320,384},{384,448},... | collective-permute-start | bytes 3145736 | tf_op jit(solution)/shard_map/ppermute | solution.py:14
  13.4 3.8 %collective-permute-start.1 = (bf16[1,2,128,256]{3,2,1,0:T(8,128)(2,1)}, bf16[1,2,128,256]{3,2,1,0:T(8,128)(2,1)S(1)}, u32[]{:S(2)}, u32[]{:S(2)}) collective-permute-start(bf16[1,2,128,256]{3,2,1,0:T(8,128)(2,1)} %param.8), channel_id=1, source_target_pairs={{0,448},{64,0},{128,64},{192,128},{256,192},{320,256},{384,320},{4... | collective-permute-start | bytes 393224 | tf_op jit(solution)/shard_map/ppermute | solution.py:14
  17.2 0.9 fusion.34
  18.1 39.9 %all-gather.12.cloned.1.call-done = bf16[1,32,64,256]{3,2,0,1:T(8,128)(2,1)} async-done(((bf16[1,2,64,256]{3,2,0,1:T(8,128)(2,1)}), bf16[1,32,64,256]{3,2,0,1:T(8,128)(2,1)}) %all-gather.12.cloned.1.call-update) | async-done | bytes 1048592 | tf_op jit(solution)/shard_map/all_gather | solution.py:49
  58.0 1.8 gather_fusion.1
  59.8 0.2 convolution_bitcast_fusion.1
  60.0 57.5 %all-gather.10.cloned.1.call-done = bf16[1,32,2048,64]{2,3,0,1:T(8,128)(2,1)} async-done(((bf16[1,2,2048,64]{2,3,0,1:T(8,128)(2,1)}), bf16[1,32,2048,64]{2,3,0,1:T(8,128)(2,1)}) %all-gather.10.cloned.1.call-update) | async-done | bytes 8388624 | tf_op jit(solution)/shard_map/all_gather | solution.py:48
  117.6 4.0 %gather_fusion = bf16[2,2048,64]{1,2,0:T(8,128)(2,1)S(1)} fusion(bf16[32,2048,64]{1,2,0:T(8,128)(2,1)} %bitcast.72, s32[1024]{0:T(1024)S(1)} %pad_clamp_fusion), kind=kCustom, calls=%fused_computation | custom fusion | bytes 1048584 | tf_op jit(solution)/shard_map/gather | solution.py:51
  121.6 0.5 convolution_bitcast_fusion
  122.1 15.5 %all-reduce.2 = (bf16[2,128,64]{1,2,0:T(8,128)(2,1)S(1)}, bf16[2,128,64]{1,2,0:T(8,128)(2,1)}) all-reduce(f32[2,128,64]{1,2,0:T(8,128)S(1)} %convolution_bitcast_fusion, f32[2,128,64]{1,2,0:T(8,128)S(1)} %convolution_bitcast_fusion.1), channel_id=1, replica_groups=mesh['section'=8,'dp'=16,'mp'=4] {'mp'}, use_global_device_ids=true, to_apply=%region_3.4 | all-reduce | flops 32768 | bytes 196608 | tf_op jit(solution)/shard_map/psum | solution.py:59
  137.6 0.6 copy-done.2
  138.2 0.2 convolution_multiply_fusion.2
  138.4 1.1 fusion.29
  139.5 2.3 %reshape.46 = f32[16,2,64,256]{3,1,0,2:T(2,128)} reshape(f32[32,64,256]{2,0,1:T(8,128)S(1)} %fusion.29) | data formatting | bytes 4194304 | tf_op jit(solution)/shard_map/reshape | solution.py:99
  141.8 4.0 %copy.24 = f32[16,2,64,256]{3,1,2,0:T(2,128)} copy(f32[16,2,64,256]{3,1,0,2:T(2,128)} %reshape.46) | data formatting | bytes 4194304 | tf_op jit(solution)/shard_map/reshape | solution.py:99
  145.8 7.7 %all-to-all-start = ((f32[16,2,64,256]{3,1,2,0:T(2,128)}), f32[16,2,64,256]{3,1,2,0:T(2,128)S(1)}, u32[]{:S(2)}, u32[]{:S(2)}) async-start(f32[16,2,64,256]{3,1,2,0:T(2,128)} %copy.24), calls=%async_computation.1 | async-start | bytes 4194304 | tf_op jit(solution)/shard_map/all_to_all | solution.py:102
  153.6 20.4 %all-gather.8.cloned.1.call-done = bf16[1,2048,1024]{1,2,0:T(8,128)(2,1)} async-done(((bf16[1,2048,64]{1,2,0:T(8,128)(2,1)}), bf16[1,2048,1024]{1,2,0:T(8,128)(2,1)}) %all-gather.8.cloned.1.call-update) | async-done | bytes 4194320 | tf_op jit(solution)/shard_map/all_gather | solution.py:32
  173.9 4.6 %fusion.19 = bf16[256,1024]{1,0:T(8,128)(2,1)} fusion(bf16[256,2048]{1,0:T(8,128)(2,1)} %bitcast.67, bf16[1,2048,1024]{1,2,0:T(8,128)(2,1)} %all-gather.8.cloned.1.call-done), kind=kOutput, calls=%fused_computation.15 | convolution fusion | flops 1074003968 | bytes 5767168 | tf_op jit(solution)/shard_map/dot_general | solution.py:35
  178.6 0.2 compare_reduce_fusion
  178.7 18.1 %all-gather.3 = bf16[1,2,128,1024]{3,2,1,0:T(8,128)(2,1)S(1)} all-gather(bf16[1,2,128,256]{3,2,1,0:T(8,128)(2,1)S(1)} %collective-permute-done.1), channel_id=5, replica_groups=mesh['section'=8,'dp'=16,'mp'=4] {'mp'}, dimensions={3}, use_global_device_ids=true | all-gather | bytes 655360 | tf_op jit(solution)/shard_map/all_gather | solution.py:40
  196.8 1.1 convolution_multiply_fusion.1
  197.9 9.5 %reduce-scatter.2.cloned.1.call-done = bf16[256,256]{1,0:T(8,128)(2,1)} async-done(((bf16[256,1024]{1,0:T(8,128)(2,1)}), bf16[256,256]{1,0:T(8,128)(2,1)}) %reduce-scatter.2.cloned.1.call-update) | async-done | bytes 131088 | tf_op jit(solution)/shard_map/reduce_scatter | solution.py:34
  207.4 1.6 fusion.26
  209.1 1.2 fusion.11
  210.3 4.5 %fusion.15 = bf16[1,2,128,2048]{3,2,1,0:T(8,128)(2,1)} fusion(f32[2,128,2048]{2,1,0:T(8,128)S(1)} %fusion.11, bf16[1,2048,1024]{1,2,0:T(8,128)(2,1)} %all-gather.8.cloned.1.call-done, pred[2]{0:T(512)(128)(4,1)S(1)} %compare_reduce_fusion, bf16[1,2,128,1024]{3,2,1,0:T(8,128)(2,1)S(1)} %all-gather.3), kind=kOutput, calls=%fused_computation.12 | convolution fusion | flops 1075314688 | bytes 7864322 | tf_op jit(solution)/shard_map/dot_general | solution.py:43
  214.8 0.8 reduce_sum.31
  215.6 0.7 copy.29
  216.3 0.1 fusion.18
  216.5 0.7 copy.30
  (20 shorter events, 0.3 us)
Async XLA Ops:
  7.2 50.9 %all-gather.12.cloned.1.call-start = ((), (), s32[]{:S(2)}) async-start(), calls=%async_computation.5 | async-start | bytes 1114112 | tf_op jit(solution)/shard_map/all_gather | solution.py:49
  7.9 109.7 %all-gather.10.cloned.1.call-start = ((), (), s32[]{:S(2)}) async-start(), calls=%async_computation.4 | async-start | bytes 8912896 | tf_op jit(solution)/shard_map/all_gather | solution.py:48
  8.6 165.3 %all-gather.8.cloned.1.call-start = ((), (), s32[]{:S(2)}) async-start(), calls=%async_computation.3 | async-start | bytes 4456448 | tf_op jit(solution)/shard_map/all_gather | solution.py:32
  9.4 112.2 %collective-permute-start = (bf16[1,2,128,2048]{3,2,1,0:T(8,128)(2,1)}, bf16[1,2,128,2048]{3,2,1,0:T(8,128)(2,1)S(1)}, u32[]{:S(2)}, u32[]{:S(2)}) collective-permute-start(bf16[1,2,128,2048]{3,2,1,0:T(8,128)(2,1)} %param.7), channel_id=1, source_target_pairs={{0,64},{64,128},{128,192},{192,256},{256,320},{320,384},{384,448},... | collective-permute-start | bytes 3145736 | tf_op jit(solution)/shard_map/ppermute | solution.py:14
  13.4 46.4 %collective-permute-start.1 = (bf16[1,2,128,256]{3,2,1,0:T(8,128)(2,1)}, bf16[1,2,128,256]{3,2,1,0:T(8,128)(2,1)S(1)}, u32[]{:S(2)}, u32[]{:S(2)}) collective-permute-start(bf16[1,2,128,256]{3,2,1,0:T(8,128)(2,1)} %param.8), channel_id=1, source_target_pairs={{0,448},{64,0},{128,64},{192,128},{256,192},{320,256},{384,320},{4... | collective-permute-start | bytes 393224 | tf_op jit(solution)/shard_map/ppermute | solution.py:14
  59.8 57.8 %copy-start.1 = (bf16[2,64,256]{2,1,0:T(8,128)(2,1)}, bf16[2,64,256]{2,1,0:T(8,128)(2,1)S(1)}, u32[]{:S(2)}) copy-start(bf16[2,64,256]{2,1,0:T(8,128)(2,1)S(1)} %gather_fusion.1) | copy-start | bytes 196612
  60.0 78.4 %copy-start.3 = (s32[1,32]{1,0:T(1,128)S(1)}, s32[1,32]{1,0:T(1,128)}, u32[]{:S(2)}) copy-start(s32[1,32]{1,0:T(1,128)} %param.12) | copy-start | bytes 388
  60.0 78.4 %copy-start.4 = (s32[1,2,1]{1,2,0:T(1,128)S(1)}, s32[1,2,1]{1,2,0:T(1,128)}, u32[]{:S(2)}) copy-start(s32[1,2,1]{1,2,0:T(1,128)} %param.13) | copy-start | bytes 28
  121.6 16.0 %copy-start = (bf16[1,2,128,2048]{3,2,1,0:T(8,128)(2,1)}, bf16[1,2,128,2048]{3,2,1,0:T(8,128)(2,1)S(1)}, u32[]{:S(2)}) copy-start(bf16[1,2,128,2048]{3,2,1,0:T(8,128)(2,1)S(1)} %collective-permute-done) | copy-start | bytes 3145732
  137.6 0.6 copy-start.2
  145.8 69.0 %all-to-all-start = ((f32[16,2,64,256]{3,1,2,0:T(2,128)}), f32[16,2,64,256]{3,1,2,0:T(2,128)S(1)}, u32[]{:S(2)}, u32[]{:S(2)}) async-start(f32[16,2,64,256]{3,1,2,0:T(2,128)} %copy.24), calls=%async_computation.1 | async-start | bytes 4194304 | tf_op jit(solution)/shard_map/all_to_all | solution.py:102
  153.5 53.9 %reduce-scatter.2.cloned.1.call-start = ((), (), s32[]{:S(2)}) async-start(), calls=%async_computation.2 | async-start | bytes 655360 | tf_op jit(solution)/shard_map/reduce_scatter | solution.py:34
Sparse Core Ops, SparseCore 0:
  10.1 47.8 all-gather.11
  60.2 57.3 all-gather.9
  119.7 54.1 all-gather.7
  178.7 28.7 reduce-scatter.1
where the time goes:
time: 225 us; the launch traced here: 224 us
  waiting for transfers between devices  129 us (57%)
  blocking collectives  33.6 us (15%)
  starting transfers between devices  15.7 us (7%)
  local copies, waits for them, and re-layouts  14.1 us (6%)
  between operations  13.9 us (6%)
  matrix products  13.3 us (6%)
  other arithmetic  3.64 us (2%)
    all_gather x1, waiting for transfers between devices, shards(): lax.all_gather(adapter_down[0], 'dp', axis=0, tiled=True)  57.5 us
    all_gather x1, waiting for transfers between devices, shards(): lax.all_gather(adapter_up[0], 'dp', axis=0, tiled=True)  39.9 us
    all_gather x1, waiting for transfers between devices, shards(): whole_weight = lax.all_gather(base_weight[0], 'dp', axis=1, tiled=True)  20.4 us
    all_gather x1, blocking collectives, shards(): lax.all_gather(returned, 'mp', axis=2, tiled=True)  18.1 us
    psum x1, blocking collectives, shards(): down_sum, up_sum = lax.psum((down_part, up_part), 'mp')  15.5 us
    reduce_scatter x1, waiting for transfers between devices, shards(): lax.psum_scatter(jnp.dot(flat_acts, whole_weight, preferred_element_type=...  9.55 us
    ppermute x2, starting transfers between devices, passed_along(): lax.ppermute(array, axis, [(i, (i + by) % devices) for i in range(devices)])  7.85 us
    all_to_all x1, starting transfers between devices, shards(): lax.all_to_all(grouped, 'dp', split_axis=0, concat_axis=0, tiled=True)  7.71 us
  transfers between devices with their start and end apart: 7, of which 4 were waited for; matrix products, arithmetic and copies ran while one was open for 13% of the time, Pallas kernels for 0%

commit v1 on v0

v1 whole, which is shorter than its diff:
```python
import jax
import jax.numpy as jnp
from jax import lax
from jax.sharding import PartitionSpec as P

BLOCK_ROWS = 128
LANES = 128

adapter_scale = 2.0


def passed_along(array, axis, by):
    devices = lax.axis_size(axis)
    return lax.ppermute(array, axis, [(i, (i + by) % devices) for i in range(devices)])


def shards(
    activations, cotangent, base_weight, adapter_down, adapter_up, slot_language, block_language
):
    bf16, f32 = jnp.bfloat16, jnp.float32
    holders = lax.axis_size("dp")
    quarters = lax.axis_size("mp")
    own_slots, width, rank = adapter_down.shape[1:]
    columns = adapter_up.shape[3]
    micro = activations.shape[1]
    rows = micro * BLOCK_ROWS
    piece = width // holders
    up_groups = holders // (columns // LANES)
    up_rows = rank // up_groups
    me = lax.axis_index("dp")

    arrived = passed_along(activations, "section", 1)[0]
    returned = passed_along(cotangent, "section", -1)[0]

    slot_table = slot_language[0]
    langs = block_language[0, :, 0]
    live = langs < slot_table.shape[0]

    down_pieces = (
        jnp.swapaxes(adapter_down[0], 1, 2)
        .reshape(own_slots, rank, holders, piece)
        .transpose(2, 0, 1, 3)
        .reshape(holders, own_slots * rank, piece)
    )
    up_pieces = (
        adapter_up[0]
        .reshape(own_slots, up_groups, up_rows, columns // LANES, LANES)
        .transpose(1, 3, 0, 2, 4)
        .reshape(holders, own_slots * up_rows, LANES)
    )
    lang_rows = jnp.broadcast_to(
        langs.astype(bf16)[None, :, None], (holders, micro, LANES)
    )
    lang_rows = jnp.pad(lang_rows, ((0, 0), (0, 16 - micro), (0, 0)))
    first = jnp.concatenate([down_pieces, up_pieces, lang_rows], axis=1)
    first = lax.all_to_all(first, "dp", split_axis=0, concat_axis=0, tiled=True)

    down_end = own_slots * rank
    up_end = down_end + own_slots * up_rows
    all_langs = first[:, up_end : up_end + micro, 0].astype(jnp.int32)
    match = all_langs.reshape(-1)[:, None] == slot_table[None, :]
    slots = jnp.sum(
        jnp.where(match, jnp.arange(slot_table.shape[0], dtype=jnp.int32)[None, :], 0), axis=1
    )
    held_down = first[:, :down_end].reshape(holders * own_slots, rank, piece)
    held_up = first[:, down_end:up_end].reshape(holders * own_slots, up_rows, LANES)
    second = jnp.concatenate(
        [
            held_down[slots].reshape(holders, micro * rank, piece),
            held_up[slots].reshape(holders, micro * up_rows, LANES),
        ],
        axis=1,
    )
    second = lax.all_to_all(second, "dp", split_axis=0, concat_axis=0, tiled=True)
    down = (
        second[:, : micro * rank]
        .reshape(holders, micro, rank, piece)
        .transpose(1, 2, 0, 3)
        .reshape(micro, rank, width)
    )
    up = (
        second[:, micro * rank :]
        .reshape(up_groups, columns // LANES, micro, up_rows, LANES)
        .transpose(2, 0, 3, 1, 4)
        .reshape(micro, rank, columns)
    )

    whole_weight = lax.all_gather(base_weight[0], "dp", axis=1, tiled=True)
    all_cots = lax.all_gather(returned, "mp", axis=2, tiled=True)
    flat_acts = arrived.reshape(rows, width)
    base_part = jnp.dot(flat_acts, whole_weight, preferred_element_type=f32).astype(bf16)
    base_part = base_part.reshape(rows, quarters, columns).transpose(1, 0, 2)
    base_parts = lax.all_to_all(base_part, "mp", split_axis=0, concat_axis=0, tiled=True)
    base = jnp.sum(base_parts.astype(f32), axis=0).reshape(micro, BLOCK_ROWS, columns)
    back_base = lax.dot_general(
        all_cots.reshape(rows, whole_weight.shape[1]),
        whole_weight,
        (((1,), (1,)), ((), ())),
        preferred_element_type=f32,
    ).reshape(micro, BLOCK_ROWS, width)

    down_part = jnp.einsum("nrd,nbd->nrb", down, arrived, preferred_element_type=f32)
    up_part = jnp.einsum("nrk,nbk->nrb", up, returned, preferred_element_type=f32)
    parts = jnp.stack([down_part, up_part]).astype(bf16)
    parts = lax.all_gather(parts, "mp", axis=0, tiled=False)
    ranks = jnp.sum(parts.astype(f32), axis=0).astype(bf16)
    rank_in, rank_back = ranks[0], ranks[1]

    keep = live[:, None, None]
    forward = base + adapter_scale * jnp.einsum(
        "nrb,nrc->nbc", rank_in, up, preferred_element_type=f32
    )
    layer_out = jnp.where(keep, forward, 0.0).astype(bf16)[None]
    lora_back = adapter_scale * jnp.einsum(
        "nrb,nrd->nbd", rank_back, down, preferred_element_type=f32
    )
    input_gradient = jnp.where(keep, back_base + lora_back, 0.0).astype(bf16)[None]

    block_gradient = (
        adapter_scale
        / BLOCK_ROWS
        * jnp.einsum("nrb,nbc->nrc", rank_in, returned, preferred_element_type=f32)
    ).astype(bf16)
    gathered = lax.all_gather(block_gradient, "dp", axis=0, tiled=False).astype(f32)
    own = lax.dynamic_slice_in_dim(slot_table, me * own_slots, own_slots)
    sums, squares = [], []
    for k in range(own_slots):
        hit = (all_langs == own[k])[:, :, None, None]
        partial = jnp.sum(jnp.where(hit, gathered, 0.0), axis=1)
        sums.append(jnp.sum(partial, axis=0))
        squares.append(jnp.sum(partial * partial, axis=0))
    return (layer_out, input_gradient, jnp.stack(sums)[None], jnp.stack(squares)[None])


def solution(mesh):
    in_specs = (
        P("section", None, "dp", "mp"),
        P("section", None, "dp", "mp"),
        P("section", "mp", "dp"),
        P("section", "dp", "mp", None),
        P("section", "dp", None, "mp"),
        P("section", None),
        P("section", None, "dp"),
    )
    out_specs = (
        P("section", None, "dp", "mp"),
        P("section", None, "dp", "mp"),
        P("section", "dp", None, "mp"),
        P("section", "dp", None, "mp"),
    )
    return jax.shard_map(shards, mesh=mesh, in_specs=in_specs, out_specs=out_specs, check_vma=False)
```

time: 225 us -> 206 us (0.916)
  waiting for transfers between devices: 129 us -> 99.8 us
  blocking collectives: 33.6 us -> 52.6 us
  local copies, waits for them, and re-layouts: 14.1 us -> 5.11 us
  other arithmetic: 3.64 us -> 8.03 us
  matrix products: 13.3 us -> 11 us
    all_gather x2 -> x1, waiting for transfers between devices: 97.5 us -> 30.8 us  [shards(): lax.all_gather(block_gradient, 'dp', axis=0, tiled=False).astype(f32)]
    all_to_all x0 -> x1, blocking collectives: none -> 31.9 us  [shards(): first = lax.all_to_all(first, 'dp', split_axis=0, concat_axis=0, tiled=True)]
    all_gather x1, waiting for transfers between devices: 20.4 us -> 42.4 us  [shards(): whole_weight = lax.all_gather(base_weight[0], 'dp', axis=1, tiled=True)]
    all_to_all x1 -> x2, waiting for transfers between devices: 0.01 us -> 16.1 us  [the longest x1 11.3 us: shards(): lax.all_to_all(second, 'dp', split_axis=0, concat_axis=0, tiled=True)]
    psum x1 -> x0, blocking collectives: 15.5 us -> none  [shards(): down_sum, up_sum = lax.psum((down_part, up_part), 'mp')]
    ppermute x2, waiting for transfers between devices: 0.01 us -> 9.71 us  [passed_along(): lax.ppermute(array, axis, [(i, (i + by) % devices) for i in range(devices)])]
    reduce_scatter x1 -> x0, waiting for transfers between devices: 9.55 us -> none  [shards(): lax.psum_scatter(jnp.dot(flat_acts, whole_weight, preferred_element_type=...]
    reshape x2 -> x4, local copies, waits for them, and re-layouts: 6.3 us -> 1.55 us  [the longest x1 0.85 us: shards(): base_part = base_part.reshape(rows, quarters, columns).transpose(1, 0, 2)]
  transfers between devices with their start and end apart: 7 -> 6, of which waited for: 4 -> 5; matrix products, arithmetic and copies ran while one was open for 13% -> 6% of each run, Pallas kernels for 0% -> 0%
where the time goes in v1:
time: 206 us
  waiting for transfers between devices  99.8 us (48%)
  blocking collectives  52.6 us (26%)
  starting transfers between devices  14.7 us (7%)
  between operations  14.3 us (7%)
  matrix products  11 us (5%)
  other arithmetic  8.03 us (4%)
  local copies, waits for them, and re-layouts  5.11 us (2%)
    all_gather x1, waiting for transfers between devices, shards(): whole_weight = lax.all_gather(base_weight[0], 'dp', axis=1, tiled=True)  42.4 us
    all_to_all x1, blocking collectives, shards(): first = lax.all_to_all(first, 'dp', split_axis=0, concat_axis=0, tiled=True)  31.9 us
    all_gather x1, waiting for transfers between devices, shards(): lax.all_gather(block_gradient, 'dp', axis=0, tiled=False).astype(f32)  30.8 us
    all_to_all x1, waiting for transfers between devices, shards(): lax.all_to_all(second, 'dp', split_axis=0, concat_axis=0, tiled=True)  11.3 us
    all_gather x1, blocking collectives, shards(): all_cots = lax.all_gather(returned, 'mp', axis=2, tiled=True)  10.6 us
    all_gather x1, blocking collectives, shards(): parts = lax.all_gather(parts, 'mp', axis=0, tiled=False)  10.1 us
    ppermute x2, waiting for transfers between devices, passed_along(): lax.ppermute(array, axis, [(i, (i + by) % devices) for i in range(devices)])  9.71 us
    ppermute x2, starting transfers between devices, passed_along(): lax.ppermute(array, axis, [(i, (i + by) % devices) for i in range(devices)])  7.02 us
  transfers between devices with their start and end apart: 6, of which 5 were waited for; matrix products, arithmetic and copies ran while one was open for 6% of the time, Pallas kernels for 0%

profile of v1, /device:TPU:1, one launch (start us, length us, event | category | flops | bytes accessed | tf_op | source)
XLA Modules:
  0.0 205.6 jit_solution(6399507893708853942)
XLA Ops:
  7.2 0.9 copy.69
  8.4 0.7 convert_bitcast_fusion
  9.3 31.9 %all_to_all.15 = bf16[16,160,128]{2,1,0:T(8,128)(2,1)S(1)} all-to-all(bf16[16,160,128]{2,1,0:T(8,128)(2,1)S(1)} %maximum_maximum_fusion), channel_id=1, replica_groups=mesh['section'=8,'dp'=16,'mp'=4] {'dp'}, dimensions={0} | all-to-all | bytes 1310720 | tf_op jit(solution)/shard_map/all_to_all | solution.py:56
  41.7 0.6 gather_fusion.1
  42.3 0.6 gather_fusion
  43.0 0.9 pad_maximum_fusion
  43.9 3.5 %all-to-all-start.2 = ((bf16[16,144,128]{2,1,0:T(8,128)(2,1)}), bf16[16,144,128]{2,1,0:T(8,128)(2,1)S(1)}, u32[]{:S(2)}, u32[]{:S(2)}) async-start(bf16[16,144,128]{2,1,0:T(8,128)(2,1)} %pad_maximum_fusion), calls=%async_computation.2 | async-start | bytes 1179648 | tf_op jit(solution)/shard_map/all_to_all | solution.py:74
  47.4 3.2 %collective-permute-start = (bf16[1,2,128,2048]{3,2,1,0:T(8,128)(2,1)}, bf16[1,2,128,2048]{3,2,1,0:T(8,128)(2,1)S(1)}, u32[]{:S(2)}, u32[]{:S(2)}) collective-permute-start(bf16[1,2,128,2048]{3,2,1,0:T(8,128)(2,1)} %param.7), channel_id=1, source_target_pairs={{0,64},{64,128},{128,192},{192,256},{256,320},{320,384},{384,448},... | collective-permute-start | bytes 3145736 | tf_op jit(solution)/shard_map/ppermute | solution.py:14
  50.6 3.8 %collective-permute-start.1 = (bf16[1,2,128,256]{3,2,1,0:T(8,128)(2,1)}, bf16[1,2,128,256]{3,2,1,0:T(8,128)(2,1)S(1)}, u32[]{:S(2)}, u32[]{:S(2)}) collective-permute-start(bf16[1,2,128,256]{3,2,1,0:T(8,128)(2,1)} %param.8), channel_id=1, source_target_pairs={{0,448},{64,0},{128,64},{192,128},{256,192},{320,256},{384,320},{4... | collective-permute-start | bytes 393224 | tf_op jit(solution)/shard_map/ppermute | solution.py:14
  54.4 11.3 %all-to-all-done.2 = bf16[16,144,128]{2,1,0:T(8,128)(2,1)S(1)} async-done(((bf16[16,144,128]{2,1,0:T(8,128)(2,1)}), bf16[16,144,128]{2,1,0:T(8,128)(2,1)S(1)}, u32[]{:S(2)}, u32[]{:S(2)}) %all-to-all-start.2) | async-done | bytes 589856 | tf_op jit(solution)/shard_map/all_to_all | solution.py:74
  65.8 0.3 copy.91
  66.6 9.7 %collective-permute-done = bf16[1,2,128,2048]{3,2,1,0:T(8,128)(2,1)S(1)} collective-permute-done((bf16[1,2,128,2048]{3,2,1,0:T(8,128)(2,1)}, bf16[1,2,128,2048]{3,2,1,0:T(8,128)(2,1)S(1)}, u32[]{:S(2)}, u32[]{:S(2)}) %collective-permute-start) | collective-permute-done | bytes 1048608 | tf_op jit(solution)/shard_map/ppermute | solution.py:14
  76.3 0.5 fusion.28
  76.8 10.1 %all_gather.17 = bf16[4,2,2,64,128]{4,3,2,1,0:T(8,128)(2,1)S(1)} all-gather(bf16[1,2,2,64,128]{4,3,2,1,0:T(8,128)(2,1)S(1)} %pad_maximum_fusion.1), channel_id=1, replica_groups=mesh['section'=8,'dp'=16,'mp'=4] {'mp'}, dimensions={0}, use_global_device_ids=true | all-gather | bytes 327680 | tf_op jit(solution)/shard_map/all_gather | solution.py:105
  87.0 0.8 fusion.27
  87.9 0.7 all-gather.6.cloned.1.call-update
  88.6 0.6 fusion.39
  89.2 10.6 %all-gather.1 = bf16[1,2,128,1024]{3,2,1,0:T(8,128)(2,1)} all-gather(bf16[1,2,128,256]{3,2,1,0:T(8,128)(2,1)S(1)} %collective-permute-done.1), channel_id=3, replica_groups=mesh['section'=8,'dp'=16,'mp'=4] {'mp'}, dimensions={3}, use_global_device_ids=true | all-gather | bytes 655360 | tf_op jit(solution)/shard_map/all_gather | solution.py:89
  99.9 1.3 compare_bitcast_fusion
  101.4 0.5 convolution_multiply_fusion
  101.9 30.8 %all-gather.8.cloned.1.call-done = bf16[32,64,256]{2,1,0:T(8,128)(2,1)} async-done(((bf16[2,64,256]{2,1,0:T(8,128)(2,1)}), bf16[32,64,256]{2,1,0:T(8,128)(2,1)}) %all-gather.8.cloned.1.call-update) | async-done | bytes 1048592 | tf_op jit(solution)/shard_map/all_gather | solution.py:124
  132.7 2.1 fusion.13
  134.8 0.7 maximum_bitcast_fusion
  135.6 0.7 maximum_bitcast_fusion.1
  136.2 42.4 %all-gather.6.cloned.1.call-done = bf16[1,2048,1024]{1,2,0:T(8,128)(2,1)} async-done(((bf16[1,2048,64]{1,2,0:T(8,128)(2,1)}), bf16[1,2048,1024]{1,2,0:T(8,128)(2,1)}) %all-gather.6.cloned.1.call-update) | async-done | bytes 4194320 | tf_op jit(solution)/shard_map/all_gather | solution.py:88
  178.6 3.8 %fusion.20 = bf16[256,1024]{1,0:T(8,128)(2,1)S(1)} fusion(bf16[256,2048]{1,0:T(8,128)(2,1)} %bitcast.127, bf16[1,2048,1024]{1,2,0:T(8,128)(2,1)} %all-gather.6.cloned.1.call-done), kind=kOutput, calls=%fused_computation.17 | convolution fusion | flops 1074003968 | bytes 5767168 | tf_op jit(solution)/shard_map/dot_general | solution.py:91
  182.5 0.9 copy.90
  183.3 4.1 %all-to-all-start = ((bf16[4,256,256]{2,1,0:T(8,128)(2,1)}), bf16[4,256,256]{2,1,0:T(8,128)(2,1)}, u32[]{:S(2)}, u32[]{:S(2)}) async-start(bf16[4,256,256]{2,1,0:T(8,128)(2,1)} %bitcast.120), calls=%async_computation | async-start | bytes 1048576 | tf_op jit(solution)/shard_map/all_to_all | solution.py:93
  187.5 4.4 %fusion.17 = bf16[1,2,128,2048]{3,2,1,0:T(8,128)(2,1)} fusion(f32[2,128,2048]{2,1,0:T(8,128)S(1)} %convolution_multiply_fusion, bf16[1,2048,1024]{1,2,0:T(8,128)(2,1)} %all-gather.6.cloned.1.call-done, pred[2]{0:T(512)(128)(4,1)S(1)} %compare_bitcast_fusion.2, bf16[1,2,128,1024]{3,2,1,0:T(8,128)(2,1)S(1)} %copy-done.1), kind=kOutput, calls=%fused_computation.16 | convolution fusion | flops 1075314688 | bytes 7864322 | tf_op jit(solution)/shard_map/dot_general | solution.py:95
  191.9 4.8 %all-to-all-done = bf16[4,256,256]{2,1,0:T(8,128)(2,1)} async-done(((bf16[4,256,256]{2,1,0:T(8,128)(2,1)}), bf16[4,256,256]{2,1,0:T(8,128)(2,1)}, u32[]{:S(2)}, u32[]{:S(2)}) %all-to-all-start) | async-done | bytes 524320 | tf_op jit(solution)/shard_map/all_to_all | solution.py:93
  196.7 1.1 convert_reduce_fusion
  197.8 0.9 fusion.26
  (38 shorter events, 2.1 us)
Async XLA Ops:
  7.2 1.1 copy-start
  7.2 34.3 %copy-start.3 = (s32[1,32]{1,0:T(1,128)S(1)}, s32[1,32]{1,0:T(1,128)}, u32[]{:S(2)}) copy-start(s32[1,32]{1,0:T(1,128)} %param.12) | copy-start | bytes 388
  43.9 21.9 %all-to-all-start.2 = ((bf16[16,144,128]{2,1,0:T(8,128)(2,1)}), bf16[16,144,128]{2,1,0:T(8,128)(2,1)S(1)}, u32[]{:S(2)}, u32[]{:S(2)}) async-start(bf16[16,144,128]{2,1,0:T(8,128)(2,1)} %pad_maximum_fusion), calls=%async_computation.2 | async-start | bytes 1179648 | tf_op jit(solution)/shard_map/all_to_all | solution.py:74
  47.3 85.4 %all-gather.8.cloned.1.call-start = ((), (), s32[]{:S(2)}) async-start(), calls=%async_computation.4 | async-start | bytes 1114112 | tf_op jit(solution)/shard_map/all_gather | solution.py:124
  47.4 28.9 %collective-permute-start = (bf16[1,2,128,2048]{3,2,1,0:T(8,128)(2,1)}, bf16[1,2,128,2048]{3,2,1,0:T(8,128)(2,1)S(1)}, u32[]{:S(2)}, u32[]{:S(2)}) collective-permute-start(bf16[1,2,128,2048]{3,2,1,0:T(8,128)(2,1)} %param.7), channel_id=1, source_target_pairs={{0,64},{64,128},{128,192},{192,256},{256,320},{320,384},{384,448},... | collective-permute-start | bytes 3145736 | tf_op jit(solution)/shard_map/ppermute | solution.py:14
  50.6 15.8 %collective-permute-start.1 = (bf16[1,2,128,256]{3,2,1,0:T(8,128)(2,1)}, bf16[1,2,128,256]{3,2,1,0:T(8,128)(2,1)S(1)}, u32[]{:S(2)}, u32[]{:S(2)}) collective-permute-start(bf16[1,2,128,256]{3,2,1,0:T(8,128)(2,1)} %param.8), channel_id=1, source_target_pairs={{0,448},{64,0},{128,64},{192,128},{256,192},{320,256},{384,320},{4... | collective-permute-start | bytes 393224 | tf_op jit(solution)/shard_map/ppermute | solution.py:14
  66.2 23.1 %copy-start.4 = (s32[1,2,1]{1,2,0:T(1,128)S(1)}, s32[1,2,1]{1,2,0:T(1,128)}, u32[]{:S(2)}) copy-start(s32[1,2,1]{1,2,0:T(1,128)} %param.13) | copy-start | bytes 28
  76.3 25.0 %copy-start.2 = (bf16[1,2,128,2048]{3,2,1,0:T(8,128)(2,1)}, bf16[1,2,128,2048]{3,2,1,0:T(8,128)(2,1)S(1)}, u32[]{:S(2)}) copy-start(bf16[1,2,128,2048]{3,2,1,0:T(8,128)(2,1)S(1)} %collective-permute-done) | copy-start | bytes 3145732
  87.8 90.8 %all-gather.6.cloned.1.call-start = ((), (), s32[]{:S(2)}) async-start(), calls=%async_computation.3 | async-start | bytes 4456448 | tf_op jit(solution)/shard_map/all_gather | solution.py:88
  182.4 5.0 %copy-start.1 = (bf16[1,2,128,1024]{3,2,1,0:T(8,128)(2,1)S(1)}, bf16[1,2,128,1024]{3,2,1,0:T(8,128)(2,1)}, u32[]{:S(2)}) copy-start(bf16[1,2,128,1024]{3,2,1,0:T(8,128)(2,1)} %all-gather.1) | copy-start | bytes 1572868
  183.3 13.4 %all-to-all-start = ((bf16[4,256,256]{2,1,0:T(8,128)(2,1)}), bf16[4,256,256]{2,1,0:T(8,128)(2,1)}, u32[]{:S(2)}, u32[]{:S(2)}) async-start(bf16[4,256,256]{2,1,0:T(8,128)(2,1)} %bitcast.120), calls=%async_computation | async-start | bytes 1048576 | tf_op jit(solution)/shard_map/all_to_all | solution.py:93
Sparse Core Ops, SparseCore 0:
  87.9 44.7 all-gather.7
  134.8 43.7 all-gather.5

commit v2 on v1

v2 whole, which is shorter than its diff:
```python
import functools

import jax
import jax.numpy as jnp
from jax import lax
from jax.experimental import pallas as pl
from jax.experimental.pallas import tpu as pltpu
from jax.sharding import PartitionSpec as P

BLOCK_ROWS = 128
LANES = 128

adapter_scale = 2.0

bf16, f32 = jnp.bfloat16, jnp.float32
VMEM_LIMIT = 24 * 1024 * 1024
WIDE_LIMIT = 60 * 1024 * 1024


def passed_along(array, axis, by):
    devices = lax.axis_size(axis)
    return lax.ppermute(array, axis, [(i, (i + by) % devices) for i in range(devices)])


def exchanged(array, axis):
    return lax.all_to_all(array, axis, split_axis=0, concat_axis=0, tiled=True)


def smem():
    return pl.BlockSpec(memory_space=pltpu.SMEM)


def params():
    return pltpu.CompilerParams(vmem_limit_bytes=VMEM_LIMIT)


def nt_dot(a, b):
    return lax.dot_general(a, b, (((1,), (1,)), ((), ())), preferred_element_type=f32)


def tn_dot(a, b):
    return lax.dot_general(a, b, (((0,), (0,)), ((), ())), preferred_element_type=f32)


def pack_kernel(halves, langs_ref, table_ref, down_ref, up_ref, out_ref):
    holders, payload, piece = out_ref.shape
    own_slots, rank, _ = down_ref.shape
    micro, count = langs_ref.shape[0], table_ref.shape[1]
    group = rank * halves // holders
    low, high = own_slots * rank, own_slots * (rank + group)
    match = table_ref[...] == langs_ref[...]
    lane = lax.broadcasted_iota(jnp.int32, (micro, count), 1)
    slots = jnp.min(jnp.where(match, lane, count), axis=1, keepdims=True).astype(f32)
    row = lax.broadcasted_iota(jnp.int32, (payload - high, piece), 0)
    marks = jnp.zeros((payload - high, piece), f32)
    for m in range(micro):
        marks = jnp.where(row == m, slots[m : m + 1], marks)
    marks = marks.astype(bf16)
    ups = [up_ref[k].astype(f32) for k in range(own_slots)]
    for p in range(holders):
        for k in range(own_slots):
            out_ref[p, k * rank : (k + 1) * rank, :] = down_ref[k, :, p * piece : (p + 1) * piece]
        top, left = (p // halves) * group, (p % halves) * LANES
        out_ref[p, low:high, :] = jnp.concatenate(
            [up[top : top + group, left : left + LANES] for up in ups], axis=0
        ).astype(bf16)
        out_ref[p, high:, :] = marks


def packed(langs, table, down, up, holders):
    own_slots, rank, width = down.shape
    halves = up.shape[2] // LANES
    payload = own_slots * (rank + rank * halves // holders) + 8
    out = (holders, payload, width // holders)
    return pl.pallas_call(
        functools.partial(pack_kernel, halves),
        grid=(1,),
        out_shape=jax.ShapeDtypeStruct(out, bf16),
        in_specs=[
            pl.BlockSpec(langs.shape, lambda i: (0, 0)),
            pl.BlockSpec(table.shape, lambda i: (0, 0)),
            pl.BlockSpec(down.shape, lambda i: (0, 0, 0)),
            pl.BlockSpec(up.shape, lambda i: (0, 0, 0)),
        ],
        out_specs=pl.BlockSpec(out, lambda i: (0, 0, 0)),
        compiler_params=pltpu.CompilerParams(vmem_limit_bytes=WIDE_LIMIT),
        name="packed_adapters",
    )(langs, table, down, up)


def base_kernel(micro, first_ref, *refs):
    acts, gathered_ref, outs = refs[:micro], refs[micro], refs[micro + 1 :]
    weight = gathered_ref[...].reshape(-1, gathered_ref.shape[2])
    for k, out_ref in enumerate(outs):

        @pl.when(pl.program_id(0) == k)
        def _():
            for m in range(micro):
                out_ref[m] = nt_dot(acts[m][0, 0], weight).astype(bf16)


def base_products(first, acts, gathered, quarters):
    micro = len(acts)
    width = gathered.shape[2]
    holders, cols = gathered.shape[:2]
    group = holders // quarters
    out = (micro, BLOCK_ROWS, group * cols)
    return pl.pallas_call(
        functools.partial(base_kernel, micro),
        grid_spec=pltpu.PrefetchScalarGridSpec(
            num_scalar_prefetch=1,
            grid=(quarters,),
            in_specs=[pl.BlockSpec(acts[0].shape, lambda i, first_ref: (0, 0, 0, 0))] * micro
            + [
                pl.BlockSpec(
                    (group, cols, width),
                    lambda i, first_ref: (lax.rem(first_ref[0] + i, quarters), 0, 0),
                ),
            ],
            out_specs=(pl.BlockSpec(out, lambda i, first_ref: (0, 0, 0)),) * quarters,
        ),
        out_shape=(jax.ShapeDtypeStruct(out, bf16),) * quarters,
        compiler_params=params(),
        cost_estimate=pl.CostEstimate(
            flops=2 * micro * BLOCK_ROWS * width * cols * holders,
            bytes_accessed=2 * holders * cols * (width + 2 * micro * BLOCK_ROWS),
            transcendentals=0,
        ),
        name="base_products",
    )(first, *acts, gathered)


def part_kernel(micro, second_ref, returned_ref, *refs):
    acts, parts_ref, up_ref = refs[:micro], refs[micro], refs[micro + 1]
    pieces, _, piece = second_ref.shape
    rank, columns = up_ref.shape[1:]
    halves = columns // LANES
    group = rank * halves // pieces
    for p in range(pieces):
        both = second_ref[p, micro * rank :, :].astype(f32)
        top, left = (p // halves) * group, (p % halves) * LANES
        for m in range(micro):
            up_ref[m, top : top + group, left : left + LANES] = both[m * group : (m + 1) * group]
    for m in range(micro):
        down = jnp.concatenate(
            [second_ref[p, m * rank : (m + 1) * rank, :] for p in range(pieces)], axis=1
        )
        parts = (
            nt_dot(down, acts[m][0, 0]).astype(bf16),
            nt_dot(up_ref[m].astype(bf16), returned_ref[m]).astype(bf16),
        )
        for q in range(parts_ref.shape[0]):
            for kind in range(2):
                parts_ref[q, kind, m] = parts[kind]


def rank_parts(second, returned, acts, rank, quarters):
    micro, _, columns = returned.shape
    return pl.pallas_call(
        functools.partial(part_kernel, micro),
        out_shape=(
            jax.ShapeDtypeStruct((quarters, 2, micro, rank, BLOCK_ROWS), bf16),
            jax.ShapeDtypeStruct((micro, rank, columns), f32),
        ),
        in_specs=[pl.BlockSpec(memory_space=pltpu.VMEM)] * (2 + micro),
        out_specs=(pl.BlockSpec(memory_space=pltpu.VMEM),) * 2,
        compiler_params=params(),
        name="rank_parts",
    )(second, returned, *acts)


def select_kernel(micro, own_slots, rank, slots_ref, first_ref, out_ref):
    holders = out_ref.shape[0]
    group = out_ref.shape[1] // micro - rank
    low = own_slots * rank
    for d in range(holders):
        ups = []
        for m in range(micro):
            slot = jnp.minimum(slots_ref[d * micro + m], holders * own_slots - 1)
            owner, k = slot // own_slots, slot % own_slots
            rows = pl.ds(pl.multiple_of(k * rank, rank), rank)
            out_ref[d, m * rank : (m + 1) * rank, :] = first_ref[owner, rows, :]
            held = first_ref[owner, low : low + own_slots * group, :].astype(f32)
            up = held[:group]
            for j in range(1, own_slots):
                up = jnp.where(k == j, held[j * group : (j + 1) * group], up)
            ups.append(up)
        out_ref[d, micro * rank :, :] = jnp.concatenate(ups, axis=0).astype(bf16)


def selected(slots, first, micro, own_slots, rank, group):
    holders, _, lanes = first.shape
    return pl.pallas_call(
        functools.partial(select_kernel, micro, own_slots, rank),
        out_shape=jax.ShapeDtypeStruct((holders, micro * (rank + group), lanes), bf16),
        in_specs=[smem(), pl.BlockSpec(memory_space=pltpu.VMEM)],
        out_specs=pl.BlockSpec(memory_space=pltpu.VMEM),
        compiler_params=params(),
        name="selected_pieces",
    )(slots, first)


def gradient_kernel(micro, live_ref, cots_ref, ranks_ref, down_ref, gathered_ref, out_ref):
    rank = ranks_ref.shape[1]
    pieces = down_ref.shape[0]
    cots = jnp.concatenate([cots_ref[q] for q in range(cots_ref.shape[0])], axis=1)
    weight = gathered_ref[...].reshape(-1, gathered_ref.shape[2])
    total = jnp.dot(cots, weight, preferred_element_type=f32)
    for m in range(micro):
        back = (adapter_scale * ranks_ref[m].astype(f32)).T.astype(bf16)
        down = jnp.concatenate(
            [down_ref[p, m * rank : (m + 1) * rank, :] for p in range(pieces)], axis=1
        )
        lora = jnp.dot(back, down, preferred_element_type=f32).astype(bf16).astype(f32)
        part = total[m * BLOCK_ROWS : (m + 1) * BLOCK_ROWS] + lora
        out_ref[m] = jnp.where(live_ref[m] > 0, part, 0.0).astype(bf16)


def input_gradients(live, cots, ranks, second, gathered):
    micro, rank = ranks.shape[:2]
    holders, cols, width = gathered.shape
    pieces, _, piece = second.shape
    steps = 4
    return pl.pallas_call(
        functools.partial(gradient_kernel, micro),
        grid=(steps,),
        out_shape=jax.ShapeDtypeStruct((micro, BLOCK_ROWS, width), bf16),
        in_specs=[
            smem(),
            pl.BlockSpec(cots.shape, lambda i: (0, 0, 0)),
            pl.BlockSpec(ranks.shape, lambda i: (0, 0, 0)),
            pl.BlockSpec((pieces // steps, micro * rank, piece), lambda i: (i, 0, 0)),
            pl.BlockSpec((holders, cols, width // steps), lambda i: (0, 0, i)),
        ],
        out_specs=pl.BlockSpec((micro, BLOCK_ROWS, width // steps), lambda i: (0, 0, i)),
        compiler_params=params(),
        cost_estimate=pl.CostEstimate(
            flops=2 * micro * BLOCK_ROWS * width * cols * holders,
            bytes_accessed=2 * (2 * micro * BLOCK_ROWS * width + holders * cols * width),
            transcendentals=0,
        ),
        name="input_gradients",
    )(live, cots, ranks, second, gathered)


def layer_kernel(micro, live_ref, ranks_ref, up_ref, *refs):
    out_ref = refs[-1]
    for m in range(micro):
        total = adapter_scale * tn_dot(ranks_ref[m], up_ref[m].astype(bf16))
        for part_ref in refs[:-1]:
            total += part_ref[m].astype(f32)
        out_ref[m] = jnp.where(live_ref[m] > 0, total, 0.0).astype(bf16)


def layer_outputs(live, ranks, up, parts):
    micro, _, columns = up.shape
    return pl.pallas_call(
        functools.partial(layer_kernel, micro),
        out_shape=jax.ShapeDtypeStruct((micro, BLOCK_ROWS, columns), bf16),
        in_specs=[smem()] + [pl.BlockSpec(memory_space=pltpu.VMEM)] * (2 + len(parts)),
        out_specs=pl.BlockSpec(memory_space=pltpu.VMEM),
        compiler_params=params(),
        name="layer_outputs",
    )(live, ranks, up, *parts)


def rank_kernel(halves, parts_ref, incoming_ref, ranks_ref, pieces_ref):
    micro, rank = parts_ref.shape[2:4]
    total = parts_ref[0].astype(f32)
    for q in range(1, parts_ref.shape[0]):
        total += parts_ref[q].astype(f32)
    ranks_ref[...] = total.astype(bf16)
    grads = [
        jnp.dot(ranks_ref[0, m], incoming_ref[m], preferred_element_type=f32)
        * (adapter_scale / BLOCK_ROWS)
        for m in range(micro)
    ]
    holders = pieces_ref.shape[0]
    group = rank * halves // holders
    for p in range(holders):
        top, left = (p // halves) * group, (p % halves) * LANES
        pieces_ref[p] = jnp.concatenate(
            [g[top : top + group, left : left + LANES] for g in grads], axis=0
        ).astype(bf16)


def ranks_and_pieces(parts, incoming, holders):
    micro, rank = parts.shape[2:4]
    columns = incoming.shape[2]
    halves = columns // LANES
    group = rank * halves // holders
    return pl.pallas_call(
        functools.partial(rank_kernel, halves),
        out_shape=(
            jax.ShapeDtypeStruct(parts.shape[1:], bf16),
            jax.ShapeDtypeStruct((holders, micro * group, LANES), bf16),
        ),
        in_specs=[pl.BlockSpec(memory_space=pltpu.VMEM)] * 2,
        out_specs=(pl.BlockSpec(memory_space=pltpu.VMEM),) * 2,
        compiler_params=params(),
        name="ranks_and_pieces",
    )(parts, incoming)


def slot_kernel(micro, slots_ref, pieces_ref, out_ref):
    count = out_ref.shape[0]
    holders = pieces_ref.shape[0]
    group = pieces_ref.shape[1] // micro
    out_ref[...] = jnp.zeros_like(out_ref)
    for d in range(holders):
        both = pieces_ref[d].astype(f32)
        marks = [slots_ref[d * micro + m] for m in range(micro)]
        terms = [
            jnp.where(marks[m] < count, both[m * group : (m + 1) * group], 0.0)
            for m in range(micro)
        ]
        slots = [jnp.minimum(mark, count - 1) for mark in marks]
        for m in range(1, micro):
            for n in range(m):
                same = marks[m] == marks[n]
                terms[n] = terms[n] + jnp.where(same, terms[m], 0.0)
                terms[m] = jnp.where(same, 0.0, terms[m])
        for m in range(micro):
            out_ref[slots[m], 0] += terms[m]
            out_ref[slots[m], 1] += terms[m] * terms[m]


def slot_sums(slots, pieces, slot_count, micro):
    group = pieces.shape[1] // micro
    return pl.pallas_call(
        functools.partial(slot_kernel, micro),
        out_shape=jax.ShapeDtypeStruct((slot_count, 2, group, LANES), f32),
        in_specs=[smem(), pl.BlockSpec(memory_space=pltpu.VMEM)],
        out_specs=pl.BlockSpec(memory_space=pltpu.VMEM),
        compiler_params=params(),
        name="slot_sums",
    )(slots, pieces)


def place_kernel(halves, pieces_ref, sum_ref, square_ref):
    holders, own_slots, _, group = pieces_ref.shape[:4]
    for p in range(holders):
        top, left = (p // halves) * group, (p % halves) * LANES
        for k in range(own_slots):
            sum_ref[k, top : top + group, left : left + LANES] = pieces_ref[p, k, 0]
            square_ref[k, top : top + group, left : left + LANES] = pieces_ref[p, k, 1]


def placed(pieces, rank, columns):
    own_slots = pieces.shape[1]
    shape = jax.ShapeDtypeStruct((own_slots, rank, columns), f32)
    return pl.pallas_call(
        functools.partial(place_kernel, columns // LANES),
        out_shape=(shape, shape),
        in_specs=[pl.BlockSpec(memory_space=pltpu.VMEM)],
        out_specs=(pl.BlockSpec(memory_space=pltpu.VMEM),) * 2,
        compiler_params=params(),
        name="placed_sums",
    )(pieces)


def shards(
    activations, cotangent, base_weight, adapter_down, adapter_up, slot_language, block_language
):
    holders = lax.axis_size("dp")
    quarters = lax.axis_size("mp")
    own_slots, width, rank = adapter_down.shape[1:]
    columns = adapter_up.shape[3]
    micro = activations.shape[1]
    rows = micro * BLOCK_ROWS
    piece = width // holders
    up_groups = holders // (columns // LANES)
    up_rows = rank // up_groups
    me = lax.axis_index("dp")

    returned = passed_along(cotangent, "section", -1)[0]
    arrived = [passed_along(activations[:, m : m + 1], "section", 1) for m in range(micro)]

    slot_table = slot_language[0]
    langs = block_language[0, :, 0]
    live = (langs < slot_table.shape[0]).astype(jnp.int32)

    weight = jnp.swapaxes(base_weight[0], 0, 1)
    gathered = lax.all_gather(weight, "dp", axis=0)
    all_cots = lax.all_gather(returned.reshape(rows, columns), "mp", axis=0)

    first = packed(block_language[0], slot_language, jnp.swapaxes(adapter_down[0], 1, 2), adapter_up[0], holders)
    first = exchanged(first, "dp")

    marked = own_slots * (rank + up_rows)
    slots = first[:, marked : marked + micro, 0].astype(jnp.int32).reshape(-1)
    second = selected(slots, first, micro, own_slots, rank, up_rows)
    second, arrived[0] = lax.optimization_barrier((second, arrived[0]))
    second = exchanged(second, "dp")
    second, all_cots = lax.optimization_barrier((second, all_cots))

    parts, up = rank_parts(second, returned, arrived, rank, quarters)
    parts = exchanged(parts, "mp")
    quarter = lax.axis_index("mp").astype(jnp.int32).reshape(1)
    base_parts = base_products(quarter, arrived, gathered, quarters)
    parts, base_parts = lax.optimization_barrier((parts, base_parts))
    ranks, pieces = ranks_and_pieces(parts, returned, holders)
    rank_in, rank_back = ranks[0], ranks[1]

    pieces = exchanged(pieces, "dp")
    input_gradient = input_gradients(live, all_cots, rank_back, second, gathered)[None]
    pieces, input_gradient = lax.optimization_barrier((pieces, input_gradient))
    sums = slot_sums(slots, pieces, slot_table.shape[0], micro)
    sums, base_parts = lax.optimization_barrier((sums, base_parts))
    sums = exchanged(sums, "dp").reshape((holders, own_slots) + sums.shape[1:])
    base_parts = [base_parts[0]] + [
        lax.ppermute(base_parts[k], "mp", [(i, (i + k) % quarters) for i in range(quarters)])
        for k in range(1, quarters)
    ]
    layer_out = layer_outputs(live, rank_in, up, base_parts)[None]
    sums, layer_out = lax.optimization_barrier((sums, layer_out))
    grad_sum, grad_square = placed(sums, rank, columns)

    return (layer_out, input_gradient, grad_sum[None], grad_square[None])


def solution(mesh):
    in_specs = (
        P("section", None, "dp", "mp"),
        P("section", None, "dp", "mp"),
        P("section", "mp", "dp"),
        P("section", "dp", "mp", None),
        P("section", "dp", None, "mp"),
        P("section", None),
        P("section", None, "dp"),
    )
    out_specs = (
        P("section", None, "dp", "mp"),
        P("section", None, "dp", "mp"),
        P("section", "dp", None, "mp"),
        P("section", "dp", None, "mp"),
    )
    return jax.shard_map(shards, mesh=mesh, in_specs=in_specs, out_specs=out_specs, check_vma=False)
```

time: 206 us -> 136 us (0.66)
  the two profiles are of different devices: /device:TPU:1 before, /device:TPU:24 now
where the time goes in v2:
time: 136 us; the launch traced here: 135 us
  starting transfers between devices  55.6 us (41%)
  waiting for transfers between devices  28.3 us (21%)
  Pallas kernels  16.7 us (12%)
  between operations  14.2 us (10%)
  blocking collectives  13.1 us (10%)
  local copies, waits for them, and re-layouts  7.04 us (5%)
    all_to_all x5, starting transfers between devices, exchanged(): return lax.all_to_all(array, axis, split_axis=0, concat_axis=0, tiled=True)  33.2 us
    all_to_all x5, waiting for transfers between devices, exchanged(): return lax.all_to_all(array, axis, split_axis=0, concat_axis=0, tiled=True)  17.1 us
    all_gather x1, blocking collectives, shards(): all_cots = lax.all_gather(returned.reshape(rows, columns), 'mp', axis=0)  13.1 us
    ppermute x3, starting transfers between devices, passed_along(): lax.ppermute(array, axis, [(i, (i + by) % devices) for i in range(devices)])  11.4 us
    ppermute x3, starting transfers between devices, shards(): lax.ppermute(base_parts[k], 'mp', [(i, (i + k) % quarters) for i in range...  11 us
    ppermute x3, waiting for transfers between devices, passed_along(): lax.ppermute(array, axis, [(i, (i + by) % devices) for i in range(devices)])  6.73 us
    unnamed x8, local copies, waits for them, and re-layouts  4.37 us
    ppermute x3, waiting for transfers between devices, shards(): lax.ppermute(base_parts[k], 'mp', [(i, (i + k) % quarters) for i in range...  3.78 us
  transfers between devices with their start and end apart: 12, of which 6 were waited for; matrix products, arithmetic and copies ran while one was open for 2% of the time, Pallas kernels for 10%

profile of v2, /device:TPU:24, one launch (start us, length us, event | category | flops | bytes accessed | tf_op | source)
XLA Modules:
  0.0 135.3 jit_solution(15794601470473954204)
XLA Ops:
  7.2 0.7 all-gather.3.cloned.1.call-update
  7.9 1.3 copy.13.langs_ref
  9.2 2.1 %packed_adapters.1 = bf16[16,152,128]{2,1,0:T(8,128)(2,1)} custom-call(s32[2,1]{1,0:T(2,128)} %copy.13.langs_ref, s32[1,32]{1,0:T(1,128)} %table_ref.1, bf16[2,64,2048]{2,1,0:T(8,128)(2,1)} %bitcast.30, bf16[2,64,256]{2,1,0:T(8,128)(2,1)} %bitcast.33), custom_call_target="tpu_custom_call" | custom-call | tf_op jit(solution)/shard_map/packed_adapters/pallas_call | solution.py:75
  11.3 10.6 %all-to-all-start = ((bf16[16,152,128]{2,1,0:T(8,128)(2,1)}), bf16[16,152,128]{2,1,0:T(8,128)(2,1)S(1)}, u32[]{:S(2)}, u32[]{:S(2)}) async-start(bf16[16,152,128]{2,1,0:T(8,128)(2,1)} %packed_adapters.1), calls=%async_computation | async-start | bytes 1245184 | tf_op jit(solution)/shard_map/all_to_all | solution.py:26
  21.9 1.3 fusion.1
  23.2 4.7 %collective-permute-start = (bf16[1,1,128,2048]{3,2,1,0:T(8,128)(2,1)S(1)}, bf16[1,1,128,2048]{3,2,1,0:T(8,128)(2,1)S(1)}, u32[]{:S(2)}, u32[]{:S(2)}) collective-permute-start(bf16[1,1,128,2048]{3,2,1,0:T(8,128)(2,1)S(1)} %get-tuple-element.61), channel_id=1, source_target_pairs={{0,64},{64,128},{128,192},{192,256},{256,320},{320,384},{384,448},... | collective-permute-start | bytes 1572872 | tf_op jit(solution)/shard_map/ppermute | solution.py:22
  27.9 14.2 %all-to-all-done.first_ref = bf16[16,152,128]{2,1,0:T(8,128)(2,1)S(1)} async-done(((bf16[16,152,128]{2,1,0:T(8,128)(2,1)}), bf16[16,152,128]{2,1,0:T(8,128)(2,1)S(1)}, u32[]{:S(2)}, u32[]{:S(2)}) %all-to-all-start) | async-done | bytes 622624 | tf_op jit(solution)/shard_map/all_to_all | solution.py:26
  42.6 1.6 %selected_pieces.1 = bf16[16,144,128]{2,1,0:T(8,128)(2,1)} custom-call(s32[32]{0:T(128)S(1)} %reshape.24.slots_ref, bf16[16,152,128]{2,1,0:T(8,128)(2,1)S(1)} %all-to-all-done.first_ref), custom_call_target="tpu_custom_call" | custom-call | tf_op jit(solution)/shard_map/selected_pieces/pallas_call | solution.py:193
  44.2 6.2 %all-to-all-start.1 = ((bf16[16,144,128]{2,1,0:T(8,128)(2,1)}), bf16[16,144,128]{2,1,0:T(8,128)(2,1)S(1)}, u32[]{:S(2)}, u32[]{:S(2)}) async-start(bf16[16,144,128]{2,1,0:T(8,128)(2,1)} %selected_pieces.1), calls=%async_computation.1 | async-start | bytes 1179648 | tf_op jit(solution)/shard_map/all_to_all | solution.py:26
  50.4 4.8 %collective-permute-start.2 = (bf16[1,1,128,2048]{3,2,1,0:T(8,128)(2,1)S(1)}, bf16[1,1,128,2048]{3,2,1,0:T(8,128)(2,1)S(1)}, u32[]{:S(2)}, u32[]{:S(2)}) collective-permute-start(bf16[1,1,128,2048]{3,2,1,0:T(8,128)(2,1)S(1)} %get-tuple-element.60), channel_id=1, source_target_pairs={{0,64},{64,128},{128,192},{192,256},{256,320},{320,384},{384,448},... | collective-permute-start | bytes 1572872 | tf_op jit(solution)/shard_map/ppermute | solution.py:22
  55.2 1.9 %collective-permute-start.1 = (bf16[1,2,128,256]{3,2,1,0:T(8,128)(2,1)S(1)}, bf16[1,2,128,256]{3,2,1,0:T(8,128)(2,1)S(1)}, u32[]{:S(2)}, u32[]{:S(2)}) collective-permute-start(bf16[1,2,128,256]{3,2,1,0:T(8,128)(2,1)S(1)} %copy-done.2), channel_id=1, source_target_pairs={{0,448},{64,0},{128,64},{192,128},{256,192},{320,256},{384,320},{4... | collective-permute-start | bytes 393224 | tf_op jit(solution)/shard_map/ppermute | solution.py:22
  57.1 6.7 %collective-permute-done.1 = bf16[1,2,128,256]{3,2,1,0:T(8,128)(2,1)S(1)} collective-permute-done((bf16[1,2,128,256]{3,2,1,0:T(8,128)(2,1)S(1)}, bf16[1,2,128,256]{3,2,1,0:T(8,128)(2,1)S(1)}, u32[]{:S(2)}, u32[]{:S(2)}) %collective-permute-start.1) | collective-permute-done | bytes 131104 | tf_op jit(solution)/shard_map/ppermute | solution.py:22
  63.8 13.1 %all_gather.9.cots_ref = bf16[4,256,256]{2,1,0:T(8,128)(2,1)S(1)} all-gather(bf16[1,256,256]{2,1,0:T(8,128)(2,1)S(1)} %bitcast.25), channel_id=1, replica_groups=mesh['section'=8,'dp'=16,'mp'=4] {'mp'}, dimensions={0}, use_global_device_ids=true | all-gather | bytes 655360 | tf_op jit(solution)/shard_map/all_gather | solution.py:385
  77.0 1.2 rank_parts.1
  78.2 4.2 %all-to-all-start.2 = ((bf16[4,2,2,64,128]{4,3,2,1,0:T(8,128)(2,1)}), bf16[4,2,2,64,128]{4,3,2,1,0:T(8,128)(2,1)S(1)}, u32[]{:S(2)}, u32[]{:S(2)}) async-start(bf16[4,2,2,64,128]{4,3,2,1,0:T(8,128)(2,1)} %get-tuple-element.35), calls=%async_computation.2 | async-start | bytes 524288 | tf_op jit(solution)/shard_map/all_to_all | solution.py:26
  82.5 2.2 %copy-done = bf16[1024,2048]{1,0:T(8,128)(2,1)S(1)} copy-done((bf16[1024,2048]{1,0:T(8,128)(2,1)S(1)}, bf16[1024,2048]{1,0:T(8,128)(2,1)}, u32[]{:S(2)}) %copy-start) | copy-done | bytes 4194328
  84.7 3.6 %base_products.1 = (bf16[2,128,256]{2,1,0:T(8,128)(2,1)S(1)}, bf16[2,128,256]{2,1,0:T(8,128)(2,1)S(1)}, bf16[2,128,256]{2,1,0:T(8,128)(2,1)S(1)}, bf16[2,128,256]{2,1,0:T(8,128)(2,1)S(1)}) custom-call(s32[1]{0:T(128)} %bitcast.6.first_ref, bf16[1,1,128,2048]{3,2,1,0:T(8,128)(2,1)S(1)} %collective-permute-done.refs_0_, ...), custom_call_target="tpu_custom_call" | custom-call | flops 1073741824 | bytes 5242880 | tf_op jit(solution)/shard_map/base_products/pallas_call | solution.py:108
  88.3 0.9 all-to-all-done.2.parts_ref
  89.1 0.8 ranks_and_pieces.1
  89.9 7.0 %all-to-all-start.3 = ((bf16[16,16,128]{2,1,0:T(8,128)(2,1)}), bf16[16,16,128]{2,1,0:T(8,128)(2,1)S(1)}, u32[]{:S(2)}, u32[]{:S(2)}) async-start(bf16[16,16,128]{2,1,0:T(8,128)(2,1)} %get-tuple-element.41), calls=%async_computation.3 | async-start | bytes 131072 | tf_op jit(solution)/shard_map/all_to_all | solution.py:26
  97.0 2.2 %copy-done.1 = bf16[1024,2048]{1,0:T(8,128)(2,1)S(1)} copy-done((bf16[1024,2048]{1,0:T(8,128)(2,1)S(1)}, bf16[1024,2048]{1,0:T(8,128)(2,1)}, u32[]{:S(2)}) %copy-start.1) | copy-done | bytes 4194328
  99.2 3.7 %input_gradients.1 = bf16[2,128,2048]{2,1,0:T(8,128)(2,1)} custom-call(s32[2]{0:T(128)S(1)} %fusion.live_ref, bf16[4,256,256]{2,1,0:T(8,128)(2,1)S(1)} %all_gather.9.cots_ref, bf16[2,64,128]{2,1,0:T(8,128)(2,1)S(1)} %get-tuple-element.63.ranks_ref, bf16[16,144,128]{2,1,0:T(8,128)(2,1)S(1)} %all-to-all-done.1.second_ref.down_ref, ...), custom_call_target="tpu_custom_call" | custom-call | flops 1073741824 | bytes 6291456 | tf_op jit(solution)/shard_map/input_gradients/pallas_call | solution.py:224
  102.9 2.0 %all-to-all-done.3.pieces_ref = bf16[16,16,128]{2,1,0:T(8,128)(2,1)S(1)} async-done(((bf16[16,16,128]{2,1,0:T(8,128)(2,1)}), bf16[16,16,128]{2,1,0:T(8,128)(2,1)S(1)}, u32[]{:S(2)}, u32[]{:S(2)}) %all-to-all-start.3) | async-done | bytes 65568 | tf_op jit(solution)/shard_map/all_to_all | solution.py:26
  104.8 1.4 %slot_sums.1 = f32[32,2,8,128]{3,2,1,0:T(8,128)} custom-call(s32[32]{0:T(128)S(1)} %reshape.24.slots_ref, bf16[16,16,128]{2,1,0:T(8,128)(2,1)S(1)} %all-to-all-done.3.pieces_ref), custom_call_target="tpu_custom_call" | custom-call | tf_op jit(solution)/shard_map/slot_sums/pallas_call | solution.py:330
  106.2 5.3 %all-to-all-start.4 = ((f32[32,2,8,128]{3,2,1,0:T(8,128)}), f32[32,2,8,128]{3,2,1,0:T(8,128)S(1)}, u32[]{:S(2)}, u32[]{:S(2)}) async-start(f32[32,2,8,128]{3,2,1,0:T(8,128)} %slot_sums.1), calls=%async_computation.4 | async-start | bytes 524288 | tf_op jit(solution)/shard_map/all_to_all | solution.py:26
  111.5 3.1 %collective-permute-start.3 = (bf16[2,128,256]{2,1,0:T(8,128)(2,1)S(1)}, bf16[2,128,256]{2,1,0:T(8,128)(2,1)S(1)}, u32[]{:S(2)}, u32[]{:S(2)}) collective-permute-start(bf16[2,128,256]{2,1,0:T(8,128)(2,1)S(1)} %get-tuple-element.52), channel_id=1, source_target_pairs={{0,1},{1,2},{2,3},{3,0},{4,5},{5,6},{6,7},{7,4},{8,9},{9,10},{10,1... | collective-permute-start | bytes 393224 | tf_op jit(solution)/shard_map/ppermute | solution.py:412
  114.6 4.6 %collective-permute-start.4 = (bf16[2,128,256]{2,1,0:T(8,128)(2,1)S(1)}, bf16[2,128,256]{2,1,0:T(8,128)(2,1)S(1)}, u32[]{:S(2)}, u32[]{:S(2)}) collective-permute-start(bf16[2,128,256]{2,1,0:T(8,128)(2,1)S(1)} %get-tuple-element.53), channel_id=1, source_target_pairs={{0,2},{1,3},{2,0},{3,1},{4,6},{5,7},{6,4},{7,5},{8,10},{9,11},{10,... | collective-permute-start | bytes 393224 | tf_op jit(solution)/shard_map/ppermute | solution.py:412
  119.2 3.4 %collective-permute-start.5 = (bf16[2,128,256]{2,1,0:T(8,128)(2,1)S(1)}, bf16[2,128,256]{2,1,0:T(8,128)(2,1)S(1)}, u32[]{:S(2)}, u32[]{:S(2)}) collective-permute-start(bf16[2,128,256]{2,1,0:T(8,128)(2,1)S(1)} %get-tuple-element.54), channel_id=1, source_target_pairs={{0,3},{1,0},{2,1},{3,2},{4,7},{5,4},{6,5},{7,6},{8,11},{9,8},{10,9... | collective-permute-start | bytes 393224 | tf_op jit(solution)/shard_map/ppermute | solution.py:412
  122.5 1.3 collective-permute-done.4.refs_2_
  123.8 2.5 %collective-permute-done.5.refs_3_ = bf16[2,128,256]{2,1,0:T(8,128)(2,1)S(1)} collective-permute-done((bf16[2,128,256]{2,1,0:T(8,128)(2,1)S(1)}, bf16[2,128,256]{2,1,0:T(8,128)(2,1)S(1)}, u32[]{:S(2)}, u32[]{:S(2)}) %collective-permute-start.5) | collective-permute-done | bytes 131104 | tf_op jit(solution)/shard_map/ppermute | solution.py:412
  126.3 1.5 %layer_outputs.1 = bf16[2,128,256]{2,1,0:T(8,128)(2,1)} custom-call(s32[2]{0:T(128)S(1)} %fusion.live_ref, bf16[2,64,128]{2,1,0:T(8,128)(2,1)S(1)} %get-tuple-element.62.ranks_ref, f32[2,64,256]{2,1,0:T(8,128)S(1)} %get-tuple-element.50.up_ref, bf16[2,128,256]{2,1,0:T(8,128)(2,1)S(1)} %get-tuple-element.51.refs_0_, ...), custom_call_target="tpu_custom_call" | custom-call | tf_op jit(solution)/shard_map/layer_outputs/pallas_call | solution.py:257
  127.8 0.7 placed_sums.1
  (17 shorter events, 0.5 us)
Async XLA Ops:
  7.2 48.0 %copy-start.2 = (bf16[1,2,128,256]{3,2,1,0:T(8,128)(2,1)S(1)}, bf16[1,2,128,256]{3,2,1,0:T(8,128)(2,1)}, u32[]{:S(2)}) copy-start(bf16[1,2,128,256]{3,2,1,0:T(8,128)(2,1)} %param.8) | copy-start | bytes 393220
  7.2 75.3 %all-gather.3.cloned.1.call-start = ((), (), s32[]{:S(2)}) async-start(), calls=%async_computation.5 | async-start | bytes 4456448 | tf_op jit(solution)/shard_map/all_gather | solution.py:384
  11.3 71.1 %copy-start.3 = (s32[1,2,1]{1,2,0:T(1,128)S(1)}, s32[1,2,1]{1,2,0:T(1,128)}, u32[]{:S(2)}) copy-start(s32[1,2,1]{1,2,0:T(1,128)} %param.13) | copy-start | bytes 28
  11.3 30.8 %all-to-all-start = ((bf16[16,152,128]{2,1,0:T(8,128)(2,1)}), bf16[16,152,128]{2,1,0:T(8,128)(2,1)S(1)}, u32[]{:S(2)}, u32[]{:S(2)}) async-start(bf16[16,152,128]{2,1,0:T(8,128)(2,1)} %packed_adapters.1), calls=%async_computation | async-start | bytes 1245184 | tf_op jit(solution)/shard_map/all_to_all | solution.py:26
  23.2 21.0 %collective-permute-start = (bf16[1,1,128,2048]{3,2,1,0:T(8,128)(2,1)S(1)}, bf16[1,1,128,2048]{3,2,1,0:T(8,128)(2,1)S(1)}, u32[]{:S(2)}, u32[]{:S(2)}) collective-permute-start(bf16[1,1,128,2048]{3,2,1,0:T(8,128)(2,1)S(1)} %get-tuple-element.61), channel_id=1, source_target_pairs={{0,64},{64,128},{128,192},{192,256},{256,320},{320,384},{384,448},... | collective-permute-start | bytes 1572872 | tf_op jit(solution)/shard_map/ppermute | solution.py:22
  44.2 32.8 %all-to-all-start.1 = ((bf16[16,144,128]{2,1,0:T(8,128)(2,1)}), bf16[16,144,128]{2,1,0:T(8,128)(2,1)S(1)}, u32[]{:S(2)}, u32[]{:S(2)}) async-start(bf16[16,144,128]{2,1,0:T(8,128)(2,1)} %selected_pieces.1), calls=%async_computation.1 | async-start | bytes 1179648 | tf_op jit(solution)/shard_map/all_to_all | solution.py:26
  50.4 26.6 %collective-permute-start.2 = (bf16[1,1,128,2048]{3,2,1,0:T(8,128)(2,1)S(1)}, bf16[1,1,128,2048]{3,2,1,0:T(8,128)(2,1)S(1)}, u32[]{:S(2)}, u32[]{:S(2)}) collective-permute-start(bf16[1,1,128,2048]{3,2,1,0:T(8,128)(2,1)S(1)} %get-tuple-element.60), channel_id=1, source_target_pairs={{0,64},{64,128},{128,192},{192,256},{256,320},{320,384},{384,448},... | collective-permute-start | bytes 1572872 | tf_op jit(solution)/shard_map/ppermute | solution.py:22
  55.2 8.7 %collective-permute-start.1 = (bf16[1,2,128,256]{3,2,1,0:T(8,128)(2,1)S(1)}, bf16[1,2,128,256]{3,2,1,0:T(8,128)(2,1)S(1)}, u32[]{:S(2)}, u32[]{:S(2)}) collective-permute-start(bf16[1,2,128,256]{3,2,1,0:T(8,128)(2,1)S(1)} %copy-done.2), channel_id=1, source_target_pairs={{0,448},{64,0},{128,64},{192,128},{256,192},{320,256},{384,320},{4... | collective-permute-start | bytes 393224 | tf_op jit(solution)/shard_map/ppermute | solution.py:22
  78.2 10.9 %all-to-all-start.2 = ((bf16[4,2,2,64,128]{4,3,2,1,0:T(8,128)(2,1)}), bf16[4,2,2,64,128]{4,3,2,1,0:T(8,128)(2,1)S(1)}, u32[]{:S(2)}, u32[]{:S(2)}) async-start(bf16[4,2,2,64,128]{4,3,2,1,0:T(8,128)(2,1)} %get-tuple-element.35), calls=%async_computation.2 | async-start | bytes 524288 | tf_op jit(solution)/shard_map/all_to_all | solution.py:26
  82.5 2.2 %copy-start = (bf16[1024,2048]{1,0:T(8,128)(2,1)S(1)}, bf16[1024,2048]{1,0:T(8,128)(2,1)}, u32[]{:S(2)}) copy-start(bf16[1024,2048]{1,0:T(8,128)(2,1)} %all-gather.3.cloned.1.call-done) | copy-start | bytes 12582916
  89.9 14.9 %all-to-all-start.3 = ((bf16[16,16,128]{2,1,0:T(8,128)(2,1)}), bf16[16,16,128]{2,1,0:T(8,128)(2,1)S(1)}, u32[]{:S(2)}, u32[]{:S(2)}) async-start(bf16[16,16,128]{2,1,0:T(8,128)(2,1)} %get-tuple-element.41), calls=%async_computation.3 | async-start | bytes 131072 | tf_op jit(solution)/shard_map/all_to_all | solution.py:26
  97.0 2.2 %copy-start.1 = (bf16[1024,2048]{1,0:T(8,128)(2,1)S(1)}, bf16[1024,2048]{1,0:T(8,128)(2,1)}, u32[]{:S(2)}) copy-start(bf16[1024,2048]{1,0:T(8,128)(2,1)} %all-gather.3.cloned.1.call-done) | copy-start | bytes 12582916
  106.2 21.6 %all-to-all-start.4 = ((f32[32,2,8,128]{3,2,1,0:T(8,128)}), f32[32,2,8,128]{3,2,1,0:T(8,128)S(1)}, u32[]{:S(2)}, u32[]{:S(2)}) async-start(f32[32,2,8,128]{3,2,1,0:T(8,128)} %slot_sums.1), calls=%async_computation.4 | async-start | bytes 524288 | tf_op jit(solution)/shard_map/all_to_all | solution.py:26
  111.5 11.0 %collective-permute-start.3 = (bf16[2,128,256]{2,1,0:T(8,128)(2,1)S(1)}, bf16[2,128,256]{2,1,0:T(8,128)(2,1)S(1)}, u32[]{:S(2)}, u32[]{:S(2)}) collective-permute-start(bf16[2,128,256]{2,1,0:T(8,128)(2,1)S(1)} %get-tuple-element.52), channel_id=1, source_target_pairs={{0,1},{1,2},{2,3},{3,0},{4,5},{5,6},{6,7},{7,4},{8,9},{9,10},{10,1... | collective-permute-start | bytes 393224 | tf_op jit(solution)/shard_map/ppermute | solution.py:412
  114.6 9.3 %collective-permute-start.4 = (bf16[2,128,256]{2,1,0:T(8,128)(2,1)S(1)}, bf16[2,128,256]{2,1,0:T(8,128)(2,1)S(1)}, u32[]{:S(2)}, u32[]{:S(2)}) collective-permute-start(bf16[2,128,256]{2,1,0:T(8,128)(2,1)S(1)} %get-tuple-element.53), channel_id=1, source_target_pairs={{0,2},{1,3},{2,0},{3,1},{4,6},{5,7},{6,4},{7,5},{8,10},{9,11},{10,... | collective-permute-start | bytes 393224 | tf_op jit(solution)/shard_map/ppermute | solution.py:412
  119.2 7.2 %collective-permute-start.5 = (bf16[2,128,256]{2,1,0:T(8,128)(2,1)S(1)}, bf16[2,128,256]{2,1,0:T(8,128)(2,1)S(1)}, u32[]{:S(2)}, u32[]{:S(2)}) collective-permute-start(bf16[2,128,256]{2,1,0:T(8,128)(2,1)S(1)} %get-tuple-element.54), channel_id=1, source_target_pairs={{0,3},{1,0},{2,1},{3,2},{4,7},{5,4},{6,5},{7,6},{8,11},{9,8},{10,9... | collective-permute-start | bytes 393224 | tf_op jit(solution)/shard_map/ppermute | solution.py:412
Sparse Core Ops, SparseCore 0:
  10.1 67.0 all-gather.2

commit v3 on v2

v3 whole, which is shorter than its diff:
```python
import functools

import jax
import jax.numpy as jnp
from jax import lax
from jax.experimental import pallas as pl
from jax.experimental.pallas import tpu as pltpu
from jax.sharding import PartitionSpec as P

BLOCK_ROWS = 128
LANES = 128

adapter_scale = 2.0

bf16, f32 = jnp.bfloat16, jnp.float32
VMEM_LIMIT = 24 * 1024 * 1024
WIDE_LIMIT = 60 * 1024 * 1024


def passed_along(array, axis, by):
    devices = lax.axis_size(axis)
    return lax.ppermute(array, axis, [(i, (i + by) % devices) for i in range(devices)])


def exchanged(array, axis):
    return lax.all_to_all(array, axis, split_axis=0, concat_axis=0, tiled=True)


def smem():
    return pl.BlockSpec(memory_space=pltpu.SMEM)


def params():
    return pltpu.CompilerParams(vmem_limit_bytes=VMEM_LIMIT)


def nt_dot(a, b):
    return lax.dot_general(a, b, (((1,), (1,)), ((), ())), preferred_element_type=f32)


def tn_dot(a, b):
    return lax.dot_general(a, b, (((0,), (0,)), ((), ())), preferred_element_type=f32)


def pack_kernel(halves, langs_ref, table_ref, down_ref, up_ref, out_ref):
    pieces, payload, piece = out_ref.shape
    own_slots, rank, _ = down_ref.shape
    micro, count = langs_ref.shape[1], table_ref.shape[1]
    group = up_ref.shape[1] * halves // pieces
    low, high = own_slots * rank, own_slots * (rank + group)
    lane = lax.broadcasted_iota(jnp.int32, (1, count), 1)
    row = lax.broadcasted_iota(jnp.int32, (payload - high, piece), 0)
    marks = jnp.zeros((payload - high, piece), f32)
    for m in range(micro):
        match = table_ref[...] == langs_ref[:, m : m + 1]
        slot = jnp.min(jnp.where(match, lane, count), axis=1, keepdims=True).astype(f32)
        marks = jnp.where(row == m, slot, marks)
    marks = marks.astype(bf16)
    ups = [up_ref[k].astype(f32) for k in range(own_slots)]
    for p in range(pieces):
        for k in range(own_slots):
            out_ref[p, k * rank : (k + 1) * rank, :] = down_ref[k, :, p * piece : (p + 1) * piece]
        top, left = (p // halves) * group, (p % halves) * LANES
        out_ref[p, low:high, :] = jnp.concatenate(
            [up[top : top + group, left : left + LANES] for up in ups], axis=0
        ).astype(bf16)
        out_ref[p, high:, :] = marks


def packed(langs, table, down, up, holders):
    own_slots, rank, width = down.shape
    columns = up.shape[2]
    halves = columns // LANES
    payload = own_slots * (rank + rank * halves // holders) + 8
    steps = 1
    return pl.pallas_call(
        functools.partial(pack_kernel, halves),
        grid=(steps,),
        out_shape=jax.ShapeDtypeStruct((holders, payload, width // holders), bf16),
        in_specs=[
            pl.BlockSpec(langs.shape, lambda i: (0, 0)),
            pl.BlockSpec(table.shape, lambda i: (0, 0)),
            pl.BlockSpec((own_slots, rank, width // steps), lambda i: (0, 0, i)),
            pl.BlockSpec((own_slots, rank // steps, columns), lambda i: (0, i, 0)),
        ],
        out_specs=pl.BlockSpec(
            (holders // steps, payload, width // holders), lambda i: (i, 0, 0)
        ),
        compiler_params=pltpu.CompilerParams(vmem_limit_bytes=WIDE_LIMIT),
        name="packed_adapters",
    )(langs, table, down, up)


def weight_kernel(micro, quarters, first_ref, *refs):
    acts, cots = refs[:micro], refs[micro : micro + quarters]
    gathered_ref = refs[micro + quarters]
    outs, back_ref, held_ref, sems = refs[micro + quarters + 1 : -3], *refs[-3:]
    group = held_ref.shape[1]
    copies = []
    for k in range(quarters):
        quarter = lax.rem(first_ref[0] + k, quarters)
        copy = pltpu.make_async_copy(
            gathered_ref.at[pl.ds(quarter * group, group)], held_ref.at[k], sems.at[k]
        )
        copy.start()
        copies.append(copy)
    rows = jnp.concatenate([ref[0, 0] for ref in acts], axis=0)
    for k in range(quarters):
        copies[k].wait()
        weight = held_ref[k].reshape(-1, held_ref.shape[3])
        outs[k][...] = nt_dot(rows, weight).astype(bf16)
        back = jnp.dot(cots[(quarters - k) % quarters][...], weight, preferred_element_type=f32)
        if k == 0:
            back_ref[...] = back
        else:
            back_ref[...] += back


def weight_products(first, acts, cots, gathered):
    micro, quarters = len(acts), len(cots)
    holders, cols, width = gathered.shape
    rows = micro * BLOCK_ROWS
    group = holders // quarters
    results = pl.pallas_call(
        functools.partial(weight_kernel, micro, quarters),
        out_shape=(jax.ShapeDtypeStruct((rows, group * cols), bf16),) * quarters
        + (jax.ShapeDtypeStruct((rows, width), f32),),
        in_specs=[smem()]
        + [pl.BlockSpec(memory_space=pltpu.VMEM)] * (micro + quarters)
        + [pl.BlockSpec(memory_space=pltpu.HBM)],
        out_specs=(pl.BlockSpec(memory_space=pltpu.VMEM),) * (quarters + 1),
        scratch_shapes=[
            pltpu.VMEM((quarters, group, cols, width), bf16),
            pltpu.SemaphoreType.DMA((quarters,)),
        ],
        compiler_params=params(),
        cost_estimate=pl.CostEstimate(
            flops=4 * rows * width * cols * holders,
            bytes_accessed=2 * holders * cols * (width + 2 * rows) + 4 * rows * width,
            transcendentals=0,
        ),
        name="weight_products",
    )(first, *acts, *cots, gathered)
    return list(results[:-1]), results[-1]


def part_kernel(micro, second_ref, returned_ref, *refs):
    acts, parts_ref, up_ref = refs[:micro], refs[micro], refs[micro + 1]
    pieces, _, piece = second_ref.shape
    rank, columns = up_ref.shape[1:]
    halves = columns // LANES
    group = rank * halves // pieces
    for p in range(pieces):
        both = second_ref[p, micro * rank :, :].astype(f32)
        top, left = (p // halves) * group, (p % halves) * LANES
        for m in range(micro):
            up_ref[m, top : top + group, left : left + LANES] = both[m * group : (m + 1) * group]
    for m in range(micro):
        down = jnp.concatenate(
            [second_ref[p, m * rank : (m + 1) * rank, :] for p in range(pieces)], axis=1
        )
        parts = (
            nt_dot(down, acts[m][0, 0]).astype(bf16),
            nt_dot(up_ref[m].astype(bf16), returned_ref[m]).astype(bf16),
        )
        for q in range(parts_ref.shape[0]):
            for kind in range(2):
                parts_ref[q, kind, m] = parts[kind]


def rank_parts(second, returned, acts, rank, quarters):
    micro, _, columns = returned.shape
    return pl.pallas_call(
        functools.partial(part_kernel, micro),
        out_shape=(
            jax.ShapeDtypeStruct((quarters, 2, micro, rank, BLOCK_ROWS), bf16),
            jax.ShapeDtypeStruct((micro, rank, columns), f32),
        ),
        in_specs=[pl.BlockSpec(memory_space=pltpu.VMEM)] * (2 + micro),
        out_specs=(pl.BlockSpec(memory_space=pltpu.VMEM),) * 2,
        compiler_params=params(),
        name="rank_parts",
    )(second, returned, *acts)


def select_kernel(micro, own_slots, rank, slots_ref, first_ref, out_ref):
    holders = out_ref.shape[0]
    group = out_ref.shape[1] // micro - rank
    low = own_slots * rank
    for d in range(holders):
        ups = []
        for m in range(micro):
            slot = jnp.minimum(slots_ref[d * micro + m], holders * own_slots - 1)
            owner, k = slot // own_slots, slot % own_slots
            rows = pl.ds(pl.multiple_of(k * rank, rank), rank)
            out_ref[d, m * rank : (m + 1) * rank, :] = first_ref[owner, rows, :]
            held = first_ref[owner, low : low + own_slots * group, :].astype(f32)
            up = held[:group]
            for j in range(1, own_slots):
                up = jnp.where(k == j, held[j * group : (j + 1) * group], up)
            ups.append(up)
        out_ref[d, micro * rank :, :] = jnp.concatenate(ups, axis=0).astype(bf16)


def selected(slots, first, micro, own_slots, rank, group):
    holders, _, lanes = first.shape
    return pl.pallas_call(
        functools.partial(select_kernel, micro, own_slots, rank),
        out_shape=jax.ShapeDtypeStruct((holders, micro * (rank + group), lanes), bf16),
        in_specs=[smem(), pl.BlockSpec(memory_space=pltpu.VMEM)],
        out_specs=pl.BlockSpec(memory_space=pltpu.VMEM),
        compiler_params=params(),
        name="selected_pieces",
    )(slots, first)


def gradient_kernel(micro, live_ref, ranks_ref, down_ref, product_ref, out_ref):
    rank = ranks_ref.shape[1]
    pieces = down_ref.shape[0]
    for m in range(micro):
        back = (adapter_scale * ranks_ref[m].astype(f32)).T.astype(bf16)
        down = jnp.concatenate(
            [down_ref[p, m * rank : (m + 1) * rank, :] for p in range(pieces)], axis=1
        )
        lora = jnp.dot(back, down, preferred_element_type=f32).astype(bf16).astype(f32)
        part = product_ref[m * BLOCK_ROWS : (m + 1) * BLOCK_ROWS] + lora
        out_ref[m] = jnp.where(live_ref[m] > 0, part, 0.0).astype(bf16)


def input_gradients(live, ranks, second, product):
    micro, rank = ranks.shape[:2]
    rows, width = product.shape
    pieces, _, piece = second.shape
    steps = 2
    return pl.pallas_call(
        functools.partial(gradient_kernel, micro),
        grid=(steps,),
        out_shape=jax.ShapeDtypeStruct((micro, BLOCK_ROWS, width), bf16),
        in_specs=[
            smem(),
            pl.BlockSpec(ranks.shape, lambda i: (0, 0, 0)),
            pl.BlockSpec((pieces // steps, micro * rank, piece), lambda i: (i, 0, 0)),
            pl.BlockSpec((rows, width // steps), lambda i: (0, i)),
        ],
        out_specs=pl.BlockSpec((micro, BLOCK_ROWS, width // steps), lambda i: (0, 0, i)),
        compiler_params=pltpu.CompilerParams(vmem_limit_bytes=WIDE_LIMIT),
        cost_estimate=pl.CostEstimate(
            flops=2 * rows * width * rank, bytes_accessed=6 * rows * width, transcendentals=0
        ),
        name="input_gradients",
    )(live, ranks, second, product)


def layer_kernel(micro, live_ref, ranks_ref, up_ref, *refs):
    out_ref = refs[-1]
    for m in range(micro):
        total = adapter_scale * tn_dot(ranks_ref[m], up_ref[m].astype(bf16))
        for part_ref in refs[:-1]:
            total += part_ref[m * BLOCK_ROWS : (m + 1) * BLOCK_ROWS, :].astype(f32)
        out_ref[m] = jnp.where(live_ref[m] > 0, total, 0.0).astype(bf16)


def layer_outputs(live, ranks, up, parts):
    micro, _, columns = up.shape
    return pl.pallas_call(
        functools.partial(layer_kernel, micro),
        out_shape=jax.ShapeDtypeStruct((micro, BLOCK_ROWS, columns), bf16),
        in_specs=[smem()] + [pl.BlockSpec(memory_space=pltpu.VMEM)] * (2 + len(parts)),
        out_specs=pl.BlockSpec(memory_space=pltpu.VMEM),
        compiler_params=params(),
        name="layer_outputs",
    )(live, ranks, up, *parts)


def rank_kernel(parts_ref, incoming_ref, ranks_ref, pieces_ref):
    micro, rank = parts_ref.shape[2:4]
    total = parts_ref[0].astype(f32)
    for q in range(1, parts_ref.shape[0]):
        total += parts_ref[q].astype(f32)
    ranks_ref[...] = total.astype(bf16)
    half = rank // 2
    for m in range(micro):
        grad = jnp.dot(ranks_ref[0, m], incoming_ref[m], preferred_element_type=f32)
        grad = (grad * (adapter_scale / BLOCK_ROWS)).astype(bf16)
        for p in range(pieces_ref.shape[0]):
            top = (p % 2) * half
            pieces_ref[p, m] = grad[top : top + half]


def ranks_and_pieces(parts, incoming, holders):
    micro, rank = parts.shape[2:4]
    columns = incoming.shape[2]
    return pl.pallas_call(
        rank_kernel,
        out_shape=(
            jax.ShapeDtypeStruct(parts.shape[1:], bf16),
            jax.ShapeDtypeStruct((holders, micro, rank // 2, columns), bf16),
        ),
        in_specs=[pl.BlockSpec(memory_space=pltpu.VMEM)] * 2,
        out_specs=(pl.BlockSpec(memory_space=pltpu.VMEM),) * 2,
        compiler_params=params(),
        name="ranks_and_pieces",
    )(parts, incoming)


def slot_kernel(marks_ref, first_ref, pieces_ref, out_ref):
    holders, micro = pieces_ref.shape[:2]
    for i in range(out_ref.shape[0]):
        total, square = None, None
        for d in range(holders):
            partial = None
            for m in range(micro):
                hit = marks_ref[d * micro + m] == first_ref[0] + i
                term = jnp.where(hit, pieces_ref[d, m].astype(f32), 0.0)
                partial = term if partial is None else partial + term
            total = partial if total is None else total + partial
            squared = partial * partial
            square = squared if square is None else square + squared
        out_ref[i, 0] = total
        out_ref[i, 1] = square


def slot_sums(marks, first_slot, pieces, own_slots):
    return pl.pallas_call(
        slot_kernel,
        out_shape=jax.ShapeDtypeStruct((own_slots, 2) + pieces.shape[2:], f32),
        in_specs=[smem(), smem(), pl.BlockSpec(memory_space=pltpu.VMEM)],
        out_specs=pl.BlockSpec(memory_space=pltpu.VMEM),
        compiler_params=params(),
        name="slot_sums",
    )(marks, first_slot, pieces)


def place_kernel(core_ref, own_ref, other_ref, sum_ref, square_ref):
    half = own_ref.shape[2]
    low = core_ref[0] == 0
    for k in range(own_ref.shape[0]):
        for kind, out_ref in enumerate((sum_ref, square_ref)):
            own, other = own_ref[k, kind], other_ref[k, kind]
            out_ref[k, :half] = jnp.where(low, own, other)
            out_ref[k, half:] = jnp.where(low, other, own)


def placed(core, own, other):
    own_slots, _, half, columns = own.shape
    shape = jax.ShapeDtypeStruct((own_slots, 2 * half, columns), f32)
    return pl.pallas_call(
        place_kernel,
        out_shape=(shape, shape),
        in_specs=[smem()] + [pl.BlockSpec(memory_space=pltpu.VMEM)] * 2,
        out_specs=(pl.BlockSpec(memory_space=pltpu.VMEM),) * 2,
        compiler_params=params(),
        name="placed_sums",
    )(core, own, other)


def shards(
    activations, cotangent, base_weight, adapter_down, adapter_up, slot_language, block_language
):
    holders = lax.axis_size("dp")
    quarters = lax.axis_size("mp")
    own_slots, width, rank = adapter_down.shape[1:]
    columns = adapter_up.shape[3]
    micro = activations.shape[1]
    rows = micro * BLOCK_ROWS
    piece = width // holders
    up_groups = holders // (columns // LANES)
    up_rows = rank // up_groups
    me = lax.axis_index("dp")

    returned = passed_along(cotangent, "section", -1)[0]
    arrived = [passed_along(activations[:, m : m + 1], "section", 1) for m in range(micro)]

    slot_table = slot_language[0]
    langs = block_language[0, :, 0]
    live = (langs < slot_table.shape[0]).astype(jnp.int32)

    weight = jnp.swapaxes(base_weight[0], 0, 1)
    gathered = lax.all_gather(weight, "dp", axis=0)
    flat_cots = returned.reshape(rows, columns)
    cots = [flat_cots] + [
        lax.ppermute(flat_cots, "mp", [(i, (i + k) % quarters) for i in range(quarters)])
        for k in range(1, quarters)
    ]

    down = jnp.swapaxes(adapter_down[0], 1, 2)
    first = packed(langs[None, :], slot_language, down, adapter_up[0], holders)
    first = exchanged(first, "dp")

    marked = own_slots * (rank + up_rows)
    slots = first[:, marked : marked + micro, 0].astype(jnp.int32).reshape(-1)
    second = selected(slots, first, micro, own_slots, rank, up_rows)
    second, arrived[0], cots[1] = lax.optimization_barrier((second, arrived[0], cots[1]))
    second = exchanged(second, "dp")
    second, cots = lax.optimization_barrier((second, cots))

    parts, up = rank_parts(second, returned, arrived, rank, quarters)
    parts = exchanged(parts, "mp")
    quarter = lax.axis_index("mp").astype(jnp.int32).reshape(1)
    base_parts, back = weight_products(quarter, arrived, cots, gathered)
    parts, base_parts = lax.optimization_barrier((parts, base_parts))
    ranks, pieces = ranks_and_pieces(parts, returned, holders)
    rank_in, rank_back = ranks[0], ranks[1]

    pieces = exchanged(pieces, "dp")
    base_parts = [base_parts[0]] + [
        lax.ppermute(base_parts[k], "mp", [(i, (i + k) % quarters) for i in range(quarters)])
        for k in range(1, quarters)
    ]
    layer_out = layer_outputs(live, rank_in, up, base_parts)[None]
    input_gradient = input_gradients(live, rank_back, second, back)[None]
    pieces, input_gradient, layer_out = lax.optimization_barrier(
        (pieces, input_gradient, layer_out)
    )
    other = slot_sums(slots, (own_slots * (me ^ 1)).astype(jnp.int32).reshape(1), pieces, own_slots)
    other = lax.ppermute(other, "dp", [(i, i ^ 1) for i in range(holders)])
    own = slot_sums(slots, (own_slots * me).astype(jnp.int32).reshape(1), pieces, own_slots)
    grad_sum, grad_square = placed((me % 2).astype(jnp.int32).reshape(1), own, other)

    return (layer_out, input_gradient, grad_sum[None], grad_square[None])


def solution(mesh):
    in_specs = (
        P("section", None, "dp", "mp"),
        P("section", None, "dp", "mp"),
        P("section", "mp", "dp"),
        P("section", "dp", "mp", None),
        P("section", "dp", None, "mp"),
        P("section", None),
        P("section", None, "dp"),
    )
    out_specs = (
        P("section", None, "dp", "mp"),
        P("section", None, "dp", "mp"),
        P("section", "dp", None, "mp"),
        P("section", "dp", None, "mp"),
    )
    return jax.shard_map(shards, mesh=mesh, in_specs=in_specs, out_specs=out_specs, check_vma=False)
```

time: 136 us -> 122 us (0.90)
  the two profiles are of different devices: /device:TPU:24 before, /device:TPU:1 now
where the time goes in v3:
time: 122 us; the launch traced here: 121 us
  starting transfers between devices  58.8 us (48%)
  waiting for transfers between devices  24.1 us (20%)
  Pallas kernels  17.3 us (14%)
  between operations  14.2 us (12%)
  local copies, waits for them, and re-layouts  6.18 us (5%)
    all_to_all x4, starting transfers between devices, exchanged(): return lax.all_to_all(array, axis, split_axis=0, concat_axis=0, tiled=True)  23.9 us
    all_to_all x4, waiting for transfers between devices, exchanged(): return lax.all_to_all(array, axis, split_axis=0, concat_axis=0, tiled=True)  16.8 us
    ppermute x3, starting transfers between devices, shards(): lax.ppermute(base_parts[k], 'mp', [(i, (i + k) % quarters) for i in range...  11.1 us
    ppermute x3, starting transfers between devices, shards(): lax.ppermute(flat_cots, 'mp', [(i, (i + k) % quarters) for i in range(qua...  10.5 us
    ppermute x3, starting transfers between devices, passed_along(): lax.ppermute(array, axis, [(i, (i + by) % devices) for i in range(devices)])  10.3 us
    pallas_call x1, Pallas kernels, weight_products(): pl.pallas_call(functools.partial(weight_kernel, micro, quarters), out_sha...  4.44 us
    unnamed x12, local copies, waits for them, and re-layouts  4.2 us
    ppermute x3, waiting for transfers between devices, shards(): lax.ppermute(flat_cots, 'mp', [(i, (i + k) % quarters) for i in range(qua...  3.62 us
  transfers between devices with their start and end apart: 15, of which 7 were waited for; matrix products, arithmetic and copies ran while one was open for 2% of the time, Pallas kernels for 12%

profile of v3, /device:TPU:1, one launch (start us, length us, event | category | flops | bytes accessed | tf_op | source)
XLA Modules:
  0.0 121.5 jit_solution(8768462441566517294)
XLA Ops:
  7.2 0.7 all-gather.3.cloned.1.call-update
  7.9 2.1 %packed_adapters.1 = bf16[16,152,128]{2,1,0:T(8,128)(2,1)} custom-call(s32[1,2]{1,0:T(1,128)} %bitcast.37, s32[1,32]{1,0:T(1,128)} %table_ref.1, bf16[2,64,2048]{2,1,0:T(8,128)(2,1)} %bitcast.33, bf16[2,64,256]{2,1,0:T(8,128)(2,1)} %bitcast.36), custom_call_target="tpu_custom_call" | custom-call | tf_op jit(solution)/shard_map/packed_adapters/pallas_call | solution.py:76
  10.1 11.8 %all-to-all-start = ((bf16[16,152,128]{2,1,0:T(8,128)(2,1)}), bf16[16,152,128]{2,1,0:T(8,128)(2,1)S(1)}, u32[]{:S(2)}, u32[]{:S(2)}) async-start(bf16[16,152,128]{2,1,0:T(8,128)(2,1)} %packed_adapters.1), calls=%async_computation | async-start | bytes 1245184 | tf_op jit(solution)/shard_map/all_to_all | solution.py:26
  21.9 1.3 %fusion.1 = (bf16[1,1,128,2048]{3,2,1,0:T(8,128)(2,1)S(1)}, bf16[1,1,128,2048]{3,2,1,0:T(8,128)(2,1)S(1)}) fusion(bf16[1,2,128,2048]{3,2,1,0:T(8,128)(2,1)} %param.7), kind=kLoop, calls=%fused_computation.5 | loop fusion | bytes 2097152 | tf_op jit(solution)/shard_map/slice | solution.py:372
  23.2 3.2 %collective-permute-start = (bf16[1,1,128,2048]{3,2,1,0:T(8,128)(2,1)S(1)}, bf16[1,1,128,2048]{3,2,1,0:T(8,128)(2,1)S(1)}, u32[]{:S(2)}, u32[]{:S(2)}) collective-permute-start(bf16[1,1,128,2048]{3,2,1,0:T(8,128)(2,1)S(1)} %get-tuple-element.59), channel_id=1, source_target_pairs={{0,64},{64,128},{128,192},{192,256},{256,320},{320,384},{384,448},... | collective-permute-start | bytes 1572872 | tf_op jit(solution)/shard_map/ppermute | solution.py:22
  26.4 3.8 %collective-permute-start.1 = (bf16[1,2,128,256]{3,2,1,0:T(8,128)(2,1)S(1)}, bf16[1,2,128,256]{3,2,1,0:T(8,128)(2,1)S(1)}, u32[]{:S(2)}, u32[]{:S(2)}) collective-permute-start(bf16[1,2,128,256]{3,2,1,0:T(8,128)(2,1)S(1)} %copy-done.5), channel_id=1, source_target_pairs={{0,448},{64,0},{128,64},{192,128},{256,192},{320,256},{384,320},{4... | collective-permute-start | bytes 393224 | tf_op jit(solution)/shard_map/ppermute | solution.py:22
  30.2 2.9 %collective-permute-done.1 = bf16[1,2,128,256]{3,2,1,0:T(8,128)(2,1)S(1)} collective-permute-done((bf16[1,2,128,256]{3,2,1,0:T(8,128)(2,1)S(1)}, bf16[1,2,128,256]{3,2,1,0:T(8,128)(2,1)S(1)}, u32[]{:S(2)}, u32[]{:S(2)}) %collective-permute-start.1) | collective-permute-done | bytes 131104 | tf_op jit(solution)/shard_map/ppermute | solution.py:22
  33.1 3.1 %collective-permute-start.2 = (bf16[256,256]{1,0:T(8,128)(2,1)S(1)}, bf16[256,256]{1,0:T(8,128)(2,1)S(1)}, u32[]{:S(2)}, u32[]{:S(2)}) collective-permute-start(bf16[256,256]{1,0:T(8,128)(2,1)S(1)} %bitcast.25), channel_id=1, source_target_pairs={{0,1},{1,2},{2,3},{3,0},{4,5},{5,6},{6,7},{7,4},{8,9},{9,10},{10,1... | collective-permute-start | bytes 393224 | tf_op jit(solution)/shard_map/ppermute | solution.py:382
  36.2 7.3 %all-to-all-done.first_ref = bf16[16,152,128]{2,1,0:T(8,128)(2,1)S(1)} async-done(((bf16[16,152,128]{2,1,0:T(8,128)(2,1)}), bf16[16,152,128]{2,1,0:T(8,128)(2,1)S(1)}, u32[]{:S(2)}, u32[]{:S(2)}) %all-to-all-start) | async-done | bytes 622624 | tf_op jit(solution)/shard_map/all_to_all | solution.py:26
  44.0 1.6 %selected_pieces.1 = bf16[16,144,128]{2,1,0:T(8,128)(2,1)} custom-call(s32[32]{0:T(128)S(1)} %reshape.32.slots_ref.marks_ref, bf16[16,152,128]{2,1,0:T(8,128)(2,1)S(1)} %all-to-all-done.first_ref), custom_call_target="tpu_custom_call" | custom-call | tf_op jit(solution)/shard_map/selected_pieces/pallas_call | solution.py:207
  45.6 3.8 %all-to-all-start.1 = ((bf16[16,144,128]{2,1,0:T(8,128)(2,1)}), bf16[16,144,128]{2,1,0:T(8,128)(2,1)S(1)}, u32[]{:S(2)}, u32[]{:S(2)}) async-start(bf16[16,144,128]{2,1,0:T(8,128)(2,1)} %selected_pieces.1), calls=%async_computation.1 | async-start | bytes 1179648 | tf_op jit(solution)/shard_map/all_to_all | solution.py:26
  49.5 3.2 %collective-permute-start.5 = (bf16[1,1,128,2048]{3,2,1,0:T(8,128)(2,1)S(1)}, bf16[1,1,128,2048]{3,2,1,0:T(8,128)(2,1)S(1)}, u32[]{:S(2)}, u32[]{:S(2)}) collective-permute-start(bf16[1,1,128,2048]{3,2,1,0:T(8,128)(2,1)S(1)} %get-tuple-element.58), channel_id=1, source_target_pairs={{0,64},{64,128},{128,192},{192,256},{256,320},{320,384},{384,448},... | collective-permute-start | bytes 1572872 | tf_op jit(solution)/shard_map/ppermute | solution.py:22
  52.7 4.7 %collective-permute-start.3 = (bf16[256,256]{1,0:T(8,128)(2,1)S(1)}, bf16[256,256]{1,0:T(8,128)(2,1)S(1)}, u32[]{:S(2)}, u32[]{:S(2)}) collective-permute-start(bf16[256,256]{1,0:T(8,128)(2,1)S(1)} %bitcast.26), channel_id=1, source_target_pairs={{0,2},{1,3},{2,0},{3,1},{4,6},{5,7},{6,4},{7,5},{8,10},{9,11},{10,... | collective-permute-start | bytes 393224 | tf_op jit(solution)/shard_map/ppermute | solution.py:382
  57.4 2.8 %collective-permute-start.4 = (bf16[256,256]{1,0:T(8,128)(2,1)S(1)}, bf16[256,256]{1,0:T(8,128)(2,1)S(1)}, u32[]{:S(2)}, u32[]{:S(2)}) collective-permute-start(bf16[256,256]{1,0:T(8,128)(2,1)S(1)} %bitcast.27), channel_id=1, source_target_pairs={{0,3},{1,0},{2,1},{3,2},{4,7},{5,4},{6,5},{7,6},{8,11},{9,8},{10,9... | collective-permute-start | bytes 393224 | tf_op jit(solution)/shard_map/ppermute | solution.py:382
  60.8 3.0 %collective-permute-done.4.refs_5_ = bf16[256,256]{1,0:T(8,128)(2,1)S(1)} collective-permute-done((bf16[256,256]{1,0:T(8,128)(2,1)S(1)}, bf16[256,256]{1,0:T(8,128)(2,1)S(1)}, u32[]{:S(2)}, u32[]{:S(2)}) %collective-permute-start.4) | collective-permute-done | bytes 131104 | tf_op jit(solution)/shard_map/ppermute | solution.py:382
  63.8 9.4 %all-to-all-done.1.second_ref.down_ref = bf16[16,144,128]{2,1,0:T(8,128)(2,1)S(1)} async-done(((bf16[16,144,128]{2,1,0:T(8,128)(2,1)}), bf16[16,144,128]{2,1,0:T(8,128)(2,1)S(1)}, u32[]{:S(2)}, u32[]{:S(2)}) %all-to-all-start.1) | async-done | bytes 589856 | tf_op jit(solution)/shard_map/all_to_all | solution.py:26
  73.2 1.2 %rank_parts.1 = (bf16[4,2,2,64,128]{4,3,2,1,0:T(8,128)(2,1)}, f32[2,64,256]{2,1,0:T(8,128)S(1)}) custom-call(bf16[16,144,128]{2,1,0:T(8,128)(2,1)S(1)} %all-to-all-done.1.second_ref.down_ref, bf16[2,128,256]{2,1,0:T(8,128)(2,1)S(1)} %bitcast.28, bf16[1,1,128,2048]{3,2,1,0:T(8,128)(2,1)S(1)} %collective-permute-done.refs_0_, ...), custom_call_target="tpu_custom_call" | custom-call | tf_op jit(solution)/shard_map/rank_parts/pallas_call | solution.py:173
  74.4 4.0 %all-to-all-start.2 = ((bf16[4,2,2,64,128]{4,3,2,1,0:T(8,128)(2,1)}), bf16[4,2,2,64,128]{4,3,2,1,0:T(8,128)(2,1)S(1)}, u32[]{:S(2)}, u32[]{:S(2)}) async-start(bf16[4,2,2,64,128]{4,3,2,1,0:T(8,128)(2,1)} %get-tuple-element.35), calls=%async_computation.2 | async-start | bytes 524288 | tf_op jit(solution)/shard_map/all_to_all | solution.py:26
  78.5 2.2 %copy-done.3 = bf16[1024,2048]{1,0:T(8,128)(2,1)S(1)} copy-done((bf16[1024,2048]{1,0:T(8,128)(2,1)S(1)}, bf16[1024,2048]{1,0:T(8,128)(2,1)}, u32[]{:S(2)}) %copy-start.3) | copy-done | bytes 4194328
  80.7 4.4 %weight_products.1 = (bf16[256,256]{1,0:T(8,128)(2,1)S(1)}, bf16[256,256]{1,0:T(8,128)(2,1)S(1)}, bf16[256,256]{1,0:T(8,128)(2,1)S(1)}, bf16[256,256]{1,0:T(8,128)(2,1)S(1)}, f32[256,2048]{1,0:T(8,128)S(1)}) custom-call(s32[1]{0:T(128)} %bitcast.6.first_ref, bf16[1,1,128,2048]{3,2,1,0:T(8,128)(2,1)S(1)} %collective-permute-done.refs_0_, ...), custom_call_target="tpu_custom_call" | custom-call | flops 2147483648 | bytes 7340032 | tf_op jit(solution)/shard_map/weight_products/pallas_call | solution.py:124
  85.2 1.3 %copy-done.1 = f32[256,2048]{1,0:T(8,128)} copy-done((f32[256,2048]{1,0:T(8,128)}, f32[256,2048]{1,0:T(8,128)S(1)}, u32[]{:S(2)}) %copy-start.1) | copy-done | bytes 2097176
  86.5 1.0 ranks_and_pieces.1
  87.5 4.2 %all-to-all-start.3 = ((bf16[16,2,32,256]{3,2,1,0:T(8,128)(2,1)}), bf16[16,2,32,256]{3,2,1,0:T(8,128)(2,1)S(1)}, u32[]{:S(2)}, u32[]{:S(2)}) async-start(bf16[16,2,32,256]{3,2,1,0:T(8,128)(2,1)} %get-tuple-element.45), calls=%async_computation.3 | async-start | bytes 1048576 | tf_op jit(solution)/shard_map/all_to_all | solution.py:26
  92.2 3.7 %collective-permute-start.6 = (bf16[256,256]{1,0:T(8,128)(2,1)S(1)}, bf16[256,256]{1,0:T(8,128)(2,1)S(1)}, u32[]{:S(2)}, u32[]{:S(2)}) collective-permute-start(bf16[256,256]{1,0:T(8,128)(2,1)S(1)} %get-tuple-element.50), channel_id=1, source_target_pairs={{0,1},{1,2},{2,3},{3,0},{4,5},{5,6},{6,7},{7,4},{8,9},{9,10},{10,1... | collective-permute-start | bytes 393224 | tf_op jit(solution)/shard_map/ppermute | solution.py:407
  95.9 4.3 %collective-permute-start.7 = (bf16[256,256]{1,0:T(8,128)(2,1)S(1)}, bf16[256,256]{1,0:T(8,128)(2,1)S(1)}, u32[]{:S(2)}, u32[]{:S(2)}) collective-permute-start(bf16[256,256]{1,0:T(8,128)(2,1)S(1)} %get-tuple-element.51), channel_id=1, source_target_pairs={{0,2},{1,3},{2,0},{3,1},{4,6},{5,7},{6,4},{7,5},{8,10},{9,11},{10,... | collective-permute-start | bytes 393224 | tf_op jit(solution)/shard_map/ppermute | solution.py:407
  100.2 3.1 %collective-permute-start.8 = (bf16[256,256]{1,0:T(8,128)(2,1)S(1)}, bf16[256,256]{1,0:T(8,128)(2,1)S(1)}, u32[]{:S(2)}, u32[]{:S(2)}) collective-permute-start(bf16[256,256]{1,0:T(8,128)(2,1)S(1)} %get-tuple-element.52), channel_id=1, source_target_pairs={{0,3},{1,0},{2,1},{3,2},{4,7},{5,4},{6,5},{7,6},{8,11},{9,8},{10,9... | collective-permute-start | bytes 393224 | tf_op jit(solution)/shard_map/ppermute | solution.py:407
  103.9 2.9 %input_gradients.1 = bf16[2,128,2048]{2,1,0:T(8,128)(2,1)} custom-call(s32[2]{0:T(128)} %fusion.live_ref, bf16[2,64,128]{2,1,0:T(8,128)(2,1)} %get-tuple-element.61.ranks_ref, bf16[16,144,128]{2,1,0:T(8,128)(2,1)} %copy-done, f32[256,2048]{1,0:T(8,128)} %copy-done.1), custom_call_target="tpu_custom_call" | custom-call | flops 67108864 | bytes 3145728 | tf_op jit(solution)/shard_map/input_gradients/pallas_call | solution.py:235
  107.5 1.5 %layer_outputs.1 = bf16[2,128,256]{2,1,0:T(8,128)(2,1)} custom-call(s32[2]{0:T(128)S(1)} %copy-done.2, bf16[2,64,128]{2,1,0:T(8,128)(2,1)S(1)} %get-tuple-element.60.ranks_ref, f32[2,64,256]{2,1,0:T(8,128)S(1)} %get-tuple-element.48.up_ref, bf16[256,256]{1,0:T(8,128)(2,1)S(1)} %get-tuple-element.49.refs_0_, ...), custom_call_target="tpu_custom_call" | custom-call | tf_op jit(solution)/shard_map/layer_outputs/pallas_call | solution.py:265
  109.0 0.9 slot_sums.3
  109.9 3.0 %collective-permute-start.9 = (f32[2,2,32,256]{3,2,1,0:T(8,128)S(1)}, f32[2,2,32,256]{3,2,1,0:T(8,128)S(1)}, u32[]{:S(2)}, u32[]{:S(2)}) collective-permute-start(f32[2,2,32,256]{3,2,1,0:T(8,128)S(1)} %slot_sums.3), channel_id=1, source_target_pairs={{0,4},{4,0},{8,12},{12,8},{16,20},{20,16},{24,28},{28,24},{32,36},... | collective-permute-start | bytes 393224 | tf_op jit(solution)/shard_map/ppermute | solution.py:416
  113.0 0.9 slot_sums.2.own_ref
  113.9 0.7 placed_sums.1
  (26 shorter events, 3.1 us)
Async XLA Ops:
  7.2 19.2 %copy-start.5 = (bf16[1,2,128,256]{3,2,1,0:T(8,128)(2,1)S(1)}, bf16[1,2,128,256]{3,2,1,0:T(8,128)(2,1)}, u32[]{:S(2)}) copy-start(bf16[1,2,128,256]{3,2,1,0:T(8,128)(2,1)} %param.8) | copy-start | bytes 393220
  7.2 71.3 %all-gather.3.cloned.1.call-start = ((), (), s32[]{:S(2)}) async-start(), calls=%async_computation.4 | async-start | bytes 4456448 | tf_op jit(solution)/shard_map/all_gather | solution.py:379
  10.1 33.5 %all-to-all-start = ((bf16[16,152,128]{2,1,0:T(8,128)(2,1)}), bf16[16,152,128]{2,1,0:T(8,128)(2,1)S(1)}, u32[]{:S(2)}, u32[]{:S(2)}) async-start(bf16[16,152,128]{2,1,0:T(8,128)(2,1)} %packed_adapters.1), calls=%async_computation | async-start | bytes 1245184 | tf_op jit(solution)/shard_map/all_to_all | solution.py:26
  23.2 22.5 %collective-permute-start = (bf16[1,1,128,2048]{3,2,1,0:T(8,128)(2,1)S(1)}, bf16[1,1,128,2048]{3,2,1,0:T(8,128)(2,1)S(1)}, u32[]{:S(2)}, u32[]{:S(2)}) collective-permute-start(bf16[1,1,128,2048]{3,2,1,0:T(8,128)(2,1)S(1)} %get-tuple-element.59), channel_id=1, source_target_pairs={{0,64},{64,128},{128,192},{192,256},{256,320},{320,384},{384,448},... | collective-permute-start | bytes 1572872 | tf_op jit(solution)/shard_map/ppermute | solution.py:22
  26.4 6.7 %collective-permute-start.1 = (bf16[1,2,128,256]{3,2,1,0:T(8,128)(2,1)S(1)}, bf16[1,2,128,256]{3,2,1,0:T(8,128)(2,1)S(1)}, u32[]{:S(2)}, u32[]{:S(2)}) collective-permute-start(bf16[1,2,128,256]{3,2,1,0:T(8,128)(2,1)S(1)} %copy-done.5), channel_id=1, source_target_pairs={{0,448},{64,0},{128,64},{192,128},{256,192},{320,256},{384,320},{4... | collective-permute-start | bytes 393224 | tf_op jit(solution)/shard_map/ppermute | solution.py:22
  33.1 12.5 %collective-permute-start.2 = (bf16[256,256]{1,0:T(8,128)(2,1)S(1)}, bf16[256,256]{1,0:T(8,128)(2,1)S(1)}, u32[]{:S(2)}, u32[]{:S(2)}) collective-permute-start(bf16[256,256]{1,0:T(8,128)(2,1)S(1)} %bitcast.25), channel_id=1, source_target_pairs={{0,1},{1,2},{2,3},{3,0},{4,5},{5,6},{6,7},{7,4},{8,9},{9,10},{10,1... | collective-permute-start | bytes 393224 | tf_op jit(solution)/shard_map/ppermute | solution.py:382
  45.6 27.6 %all-to-all-start.1 = ((bf16[16,144,128]{2,1,0:T(8,128)(2,1)}), bf16[16,144,128]{2,1,0:T(8,128)(2,1)S(1)}, u32[]{:S(2)}, u32[]{:S(2)}) async-start(bf16[16,144,128]{2,1,0:T(8,128)(2,1)} %selected_pieces.1), calls=%async_computation.1 | async-start | bytes 1179648 | tf_op jit(solution)/shard_map/all_to_all | solution.py:26
  49.5 23.7 %collective-permute-start.5 = (bf16[1,1,128,2048]{3,2,1,0:T(8,128)(2,1)S(1)}, bf16[1,1,128,2048]{3,2,1,0:T(8,128)(2,1)S(1)}, u32[]{:S(2)}, u32[]{:S(2)}) collective-permute-start(bf16[1,1,128,2048]{3,2,1,0:T(8,128)(2,1)S(1)} %get-tuple-element.58), channel_id=1, source_target_pairs={{0,64},{64,128},{128,192},{192,256},{256,320},{320,384},{384,448},... | collective-permute-start | bytes 1572872 | tf_op jit(solution)/shard_map/ppermute | solution.py:22
  52.7 8.1 %collective-permute-start.3 = (bf16[256,256]{1,0:T(8,128)(2,1)S(1)}, bf16[256,256]{1,0:T(8,128)(2,1)S(1)}, u32[]{:S(2)}, u32[]{:S(2)}) collective-permute-start(bf16[256,256]{1,0:T(8,128)(2,1)S(1)} %bitcast.26), channel_id=1, source_target_pairs={{0,2},{1,3},{2,0},{3,1},{4,6},{5,7},{6,4},{7,5},{8,10},{9,11},{10,... | collective-permute-start | bytes 393224 | tf_op jit(solution)/shard_map/ppermute | solution.py:382
  57.4 6.4 %collective-permute-start.4 = (bf16[256,256]{1,0:T(8,128)(2,1)S(1)}, bf16[256,256]{1,0:T(8,128)(2,1)S(1)}, u32[]{:S(2)}, u32[]{:S(2)}) collective-permute-start(bf16[256,256]{1,0:T(8,128)(2,1)S(1)} %bitcast.27), channel_id=1, source_target_pairs={{0,3},{1,0},{2,1},{3,2},{4,7},{5,4},{6,5},{7,6},{8,11},{9,8},{10,9... | collective-permute-start | bytes 393224 | tf_op jit(solution)/shard_map/ppermute | solution.py:382
  73.2 11.9 %copy-start = (bf16[16,144,128]{2,1,0:T(8,128)(2,1)}, bf16[16,144,128]{2,1,0:T(8,128)(2,1)S(1)}, u32[]{:S(2)}) copy-start(bf16[16,144,128]{2,1,0:T(8,128)(2,1)S(1)} %all-to-all-done.1.second_ref.down_ref) | copy-start | bytes 1769476
  74.4 12.1 %all-to-all-start.2 = ((bf16[4,2,2,64,128]{4,3,2,1,0:T(8,128)(2,1)}), bf16[4,2,2,64,128]{4,3,2,1,0:T(8,128)(2,1)S(1)}, u32[]{:S(2)}, u32[]{:S(2)}) async-start(bf16[4,2,2,64,128]{4,3,2,1,0:T(8,128)(2,1)} %get-tuple-element.35), calls=%async_computation.2 | async-start | bytes 524288 | tf_op jit(solution)/shard_map/all_to_all | solution.py:26
  78.5 2.2 %copy-start.3 = (bf16[1024,2048]{1,0:T(8,128)(2,1)S(1)}, bf16[1024,2048]{1,0:T(8,128)(2,1)}, u32[]{:S(2)}) copy-start(bf16[1024,2048]{1,0:T(8,128)(2,1)} %all-gather.3.cloned.1.call-done) | copy-start | bytes 12582916
  80.7 11.0 %copy-start.4 = (s32[1,2,1]{1,2,0:T(1,128)S(1)}, s32[1,2,1]{1,2,0:T(1,128)}, u32[]{:S(2)}) copy-start(s32[1,2,1]{1,2,0:T(1,128)} %param.13) | copy-start | bytes 28
  85.1 1.4 %copy-start.1 = (f32[256,2048]{1,0:T(8,128)}, f32[256,2048]{1,0:T(8,128)S(1)}, u32[]{:S(2)}) copy-start(f32[256,2048]{1,0:T(8,128)S(1)} %get-tuple-element.47.product_ref) | copy-start | bytes 6291460
  87.5 21.5 %all-to-all-start.3 = ((bf16[16,2,32,256]{3,2,1,0:T(8,128)(2,1)}), bf16[16,2,32,256]{3,2,1,0:T(8,128)(2,1)S(1)}, u32[]{:S(2)}, u32[]{:S(2)}) async-start(bf16[16,2,32,256]{3,2,1,0:T(8,128)(2,1)} %get-tuple-element.45), calls=%async_computation.3 | async-start | bytes 1048576 | tf_op jit(solution)/shard_map/all_to_all | solution.py:26
  92.2 14.6 %collective-permute-start.6 = (bf16[256,256]{1,0:T(8,128)(2,1)S(1)}, bf16[256,256]{1,0:T(8,128)(2,1)S(1)}, u32[]{:S(2)}, u32[]{:S(2)}) collective-permute-start(bf16[256,256]{1,0:T(8,128)(2,1)S(1)} %get-tuple-element.50), channel_id=1, source_target_pairs={{0,1},{1,2},{2,3},{3,0},{4,5},{5,6},{6,7},{7,4},{8,9},{9,10},{10,1... | collective-permute-start | bytes 393224 | tf_op jit(solution)/shard_map/ppermute | solution.py:407
  95.9 10.9 %collective-permute-start.7 = (bf16[256,256]{1,0:T(8,128)(2,1)S(1)}, bf16[256,256]{1,0:T(8,128)(2,1)S(1)}, u32[]{:S(2)}, u32[]{:S(2)}) collective-permute-start(bf16[256,256]{1,0:T(8,128)(2,1)S(1)} %get-tuple-element.51), channel_id=1, source_target_pairs={{0,2},{1,3},{2,0},{3,1},{4,6},{5,7},{6,4},{7,5},{8,10},{9,11},{10,... | collective-permute-start | bytes 393224 | tf_op jit(solution)/shard_map/ppermute | solution.py:407
  100.2 6.6 %collective-permute-start.8 = (bf16[256,256]{1,0:T(8,128)(2,1)S(1)}, bf16[256,256]{1,0:T(8,128)(2,1)S(1)}, u32[]{:S(2)}, u32[]{:S(2)}) collective-permute-start(bf16[256,256]{1,0:T(8,128)(2,1)S(1)} %get-tuple-element.52), channel_id=1, source_target_pairs={{0,3},{1,0},{2,1},{3,2},{4,7},{5,4},{6,5},{7,6},{8,11},{9,8},{10,9... | collective-permute-start | bytes 393224 | tf_op jit(solution)/shard_map/ppermute | solution.py:407
  106.8 0.7 copy-start.2
  109.9 4.0 %collective-permute-start.9 = (f32[2,2,32,256]{3,2,1,0:T(8,128)S(1)}, f32[2,2,32,256]{3,2,1,0:T(8,128)S(1)}, u32[]{:S(2)}, u32[]{:S(2)}) collective-permute-start(f32[2,2,32,256]{3,2,1,0:T(8,128)S(1)} %slot_sums.3), channel_id=1, source_target_pairs={{0,4},{4,0},{8,12},{12,8},{16,20},{20,16},{24,28},{28,24},{32,36},... | collective-permute-start | bytes 393224 | tf_op jit(solution)/shard_map/ppermute | solution.py:416
Sparse Core Ops, SparseCore 0:
  10.1 66.8 all-gather.2

commit v4 on v3

--- a/solution.py
+++ b/solution.py
@@ -94,20 +94,13 @@
 def weight_kernel(micro, quarters, first_ref, *refs):
     acts, cots = refs[:micro], refs[micro : micro + quarters]
     gathered_ref = refs[micro + quarters]
-    outs, back_ref, held_ref, sems = refs[micro + quarters + 1 : -3], *refs[-3:]
-    group = held_ref.shape[1]
-    copies = []
+    outs, back_ref = refs[micro + quarters + 1 : -1], refs[-1]
+    holders, _, width = gathered_ref.shape
+    group = holders // quarters
+    rows = jnp.concatenate([ref[0, 0] for ref in acts], axis=0)
     for k in range(quarters):
         quarter = lax.rem(first_ref[0] + k, quarters)
-        copy = pltpu.make_async_copy(
-            gathered_ref.at[pl.ds(quarter * group, group)], held_ref.at[k], sems.at[k]
-        )
-        copy.start()
-        copies.append(copy)
-    rows = jnp.concatenate([ref[0, 0] for ref in acts], axis=0)
-    for k in range(quarters):
-        copies[k].wait()
-        weight = held_ref[k].reshape(-1, held_ref.shape[3])
+        weight = gathered_ref[pl.ds(quarter * group, group)].reshape(-1, width)
         outs[k][...] = nt_dot(rows, weight).astype(bf16)
         back = jnp.dot(cots[(quarters - k) % quarters][...], weight, preferred_element_type=f32)
         if k == 0:
@@ -125,15 +118,9 @@
         functools.partial(weight_kernel, micro, quarters),
         out_shape=(jax.ShapeDtypeStruct((rows, group * cols), bf16),) * quarters
         + (jax.ShapeDtypeStruct((rows, width), f32),),
-        in_specs=[smem()]
-        + [pl.BlockSpec(memory_space=pltpu.VMEM)] * (micro + quarters)
-        + [pl.BlockSpec(memory_space=pltpu.HBM)],
+        in_specs=[smem()] + [pl.BlockSpec(memory_space=pltpu.VMEM)] * (micro + quarters + 1),
         out_specs=(pl.BlockSpec(memory_space=pltpu.VMEM),) * (quarters + 1),
-        scratch_shapes=[
-            pltpu.VMEM((quarters, group, cols, width), bf16),
-            pltpu.SemaphoreType.DMA((quarters,)),
-        ],
-        compiler_params=params(),
+        compiler_params=pltpu.CompilerParams(vmem_limit_bytes=VMEM_LIMIT),
         cost_estimate=pl.CostEstimate(
             flops=4 * rows * width * cols * holders,
             bytes_accessed=2 * holders * cols * (width + 2 * rows) + 4 * rows * width,

time: 122 us -> 121 us (level)
  waiting for transfers between devices: 24.1 us -> 26.4 us
  Pallas kernels: 17.3 us -> 15.3 us
  starting transfers between devices: 58.8 us -> 57 us
    pallas_call x1, Pallas kernels: 4.44 us -> 2.4 us  [weight_products(): pl.pallas_call(functools.partial(weight_kernel, micro, quarters), out_sha...]
    all_to_all x4, waiting for transfers between devices: 16.8 us -> 18.8 us  [exchanged(): return lax.all_to_all(array, axis, split_axis=0, concat_axis=0, tiled=True)]
    ppermute x3, starting transfers between devices: 11.1 us -> 9.77 us  [shards(): lax.ppermute(base_parts[k], 'mp', [(i, (i + k) % quarters) for i in range...]
  transfers between devices with their start and end apart: 15 -> 15, of which waited for: 7 -> 8; matrix products, arithmetic and copies ran while one was open for 2% -> 2% of each run, Pallas kernels for 12% -> 11%
where the time goes in v4:
time: 121 us; the launch traced here: 120 us
  starting transfers between devices  57 us (47%)
  waiting for transfers between devices  26.4 us (22%)
  Pallas kernels  15.3 us (13%)
  between operations  14.2 us (12%)
  local copies, waits for them, and re-layouts  6.18 us (5%)
    all_to_all x4, starting transfers between devices, exchanged(): return lax.all_to_all(array, axis, split_axis=0, concat_axis=0, tiled=True)  24.5 us
    all_to_all x4, waiting for transfers between devices, exchanged(): return lax.all_to_all(array, axis, split_axis=0, concat_axis=0, tiled=True)  18.8 us
    ppermute x3, starting transfers between devices, shards(): lax.ppermute(flat_cots, 'mp', [(i, (i + k) % quarters) for i in range(qua...  10.5 us
    ppermute x3, starting transfers between devices, passed_along(): lax.ppermute(array, axis, [(i, (i + by) % devices) for i in range(devices)])  10.3 us
    ppermute x3, starting transfers between devices, shards(): lax.ppermute(base_parts[k], 'mp', [(i, (i + k) % quarters) for i in range...  9.77 us
    unnamed x12, local copies, waits for them, and re-layouts  4.2 us
    ppermute x3, waiting for transfers between devices, shards(): lax.ppermute(flat_cots, 'mp', [(i, (i + k) % quarters) for i in range(qua...  3.62 us
    ppermute x3, waiting for transfers between devices, passed_along(): lax.ppermute(array, axis, [(i, (i + by) % devices) for i in range(devices)])  2.91 us
  transfers between devices with their start and end apart: 15, of which 8 were waited for; matrix products, arithmetic and copies ran while one was open for 2% of the time, Pallas kernels for 11%

profile of v4, /device:TPU:1, one launch (start us, length us, event | category | flops | bytes accessed | tf_op | source)
XLA Modules:
  0.0 120.0 jit_solution(13573354492294505110)
XLA Ops:
  7.9 2.1 %packed_adapters.1 = bf16[16,152,128]{2,1,0:T(8,128)(2,1)} custom-call(s32[1,2]{1,0:T(1,128)} %bitcast.37, s32[1,32]{1,0:T(1,128)} %table_ref.1, bf16[2,64,2048]{2,1,0:T(8,128)(2,1)} %bitcast.33, bf16[2,64,256]{2,1,0:T(8,128)(2,1)} %bitcast.36), custom_call_target="tpu_custom_call" | custom-call | tf_op jit(solution)/shard_map/packed_adapters/pallas_call | solution.py:76
  10.1 11.8 %all-to-all-start = ((bf16[16,152,128]{2,1,0:T(8,128)(2,1)}), bf16[16,152,128]{2,1,0:T(8,128)(2,1)S(1)}, u32[]{:S(2)}, u32[]{:S(2)}) async-start(bf16[16,152,128]{2,1,0:T(8,128)(2,1)} %packed_adapters.1), calls=%async_computation | async-start | bytes 1245184 | tf_op jit(solution)/shard_map/all_to_all | solution.py:26
  21.9 1.3 %fusion.1 = (bf16[1,1,128,2048]{3,2,1,0:T(8,128)(2,1)S(1)}, bf16[1,1,128,2048]{3,2,1,0:T(8,128)(2,1)S(1)}) fusion(bf16[1,2,128,2048]{3,2,1,0:T(8,128)(2,1)} %param.7), kind=kLoop, calls=%fused_computation.5 | loop fusion | bytes 2097152 | tf_op jit(solution)/shard_map/slice | solution.py:359
  23.2 3.2 %collective-permute-start = (bf16[1,1,128,2048]{3,2,1,0:T(8,128)(2,1)S(1)}, bf16[1,1,128,2048]{3,2,1,0:T(8,128)(2,1)S(1)}, u32[]{:S(2)}, u32[]{:S(2)}) collective-permute-start(bf16[1,1,128,2048]{3,2,1,0:T(8,128)(2,1)S(1)} %get-tuple-element.59), channel_id=1, source_target_pairs={{0,64},{64,128},{128,192},{192,256},{256,320},{320,384},{384,448},... | collective-permute-start | bytes 1572872 | tf_op jit(solution)/shard_map/ppermute | solution.py:22
  26.4 3.8 %collective-permute-start.1 = (bf16[1,2,128,256]{3,2,1,0:T(8,128)(2,1)S(1)}, bf16[1,2,128,256]{3,2,1,0:T(8,128)(2,1)S(1)}, u32[]{:S(2)}, u32[]{:S(2)}) collective-permute-start(bf16[1,2,128,256]{3,2,1,0:T(8,128)(2,1)S(1)} %copy-done.5), channel_id=1, source_target_pairs={{0,448},{64,0},{128,64},{192,128},{256,192},{320,256},{384,320},{4... | collective-permute-start | bytes 393224 | tf_op jit(solution)/shard_map/ppermute | solution.py:22
  30.2 2.9 %collective-permute-done.1 = bf16[1,2,128,256]{3,2,1,0:T(8,128)(2,1)S(1)} collective-permute-done((bf16[1,2,128,256]{3,2,1,0:T(8,128)(2,1)S(1)}, bf16[1,2,128,256]{3,2,1,0:T(8,128)(2,1)S(1)}, u32[]{:S(2)}, u32[]{:S(2)}) %collective-permute-start.1) | collective-permute-done | bytes 131104 | tf_op jit(solution)/shard_map/ppermute | solution.py:22
  33.1 3.1 %collective-permute-start.2 = (bf16[256,256]{1,0:T(8,128)(2,1)S(1)}, bf16[256,256]{1,0:T(8,128)(2,1)S(1)}, u32[]{:S(2)}, u32[]{:S(2)}) collective-permute-start(bf16[256,256]{1,0:T(8,128)(2,1)S(1)} %bitcast.25), channel_id=1, source_target_pairs={{0,1},{1,2},{2,3},{3,0},{4,5},{5,6},{6,7},{7,4},{8,9},{9,10},{10,1... | collective-permute-start | bytes 393224 | tf_op jit(solution)/shard_map/ppermute | solution.py:369
  36.2 7.3 %all-to-all-done.first_ref = bf16[16,152,128]{2,1,0:T(8,128)(2,1)S(1)} async-done(((bf16[16,152,128]{2,1,0:T(8,128)(2,1)}), bf16[16,152,128]{2,1,0:T(8,128)(2,1)S(1)}, u32[]{:S(2)}, u32[]{:S(2)}) %all-to-all-start) | async-done | bytes 622624 | tf_op jit(solution)/shard_map/all_to_all | solution.py:26
  44.0 1.6 %selected_pieces.1 = bf16[16,144,128]{2,1,0:T(8,128)(2,1)} custom-call(s32[32]{0:T(128)S(1)} %reshape.32.slots_ref.marks_ref, bf16[16,152,128]{2,1,0:T(8,128)(2,1)S(1)} %all-to-all-done.first_ref), custom_call_target="tpu_custom_call" | custom-call | tf_op jit(solution)/shard_map/selected_pieces/pallas_call | solution.py:194
  45.6 3.8 %all-to-all-start.1 = ((bf16[16,144,128]{2,1,0:T(8,128)(2,1)}), bf16[16,144,128]{2,1,0:T(8,128)(2,1)S(1)}, u32[]{:S(2)}, u32[]{:S(2)}) async-start(bf16[16,144,128]{2,1,0:T(8,128)(2,1)} %selected_pieces.1), calls=%async_computation.1 | async-start | bytes 1179648 | tf_op jit(solution)/shard_map/all_to_all | solution.py:26
  49.5 3.2 %collective-permute-start.5 = (bf16[1,1,128,2048]{3,2,1,0:T(8,128)(2,1)S(1)}, bf16[1,1,128,2048]{3,2,1,0:T(8,128)(2,1)S(1)}, u32[]{:S(2)}, u32[]{:S(2)}) collective-permute-start(bf16[1,1,128,2048]{3,2,1,0:T(8,128)(2,1)S(1)} %get-tuple-element.58), channel_id=1, source_target_pairs={{0,64},{64,128},{128,192},{192,256},{256,320},{320,384},{384,448},... | collective-permute-start | bytes 1572872 | tf_op jit(solution)/shard_map/ppermute | solution.py:22
  52.7 4.7 %collective-permute-start.3 = (bf16[256,256]{1,0:T(8,128)(2,1)S(1)}, bf16[256,256]{1,0:T(8,128)(2,1)S(1)}, u32[]{:S(2)}, u32[]{:S(2)}) collective-permute-start(bf16[256,256]{1,0:T(8,128)(2,1)S(1)} %bitcast.26), channel_id=1, source_target_pairs={{0,2},{1,3},{2,0},{3,1},{4,6},{5,7},{6,4},{7,5},{8,10},{9,11},{10,... | collective-permute-start | bytes 393224 | tf_op jit(solution)/shard_map/ppermute | solution.py:369
  57.4 2.8 %collective-permute-start.4 = (bf16[256,256]{1,0:T(8,128)(2,1)S(1)}, bf16[256,256]{1,0:T(8,128)(2,1)S(1)}, u32[]{:S(2)}, u32[]{:S(2)}) collective-permute-start(bf16[256,256]{1,0:T(8,128)(2,1)S(1)} %bitcast.27), channel_id=1, source_target_pairs={{0,3},{1,0},{2,1},{3,2},{4,7},{5,4},{6,5},{7,6},{8,11},{9,8},{10,9... | collective-permute-start | bytes 393224 | tf_op jit(solution)/shard_map/ppermute | solution.py:369
  60.8 3.0 %collective-permute-done.4.refs_5_ = bf16[256,256]{1,0:T(8,128)(2,1)S(1)} collective-permute-done((bf16[256,256]{1,0:T(8,128)(2,1)S(1)}, bf16[256,256]{1,0:T(8,128)(2,1)S(1)}, u32[]{:S(2)}, u32[]{:S(2)}) %collective-permute-start.4) | collective-permute-done | bytes 131104 | tf_op jit(solution)/shard_map/ppermute | solution.py:369
  63.8 9.4 %all-to-all-done.1.second_ref.down_ref = bf16[16,144,128]{2,1,0:T(8,128)(2,1)S(1)} async-done(((bf16[16,144,128]{2,1,0:T(8,128)(2,1)}), bf16[16,144,128]{2,1,0:T(8,128)(2,1)S(1)}, u32[]{:S(2)}, u32[]{:S(2)}) %all-to-all-start.1) | async-done | bytes 589856 | tf_op jit(solution)/shard_map/all_to_all | solution.py:26
  73.2 1.2 %rank_parts.1 = (bf16[4,2,2,64,128]{4,3,2,1,0:T(8,128)(2,1)}, f32[2,64,256]{2,1,0:T(8,128)S(1)}) custom-call(bf16[16,144,128]{2,1,0:T(8,128)(2,1)S(1)} %all-to-all-done.1.second_ref.down_ref, bf16[2,128,256]{2,1,0:T(8,128)(2,1)S(1)} %bitcast.28, bf16[1,1,128,2048]{3,2,1,0:T(8,128)(2,1)S(1)} %collective-permute-done.refs_0_, ...), custom_call_target="tpu_custom_call" | custom-call | tf_op jit(solution)/shard_map/rank_parts/pallas_call | solution.py:160
  74.4 4.0 %all-to-all-start.2 = ((bf16[4,2,2,64,128]{4,3,2,1,0:T(8,128)(2,1)}), bf16[4,2,2,64,128]{4,3,2,1,0:T(8,128)(2,1)S(1)}, u32[]{:S(2)}, u32[]{:S(2)}) async-start(bf16[4,2,2,64,128]{4,3,2,1,0:T(8,128)(2,1)} %get-tuple-element.35), calls=%async_computation.2 | async-start | bytes 524288 | tf_op jit(solution)/shard_map/all_to_all | solution.py:26
  78.5 2.2 %copy-done.3 = bf16[1024,2048]{1,0:T(8,128)(2,1)S(1)} copy-done((bf16[1024,2048]{1,0:T(8,128)(2,1)S(1)}, bf16[1024,2048]{1,0:T(8,128)(2,1)}, u32[]{:S(2)}) %copy-start.3) | copy-done | bytes 4194328
  80.7 2.4 %weight_products.1 = (bf16[256,256]{1,0:T(8,128)(2,1)S(1)}, bf16[256,256]{1,0:T(8,128)(2,1)S(1)}, bf16[256,256]{1,0:T(8,128)(2,1)S(1)}, bf16[256,256]{1,0:T(8,128)(2,1)S(1)}, f32[256,2048]{1,0:T(8,128)S(1)}) custom-call(s32[1]{0:T(128)} %bitcast.6.first_ref, bf16[1,1,128,2048]{3,2,1,0:T(8,128)(2,1)S(1)} %collective-permute-done.refs_0_, ...), custom_call_target="tpu_custom_call" | custom-call | flops 2147483648 | bytes 7340032 | tf_op jit(solution)/shard_map/weight_products/pallas_call | solution.py:117
  83.1 1.3 %copy-done.1 = f32[256,2048]{1,0:T(8,128)} copy-done((f32[256,2048]{1,0:T(8,128)}, f32[256,2048]{1,0:T(8,128)S(1)}, u32[]{:S(2)}) %copy-start.1) | copy-done | bytes 2097176
  85.2 1.0 ranks_and_pieces.1
  86.2 4.8 %all-to-all-start.3 = ((bf16[16,2,32,256]{3,2,1,0:T(8,128)(2,1)}), bf16[16,2,32,256]{3,2,1,0:T(8,128)(2,1)S(1)}, u32[]{:S(2)}, u32[]{:S(2)}) async-start(bf16[16,2,32,256]{3,2,1,0:T(8,128)(2,1)} %get-tuple-element.45), calls=%async_computation.3 | async-start | bytes 1048576 | tf_op jit(solution)/shard_map/all_to_all | solution.py:26
  91.5 2.4 %collective-permute-start.6 = (bf16[256,256]{1,0:T(8,128)(2,1)S(1)}, bf16[256,256]{1,0:T(8,128)(2,1)S(1)}, u32[]{:S(2)}, u32[]{:S(2)}) collective-permute-start(bf16[256,256]{1,0:T(8,128)(2,1)S(1)} %get-tuple-element.50), channel_id=1, source_target_pairs={{0,1},{1,2},{2,3},{3,0},{4,5},{5,6},{6,7},{7,4},{8,9},{9,10},{10,1... | collective-permute-start | bytes 393224 | tf_op jit(solution)/shard_map/ppermute | solution.py:394
  93.9 4.3 %collective-permute-start.7 = (bf16[256,256]{1,0:T(8,128)(2,1)S(1)}, bf16[256,256]{1,0:T(8,128)(2,1)S(1)}, u32[]{:S(2)}, u32[]{:S(2)}) collective-permute-start(bf16[256,256]{1,0:T(8,128)(2,1)S(1)} %get-tuple-element.51), channel_id=1, source_target_pairs={{0,2},{1,3},{2,0},{3,1},{4,6},{5,7},{6,4},{7,5},{8,10},{9,11},{10,... | collective-permute-start | bytes 393224 | tf_op jit(solution)/shard_map/ppermute | solution.py:394
  98.2 3.1 %collective-permute-start.8 = (bf16[256,256]{1,0:T(8,128)(2,1)S(1)}, bf16[256,256]{1,0:T(8,128)(2,1)S(1)}, u32[]{:S(2)}, u32[]{:S(2)}) collective-permute-start(bf16[256,256]{1,0:T(8,128)(2,1)S(1)} %get-tuple-element.52), channel_id=1, source_target_pairs={{0,3},{1,0},{2,1},{3,2},{4,7},{5,4},{6,5},{7,6},{8,11},{9,8},{10,9... | collective-permute-start | bytes 393224 | tf_op jit(solution)/shard_map/ppermute | solution.py:394
  101.9 2.9 %input_gradients.1 = bf16[2,128,2048]{2,1,0:T(8,128)(2,1)} custom-call(s32[2]{0:T(128)} %fusion.live_ref, bf16[2,64,128]{2,1,0:T(8,128)(2,1)} %get-tuple-element.61.ranks_ref, bf16[16,144,128]{2,1,0:T(8,128)(2,1)} %copy-done, f32[256,2048]{1,0:T(8,128)} %copy-done.1), custom_call_target="tpu_custom_call" | custom-call | flops 67108864 | bytes 3145728 | tf_op jit(solution)/shard_map/input_gradients/pallas_call | solution.py:222
  105.4 1.5 %layer_outputs.1 = bf16[2,128,256]{2,1,0:T(8,128)(2,1)} custom-call(s32[2]{0:T(128)S(1)} %copy-done.2, bf16[2,64,128]{2,1,0:T(8,128)(2,1)S(1)} %get-tuple-element.60.ranks_ref, f32[2,64,256]{2,1,0:T(8,128)S(1)} %get-tuple-element.48.up_ref, bf16[256,256]{1,0:T(8,128)(2,1)S(1)} %get-tuple-element.49.refs_0_, ...), custom_call_target="tpu_custom_call" | custom-call | tf_op jit(solution)/shard_map/layer_outputs/pallas_call | solution.py:252
  106.9 1.4 %all-to-all-done.3.pieces_ref = bf16[16,2,32,256]{3,2,1,0:T(8,128)(2,1)S(1)} async-done(((bf16[16,2,32,256]{3,2,1,0:T(8,128)(2,1)}), bf16[16,2,32,256]{3,2,1,0:T(8,128)(2,1)S(1)}, u32[]{:S(2)}, u32[]{:S(2)}) %all-to-all-start.3) | async-done | bytes 524320 | tf_op jit(solution)/shard_map/all_to_all | solution.py:26
  108.3 0.9 slot_sums.3
  109.2 1.9 %collective-permute-start.9 = (f32[2,2,32,256]{3,2,1,0:T(8,128)S(1)}, f32[2,2,32,256]{3,2,1,0:T(8,128)S(1)}, u32[]{:S(2)}, u32[]{:S(2)}) collective-permute-start(f32[2,2,32,256]{3,2,1,0:T(8,128)S(1)} %slot_sums.3), channel_id=1, source_target_pairs={{0,4},{4,0},{8,12},{12,8},{16,20},{20,16},{24,28},{28,24},{32,36},... | collective-permute-start | bytes 393224 | tf_op jit(solution)/shard_map/ppermute | solution.py:403
  111.1 0.9 slot_sums.2.own_ref
  112.4 0.7 placed_sums.1
  (26 shorter events, 4.8 us)
Async XLA Ops:
  7.2 19.2 %copy-start.5 = (bf16[1,2,128,256]{3,2,1,0:T(8,128)(2,1)S(1)}, bf16[1,2,128,256]{3,2,1,0:T(8,128)(2,1)}, u32[]{:S(2)}) copy-start(bf16[1,2,128,256]{3,2,1,0:T(8,128)(2,1)} %param.8) | copy-start | bytes 393220
  7.2 71.3 %all-gather.3.cloned.1.call-start = ((), (), s32[]{:S(2)}) async-start(), calls=%async_computation.4 | async-start | bytes 4456448 | tf_op jit(solution)/shard_map/all_gather | solution.py:366
  10.1 33.5 %all-to-all-start = ((bf16[16,152,128]{2,1,0:T(8,128)(2,1)}), bf16[16,152,128]{2,1,0:T(8,128)(2,1)S(1)}, u32[]{:S(2)}, u32[]{:S(2)}) async-start(bf16[16,152,128]{2,1,0:T(8,128)(2,1)} %packed_adapters.1), calls=%async_computation | async-start | bytes 1245184 | tf_op jit(solution)/shard_map/all_to_all | solution.py:26
  23.2 22.5 %collective-permute-start = (bf16[1,1,128,2048]{3,2,1,0:T(8,128)(2,1)S(1)}, bf16[1,1,128,2048]{3,2,1,0:T(8,128)(2,1)S(1)}, u32[]{:S(2)}, u32[]{:S(2)}) collective-permute-start(bf16[1,1,128,2048]{3,2,1,0:T(8,128)(2,1)S(1)} %get-tuple-element.59), channel_id=1, source_target_pairs={{0,64},{64,128},{128,192},{192,256},{256,320},{320,384},{384,448},... | collective-permute-start | bytes 1572872 | tf_op jit(solution)/shard_map/ppermute | solution.py:22
  26.4 6.7 %collective-permute-start.1 = (bf16[1,2,128,256]{3,2,1,0:T(8,128)(2,1)S(1)}, bf16[1,2,128,256]{3,2,1,0:T(8,128)(2,1)S(1)}, u32[]{:S(2)}, u32[]{:S(2)}) collective-permute-start(bf16[1,2,128,256]{3,2,1,0:T(8,128)(2,1)S(1)} %copy-done.5), channel_id=1, source_target_pairs={{0,448},{64,0},{128,64},{192,128},{256,192},{320,256},{384,320},{4... | collective-permute-start | bytes 393224 | tf_op jit(solution)/shard_map/ppermute | solution.py:22
  33.1 12.5 %collective-permute-start.2 = (bf16[256,256]{1,0:T(8,128)(2,1)S(1)}, bf16[256,256]{1,0:T(8,128)(2,1)S(1)}, u32[]{:S(2)}, u32[]{:S(2)}) collective-permute-start(bf16[256,256]{1,0:T(8,128)(2,1)S(1)} %bitcast.25), channel_id=1, source_target_pairs={{0,1},{1,2},{2,3},{3,0},{4,5},{5,6},{6,7},{7,4},{8,9},{9,10},{10,1... | collective-permute-start | bytes 393224 | tf_op jit(solution)/shard_map/ppermute | solution.py:369
  45.6 27.6 %all-to-all-start.1 = ((bf16[16,144,128]{2,1,0:T(8,128)(2,1)}), bf16[16,144,128]{2,1,0:T(8,128)(2,1)S(1)}, u32[]{:S(2)}, u32[]{:S(2)}) async-start(bf16[16,144,128]{2,1,0:T(8,128)(2,1)} %selected_pieces.1), calls=%async_computation.1 | async-start | bytes 1179648 | tf_op jit(solution)/shard_map/all_to_all | solution.py:26
  49.5 23.7 %collective-permute-start.5 = (bf16[1,1,128,2048]{3,2,1,0:T(8,128)(2,1)S(1)}, bf16[1,1,128,2048]{3,2,1,0:T(8,128)(2,1)S(1)}, u32[]{:S(2)}, u32[]{:S(2)}) collective-permute-start(bf16[1,1,128,2048]{3,2,1,0:T(8,128)(2,1)S(1)} %get-tuple-element.58), channel_id=1, source_target_pairs={{0,64},{64,128},{128,192},{192,256},{256,320},{320,384},{384,448},... | collective-permute-start | bytes 1572872 | tf_op jit(solution)/shard_map/ppermute | solution.py:22
  52.7 8.1 %collective-permute-start.3 = (bf16[256,256]{1,0:T(8,128)(2,1)S(1)}, bf16[256,256]{1,0:T(8,128)(2,1)S(1)}, u32[]{:S(2)}, u32[]{:S(2)}) collective-permute-start(bf16[256,256]{1,0:T(8,128)(2,1)S(1)} %bitcast.26), channel_id=1, source_target_pairs={{0,2},{1,3},{2,0},{3,1},{4,6},{5,7},{6,4},{7,5},{8,10},{9,11},{10,... | collective-permute-start | bytes 393224 | tf_op jit(solution)/shard_map/ppermute | solution.py:369
  57.4 6.4 %collective-permute-start.4 = (bf16[256,256]{1,0:T(8,128)(2,1)S(1)}, bf16[256,256]{1,0:T(8,128)(2,1)S(1)}, u32[]{:S(2)}, u32[]{:S(2)}) collective-permute-start(bf16[256,256]{1,0:T(8,128)(2,1)S(1)} %bitcast.27), channel_id=1, source_target_pairs={{0,3},{1,0},{2,1},{3,2},{4,7},{5,4},{6,5},{7,6},{8,11},{9,8},{10,9... | collective-permute-start | bytes 393224 | tf_op jit(solution)/shard_map/ppermute | solution.py:369
  73.2 9.9 %copy-start = (bf16[16,144,128]{2,1,0:T(8,128)(2,1)}, bf16[16,144,128]{2,1,0:T(8,128)(2,1)S(1)}, u32[]{:S(2)}) copy-start(bf16[16,144,128]{2,1,0:T(8,128)(2,1)S(1)} %all-to-all-done.1.second_ref.down_ref) | copy-start | bytes 1769476
  74.4 10.7 %all-to-all-start.2 = ((bf16[4,2,2,64,128]{4,3,2,1,0:T(8,128)(2,1)}), bf16[4,2,2,64,128]{4,3,2,1,0:T(8,128)(2,1)S(1)}, u32[]{:S(2)}, u32[]{:S(2)}) async-start(bf16[4,2,2,64,128]{4,3,2,1,0:T(8,128)(2,1)} %get-tuple-element.35), calls=%async_computation.2 | async-start | bytes 524288 | tf_op jit(solution)/shard_map/all_to_all | solution.py:26
  78.5 2.2 %copy-start.3 = (bf16[1024,2048]{1,0:T(8,128)(2,1)S(1)}, bf16[1024,2048]{1,0:T(8,128)(2,1)}, u32[]{:S(2)}) copy-start(bf16[1024,2048]{1,0:T(8,128)(2,1)} %all-gather.3.cloned.1.call-done) | copy-start | bytes 12582916
  80.7 10.3 %copy-start.4 = (s32[1,2,1]{1,2,0:T(1,128)S(1)}, s32[1,2,1]{1,2,0:T(1,128)}, u32[]{:S(2)}) copy-start(s32[1,2,1]{1,2,0:T(1,128)} %param.13) | copy-start | bytes 28
  83.1 1.4 %copy-start.1 = (f32[256,2048]{1,0:T(8,128)}, f32[256,2048]{1,0:T(8,128)S(1)}, u32[]{:S(2)}) copy-start(f32[256,2048]{1,0:T(8,128)S(1)} %get-tuple-element.47.product_ref) | copy-start | bytes 6291460
  86.2 22.1 %all-to-all-start.3 = ((bf16[16,2,32,256]{3,2,1,0:T(8,128)(2,1)}), bf16[16,2,32,256]{3,2,1,0:T(8,128)(2,1)S(1)}, u32[]{:S(2)}, u32[]{:S(2)}) async-start(bf16[16,2,32,256]{3,2,1,0:T(8,128)(2,1)} %get-tuple-element.45), calls=%async_computation.3 | async-start | bytes 1048576 | tf_op jit(solution)/shard_map/all_to_all | solution.py:26
  91.5 13.3 %collective-permute-start.6 = (bf16[256,256]{1,0:T(8,128)(2,1)S(1)}, bf16[256,256]{1,0:T(8,128)(2,1)S(1)}, u32[]{:S(2)}, u32[]{:S(2)}) collective-permute-start(bf16[256,256]{1,0:T(8,128)(2,1)S(1)} %get-tuple-element.50), channel_id=1, source_target_pairs={{0,1},{1,2},{2,3},{3,0},{4,5},{5,6},{6,7},{7,4},{8,9},{9,10},{10,1... | collective-permute-start | bytes 393224 | tf_op jit(solution)/shard_map/ppermute | solution.py:394
  93.9 10.9 %collective-permute-start.7 = (bf16[256,256]{1,0:T(8,128)(2,1)S(1)}, bf16[256,256]{1,0:T(8,128)(2,1)S(1)}, u32[]{:S(2)}, u32[]{:S(2)}) collective-permute-start(bf16[256,256]{1,0:T(8,128)(2,1)S(1)} %get-tuple-element.51), channel_id=1, source_target_pairs={{0,2},{1,3},{2,0},{3,1},{4,6},{5,7},{6,4},{7,5},{8,10},{9,11},{10,... | collective-permute-start | bytes 393224 | tf_op jit(solution)/shard_map/ppermute | solution.py:394
  98.2 6.6 %collective-permute-start.8 = (bf16[256,256]{1,0:T(8,128)(2,1)S(1)}, bf16[256,256]{1,0:T(8,128)(2,1)S(1)}, u32[]{:S(2)}, u32[]{:S(2)}) collective-permute-start(bf16[256,256]{1,0:T(8,128)(2,1)S(1)} %get-tuple-element.52), channel_id=1, source_target_pairs={{0,3},{1,0},{2,1},{3,2},{4,7},{5,4},{6,5},{7,6},{8,11},{9,8},{10,9... | collective-permute-start | bytes 393224 | tf_op jit(solution)/shard_map/ppermute | solution.py:394
  104.8 0.7 copy-start.2
  109.2 3.2 %collective-permute-start.9 = (f32[2,2,32,256]{3,2,1,0:T(8,128)S(1)}, f32[2,2,32,256]{3,2,1,0:T(8,128)S(1)}, u32[]{:S(2)}, u32[]{:S(2)}) collective-permute-start(f32[2,2,32,256]{3,2,1,0:T(8,128)S(1)} %slot_sums.3), channel_id=1, source_target_pairs={{0,4},{4,0},{8,12},{12,8},{16,20},{20,16},{24,28},{28,24},{32,36},... | collective-permute-start | bytes 393224 | tf_op jit(solution)/shard_map/ppermute | solution.py:403
Sparse Core Ops, SparseCore 0:
  10.1 66.8 all-gather.2

commit v5 on v4

--- a/solution.py
+++ b/solution.py
@@ -15,6 +15,7 @@
 bf16, f32 = jnp.bfloat16, jnp.float32
 VMEM_LIMIT = 24 * 1024 * 1024
 WIDE_LIMIT = 60 * 1024 * 1024
+PARTS = 4
 
 
 def passed_along(array, axis, by):
@@ -42,12 +43,48 @@
     return lax.dot_general(a, b, (((0,), (0,)), ((), ())), preferred_element_type=f32)
 
 
-def pack_kernel(halves, langs_ref, table_ref, down_ref, up_ref, out_ref):
+def started(source, target, sem):
+    copy = pltpu.make_async_copy(source, target, sem)
+    copy.start()
+    return copy
+
+
+def pack_kernel(
+    halves,
+    langs_in,
+    table_in,
+    down_in,
+    up_in,
+    out,
+    langs_ref,
+    table_ref,
+    down_ref,
+    up_ref,
+    out_ref,
+    in_sems,
+    out_sems,
+):
     pieces, payload, piece = out_ref.shape
-    own_slots, rank, _ = down_ref.shape
+    own_slots, rank, width = down_ref.shape
     micro, count = langs_ref.shape[1], table_ref.shape[1]
-    group = up_ref.shape[1] * halves // pieces
+    group = rank * halves // pieces
     low, high = own_slots * rank, own_slots * (rank + group)
+    span, chunk = width // PARTS, pieces // PARTS
+    small = [
+        started(langs_in, langs_ref, in_sems.at[0]),
+        started(table_in, table_ref, in_sems.at[1]),
+        started(up_in, up_ref, in_sems.at[2]),
+    ]
+    large = []
+    for i in range(PARTS):
+        columns = pl.ds(i * span, span)
+        large.append(
+            started(
+                down_in.at[:, :, columns], down_ref.at[:, :, columns], in_sems.at[3 + i]
+            )
+        )
+    for copy in small:
+        copy.wait()
     lane = lax.broadcasted_iota(jnp.int32, (1, count), 1)
     row = lax.broadcasted_iota(jnp.int32, (payload - high, piece), 0)
     marks = jnp.zeros((payload - high, piece), f32)
@@ -57,35 +94,44 @@
         marks = jnp.where(row == m, slot, marks)
     marks = marks.astype(bf16)
     ups = [up_ref[k].astype(f32) for k in range(own_slots)]
-    for p in range(pieces):
-        for k in range(own_slots):
-            out_ref[p, k * rank : (k + 1) * rank, :] = down_ref[k, :, p * piece : (p + 1) * piece]
-        top, left = (p // halves) * group, (p % halves) * LANES
-        out_ref[p, low:high, :] = jnp.concatenate(
-            [up[top : top + group, left : left + LANES] for up in ups], axis=0
-        ).astype(bf16)
-        out_ref[p, high:, :] = marks
+    sent = []
+    for i in range(PARTS):
+        large[i].wait()
+        for p in range(i * chunk, (i + 1) * chunk):
+            for k in range(own_slots):
+                out_ref[p, k * rank : (k + 1) * rank, :] = down_ref[
+                    k, :, p * piece : (p + 1) * piece
+                ]
+            top, left = (p // halves) * group, (p % halves) * LANES
+            out_ref[p, low:high, :] = jnp.concatenate(
+                [up[top : top + group, left : left + LANES] for up in ups], axis=0
+            ).astype(bf16)
+            out_ref[p, high:, :] = marks
+        some = pl.ds(i * chunk, chunk)
+        sent.append(started(out_ref.at[some], out.at[some], out_sems.at[i]))
+    for copy in sent:
+        copy.wait()
 
 
 def packed(langs, table, down, up, holders):
     own_slots, rank, width = down.shape
-    columns = up.shape[2]
-    halves = columns // LANES
+    halves = up.shape[2] // LANES
     payload = own_slots * (rank + rank * halves // holders) + 8
-    steps = 1
+    out = (holders, payload, width // holders)
     return pl.pallas_call(
         functools.partial(pack_kernel, halves),
-        grid=(steps,),
-        out_shape=jax.ShapeDtypeStruct((holders, payload, width // holders), bf16),
-        in_specs=[
-            pl.BlockSpec(langs.shape, lambda i: (0, 0)),
-            pl.BlockSpec(table.shape, lambda i: (0, 0)),
-            pl.BlockSpec((own_slots, rank, width // steps), lambda i: (0, 0, i)),
-            pl.BlockSpec((own_slots, rank // steps, columns), lambda i: (0, i, 0)),
+        out_shape=jax.ShapeDtypeStruct(out, bf16),
+        in_specs=[pl.BlockSpec(memory_space=pl.ANY)] * 4,
+        out_specs=pl.BlockSpec(memory_space=pl.ANY),
+        scratch_shapes=[
+            pltpu.VMEM(langs.shape, jnp.int32),
+            pltpu.VMEM(table.shape, jnp.int32),
+            pltpu.VMEM(down.shape, bf16),
+            pltpu.VMEM(up.shape, bf16),
+            pltpu.VMEM(out, bf16),
+            pltpu.SemaphoreType.DMA((3 + PARTS,)),
+            pltpu.SemaphoreType.DMA((PARTS,)),
         ],
-        out_specs=pl.BlockSpec(
-            (holders // steps, payload, width // holders), lambda i: (i, 0, 0)
-        ),
         compiler_params=pltpu.CompilerParams(vmem_limit_bytes=WIDE_LIMIT),
         name="packed_adapters",
     )(langs, table, down, up)
@@ -170,32 +216,41 @@
     )(second, returned, *acts)
 
 
-def select_kernel(micro, own_slots, rank, slots_ref, first_ref, out_ref):
+def select_kernel(micro, own_slots, rank, slots_ref, first_ref, out, out_ref, sems):
     holders = out_ref.shape[0]
     group = out_ref.shape[1] // micro - rank
     low = own_slots * rank
-    for d in range(holders):
-        ups = []
-        for m in range(micro):
-            slot = jnp.minimum(slots_ref[d * micro + m], holders * own_slots - 1)
-            owner, k = slot // own_slots, slot % own_slots
-            rows = pl.ds(pl.multiple_of(k * rank, rank), rank)
-            out_ref[d, m * rank : (m + 1) * rank, :] = first_ref[owner, rows, :]
-            held = first_ref[owner, low : low + own_slots * group, :].astype(f32)
-            up = held[:group]
-            for j in range(1, own_slots):
-                up = jnp.where(k == j, held[j * group : (j + 1) * group], up)
-            ups.append(up)
-        out_ref[d, micro * rank :, :] = jnp.concatenate(ups, axis=0).astype(bf16)
+    chunk = holders // PARTS
+    sent = []
+    for i in range(PARTS):
+        for d in range(i * chunk, (i + 1) * chunk):
+            ups = []
+            for m in range(micro):
+                slot = jnp.minimum(slots_ref[d * micro + m], holders * own_slots - 1)
+                owner, k = lax.div(slot, own_slots), lax.rem(slot, own_slots)
+                rows = pl.ds(pl.multiple_of(k * rank, rank), rank)
+                out_ref[d, m * rank : (m + 1) * rank, :] = first_ref[owner, rows, :]
+                held = first_ref[owner, low : low + own_slots * group, :].astype(f32)
+                up = held[:group]
+                for j in range(1, own_slots):
+                    up = jnp.where(k == j, held[j * group : (j + 1) * group], up)
+                ups.append(up)
+            out_ref[d, micro * rank :, :] = jnp.concatenate(ups, axis=0).astype(bf16)
+        some = pl.ds(i * chunk, chunk)
+        sent.append(started(out_ref.at[some], out.at[some], sems.at[i]))
+    for copy in sent:
+        copy.wait()
 
 
 def selected(slots, first, micro, own_slots, rank, group):
     holders, _, lanes = first.shape
+    out = (holders, micro * (rank + group), lanes)
     return pl.pallas_call(
         functools.partial(select_kernel, micro, own_slots, rank),
-        out_shape=jax.ShapeDtypeStruct((holders, micro * (rank + group), lanes), bf16),
+        out_shape=jax.ShapeDtypeStruct(out, bf16),
         in_specs=[smem(), pl.BlockSpec(memory_space=pltpu.VMEM)],
-        out_specs=pl.BlockSpec(memory_space=pltpu.VMEM),
+        out_specs=pl.BlockSpec(memory_space=pl.ANY),
+        scratch_shapes=[pltpu.VMEM(out, bf16), pltpu.SemaphoreType.DMA((PARTS,))],
         compiler_params=params(),
         name="selected_pieces",
     )(slots, first)
@@ -292,19 +347,20 @@
 
 def slot_kernel(marks_ref, first_ref, pieces_ref, out_ref):
     holders, micro = pieces_ref.shape[:2]
-    for i in range(out_ref.shape[0]):
-        total, square = None, None
-        for d in range(holders):
-            partial = None
-            for m in range(micro):
-                hit = marks_ref[d * micro + m] == first_ref[0] + i
-                term = jnp.where(hit, pieces_ref[d, m].astype(f32), 0.0)
-                partial = term if partial is None else partial + term
-            total = partial if total is None else total + partial
-            squared = partial * partial
-            square = squared if square is None else square + squared
-        out_ref[i, 0] = total
-        out_ref[i, 1] = square
+    out_ref[...] = jnp.zeros_like(out_ref)
+    for d in range(holders):
+        marks = [marks_ref[d * micro + m] for m in range(micro)]
+        for i in range(out_ref.shape[0]):
+            hits = [mark == first_ref[0] + i for mark in marks]
+
+            @pl.when(functools.reduce(jnp.logical_or, hits))
+            def _():
+                partial = None
+                for m in range(micro):
+                    term = jnp.where(hits[m], pieces_ref[d, m].astype(f32), 0.0)
+                    partial = term if partial is None else partial + term
+                out_ref[i, 0] += partial
+                out_ref[i, 1] += partial * partial
 
 
 def slot_sums(marks, first_slot, pieces, own_slots):
@@ -363,7 +419,6 @@
     live = (langs < slot_table.shape[0]).astype(jnp.int32)
 
     weight = jnp.swapaxes(base_weight[0], 0, 1)
-    gathered = lax.all_gather(weight, "dp", axis=0)
     flat_cots = returned.reshape(rows, columns)
     cots = [flat_cots] + [
         lax.ppermute(flat_cots, "mp", [(i, (i + k) % quarters) for i in range(quarters)])
@@ -372,6 +427,8 @@
 
     down = jnp.swapaxes(adapter_down[0], 1, 2)
     first = packed(langs[None, :], slot_language, down, adapter_up[0], holders)
+    first, weight = lax.optimization_barrier((first, weight))
+    gathered = lax.all_gather(weight, "dp", axis=0)
     first = exchanged(first, "dp")
 
     marked = own_slots * (rank + up_rows)

time: 121 us -> 120 us (level)
  waiting for transfers between devices: 26.4 us -> 25 us
  transfers between devices with their start and end apart: 15 -> 15, of which waited for: 8 -> 7; matrix products, arithmetic and copies ran while one was open for 2% -> 2% of each run, Pallas kernels for 11% -> 9%
where the time goes in v5:
time: 120 us; the launch traced here: 119 us
  starting transfers between devices  57.8 us (48%)
  waiting for transfers between devices  25 us (21%)
  Pallas kernels  14.9 us (12%)
  between operations  14.3 us (12%)
  local copies, waits for them, and re-layouts  6.18 us (5%)
    all_to_all x4, starting transfers between devices, exchanged(): return lax.all_to_all(array, axis, split_axis=0, concat_axis=0, tiled=True)  25.3 us
    all_to_all x4, waiting for transfers between devices, exchanged(): return lax.all_to_all(array, axis, split_axis=0, concat_axis=0, tiled=True)  18.1 us
    ppermute x3, starting transfers between devices, shards(): lax.ppermute(flat_cots, 'mp', [(i, (i + k) % quarters) for i in range(qua...  10.5 us
    ppermute x3, starting transfers between devices, passed_along(): lax.ppermute(array, axis, [(i, (i + by) % devices) for i in range(devices)])  10.3 us
    ppermute x3, starting transfers between devices, shards(): lax.ppermute(base_parts[k], 'mp', [(i, (i + k) % quarters) for i in range...  9.77 us
    unnamed x12, local copies, waits for them, and re-layouts  4.2 us
    ppermute x3, waiting for transfers between devices, shards(): lax.ppermute(flat_cots, 'mp', [(i, (i + k) % quarters) for i in range(qua...  3.64 us
    pallas_call x1, Pallas kernels, input_gradients(): pl.pallas_call(functools.partial(gradient_kernel, micro), grid=(steps,),...  2.87 us
  transfers between devices with their start and end apart: 15, of which 7 were waited for; matrix products, arithmetic and copies ran while one was open for 2% of the time, Pallas kernels for 9%

profile of v5, /device:TPU:1, one launch (start us, length us, event | category | flops | bytes accessed | tf_op | source)
XLA Modules:
  0.0 119.0 jit_solution(8701330124569550266)
XLA Ops:
  7.2 2.1 %packed_adapters.1 = bf16[16,152,128]{2,1,0:T(8,128)(2,1)} custom-call(s32[1,2]{1,0:T(1,128)} %bitcast.37, s32[1,32]{1,0:T(1,128)} %table_in.1, bf16[2,64,2048]{2,1,0:T(8,128)(2,1)} %bitcast.33, bf16[2,64,256]{2,1,0:T(8,128)(2,1)} %bitcast.36), custom_call_target="tpu_custom_call" | custom-call | tf_op jit(solution)/shard_map/packed_adapters/pallas_call | solution.py:121
  9.3 11.8 %all-to-all-start = ((bf16[16,152,128]{2,1,0:T(8,128)(2,1)}), bf16[16,152,128]{2,1,0:T(8,128)(2,1)S(1)}, u32[]{:S(2)}, u32[]{:S(2)}) async-start(bf16[16,152,128]{2,1,0:T(8,128)(2,1)} %packed_adapters.1), calls=%async_computation | async-start | bytes 1245184 | tf_op jit(solution)/shard_map/all_to_all | solution.py:27
  21.2 1.3 %fusion.1 = (bf16[1,1,128,2048]{3,2,1,0:T(8,128)(2,1)S(1)}, bf16[1,1,128,2048]{3,2,1,0:T(8,128)(2,1)S(1)}) fusion(bf16[1,2,128,2048]{3,2,1,0:T(8,128)(2,1)} %param.7), kind=kLoop, calls=%fused_computation.5 | loop fusion | bytes 2097152 | tf_op jit(solution)/shard_map/slice | solution.py:415
  22.4 3.2 %collective-permute-start = (bf16[1,1,128,2048]{3,2,1,0:T(8,128)(2,1)S(1)}, bf16[1,1,128,2048]{3,2,1,0:T(8,128)(2,1)S(1)}, u32[]{:S(2)}, u32[]{:S(2)}) collective-permute-start(bf16[1,1,128,2048]{3,2,1,0:T(8,128)(2,1)S(1)} %get-tuple-element.63), channel_id=1, source_target_pairs={{0,64},{64,128},{128,192},{192,256},{256,320},{320,384},{384,448},... | collective-permute-start | bytes 1572872 | tf_op jit(solution)/shard_map/ppermute | solution.py:23
  25.7 3.8 %collective-permute-start.1 = (bf16[1,2,128,256]{3,2,1,0:T(8,128)(2,1)S(1)}, bf16[1,2,128,256]{3,2,1,0:T(8,128)(2,1)S(1)}, u32[]{:S(2)}, u32[]{:S(2)}) collective-permute-start(bf16[1,2,128,256]{3,2,1,0:T(8,128)(2,1)S(1)} %copy-done.5), channel_id=1, source_target_pairs={{0,448},{64,0},{128,64},{192,128},{256,192},{320,256},{384,320},{4... | collective-permute-start | bytes 393224 | tf_op jit(solution)/shard_map/ppermute | solution.py:23
  29.5 2.8 %collective-permute-done.1 = bf16[1,2,128,256]{3,2,1,0:T(8,128)(2,1)S(1)} collective-permute-done((bf16[1,2,128,256]{3,2,1,0:T(8,128)(2,1)S(1)}, bf16[1,2,128,256]{3,2,1,0:T(8,128)(2,1)S(1)}, u32[]{:S(2)}, u32[]{:S(2)}) %collective-permute-start.1) | collective-permute-done | bytes 131104 | tf_op jit(solution)/shard_map/ppermute | solution.py:23
  32.3 3.1 %collective-permute-start.2 = (bf16[256,256]{1,0:T(8,128)(2,1)S(1)}, bf16[256,256]{1,0:T(8,128)(2,1)S(1)}, u32[]{:S(2)}, u32[]{:S(2)}) collective-permute-start(bf16[256,256]{1,0:T(8,128)(2,1)S(1)} %bitcast.25), channel_id=1, source_target_pairs={{0,1},{1,2},{2,3},{3,0},{4,5},{5,6},{6,7},{7,4},{8,9},{9,10},{10,1... | collective-permute-start | bytes 393224 | tf_op jit(solution)/shard_map/ppermute | solution.py:424
  35.4 7.3 %all-to-all-done.first_ref = bf16[16,152,128]{2,1,0:T(8,128)(2,1)S(1)} async-done(((bf16[16,152,128]{2,1,0:T(8,128)(2,1)}), bf16[16,152,128]{2,1,0:T(8,128)(2,1)S(1)}, u32[]{:S(2)}, u32[]{:S(2)}) %all-to-all-start) | async-done | bytes 622624 | tf_op jit(solution)/shard_map/all_to_all | solution.py:27
  43.2 1.5 %selected_pieces.1 = bf16[16,144,128]{2,1,0:T(8,128)(2,1)} custom-call(s32[32]{0:T(128)S(1)} %reshape.32.slots_ref.marks_ref, bf16[16,152,128]{2,1,0:T(8,128)(2,1)S(1)} %all-to-all-done.first_ref), custom_call_target="tpu_custom_call" | custom-call | tf_op jit(solution)/shard_map/selected_pieces/pallas_call | solution.py:248
  44.7 3.8 %all-to-all-start.1 = ((bf16[16,144,128]{2,1,0:T(8,128)(2,1)}), bf16[16,144,128]{2,1,0:T(8,128)(2,1)S(1)}, u32[]{:S(2)}, u32[]{:S(2)}) async-start(bf16[16,144,128]{2,1,0:T(8,128)(2,1)} %selected_pieces.1), calls=%async_computation.1 | async-start | bytes 1179648 | tf_op jit(solution)/shard_map/all_to_all | solution.py:27
  48.5 3.2 %collective-permute-start.5 = (bf16[1,1,128,2048]{3,2,1,0:T(8,128)(2,1)S(1)}, bf16[1,1,128,2048]{3,2,1,0:T(8,128)(2,1)S(1)}, u32[]{:S(2)}, u32[]{:S(2)}) collective-permute-start(bf16[1,1,128,2048]{3,2,1,0:T(8,128)(2,1)S(1)} %get-tuple-element.62), channel_id=1, source_target_pairs={{0,64},{64,128},{128,192},{192,256},{256,320},{320,384},{384,448},... | collective-permute-start | bytes 1572872 | tf_op jit(solution)/shard_map/ppermute | solution.py:23
  51.7 4.7 %collective-permute-start.3 = (bf16[256,256]{1,0:T(8,128)(2,1)S(1)}, bf16[256,256]{1,0:T(8,128)(2,1)S(1)}, u32[]{:S(2)}, u32[]{:S(2)}) collective-permute-start(bf16[256,256]{1,0:T(8,128)(2,1)S(1)} %bitcast.26), channel_id=1, source_target_pairs={{0,2},{1,3},{2,0},{3,1},{4,6},{5,7},{6,4},{7,5},{8,10},{9,11},{10,... | collective-permute-start | bytes 393224 | tf_op jit(solution)/shard_map/ppermute | solution.py:424
  56.4 2.8 %collective-permute-start.4 = (bf16[256,256]{1,0:T(8,128)(2,1)S(1)}, bf16[256,256]{1,0:T(8,128)(2,1)S(1)}, u32[]{:S(2)}, u32[]{:S(2)}) collective-permute-start(bf16[256,256]{1,0:T(8,128)(2,1)S(1)} %bitcast.27), channel_id=1, source_target_pairs={{0,3},{1,0},{2,1},{3,2},{4,7},{5,4},{6,5},{7,6},{8,11},{9,8},{10,9... | collective-permute-start | bytes 393224 | tf_op jit(solution)/shard_map/ppermute | solution.py:424
  59.9 3.0 %collective-permute-done.4.refs_5_ = bf16[256,256]{1,0:T(8,128)(2,1)S(1)} collective-permute-done((bf16[256,256]{1,0:T(8,128)(2,1)S(1)}, bf16[256,256]{1,0:T(8,128)(2,1)S(1)}, u32[]{:S(2)}, u32[]{:S(2)}) %collective-permute-start.4) | collective-permute-done | bytes 131104 | tf_op jit(solution)/shard_map/ppermute | solution.py:424
  62.8 9.3 %all-to-all-done.1.second_ref.down_ref = bf16[16,144,128]{2,1,0:T(8,128)(2,1)S(1)} async-done(((bf16[16,144,128]{2,1,0:T(8,128)(2,1)}), bf16[16,144,128]{2,1,0:T(8,128)(2,1)S(1)}, u32[]{:S(2)}, u32[]{:S(2)}) %all-to-all-start.1) | async-done | bytes 589856 | tf_op jit(solution)/shard_map/all_to_all | solution.py:27
  72.2 1.2 %rank_parts.1 = (bf16[4,2,2,64,128]{4,3,2,1,0:T(8,128)(2,1)}, f32[2,64,256]{2,1,0:T(8,128)S(1)}) custom-call(bf16[16,144,128]{2,1,0:T(8,128)(2,1)S(1)} %all-to-all-done.1.second_ref.down_ref, bf16[2,128,256]{2,1,0:T(8,128)(2,1)S(1)} %bitcast.28, bf16[1,1,128,2048]{3,2,1,0:T(8,128)(2,1)S(1)} %collective-permute-done.refs_0_, ...), custom_call_target="tpu_custom_call" | custom-call | tf_op jit(solution)/shard_map/rank_parts/pallas_call | solution.py:206
  73.4 4.0 %all-to-all-start.2 = ((bf16[4,2,2,64,128]{4,3,2,1,0:T(8,128)(2,1)}), bf16[4,2,2,64,128]{4,3,2,1,0:T(8,128)(2,1)S(1)}, u32[]{:S(2)}, u32[]{:S(2)}) async-start(bf16[4,2,2,64,128]{4,3,2,1,0:T(8,128)(2,1)} %get-tuple-element.38), calls=%async_computation.2 | async-start | bytes 524288 | tf_op jit(solution)/shard_map/all_to_all | solution.py:27
  77.4 2.2 %copy-done.3 = bf16[1024,2048]{1,0:T(8,128)(2,1)S(1)} copy-done((bf16[1024,2048]{1,0:T(8,128)(2,1)S(1)}, bf16[1024,2048]{1,0:T(8,128)(2,1)}, u32[]{:S(2)}) %copy-start.3) | copy-done | bytes 4194328
  79.6 2.4 %weight_products.1 = (bf16[256,256]{1,0:T(8,128)(2,1)S(1)}, bf16[256,256]{1,0:T(8,128)(2,1)S(1)}, bf16[256,256]{1,0:T(8,128)(2,1)S(1)}, bf16[256,256]{1,0:T(8,128)(2,1)S(1)}, f32[256,2048]{1,0:T(8,128)S(1)}) custom-call(s32[1]{0:T(128)} %bitcast.8.first_ref, bf16[1,1,128,2048]{3,2,1,0:T(8,128)(2,1)S(1)} %collective-permute-done.refs_0_, ...), custom_call_target="tpu_custom_call" | custom-call | flops 2147483648 | bytes 7340032 | tf_op jit(solution)/shard_map/weight_products/pallas_call | solution.py:163
  82.0 1.3 %copy-done.1 = f32[256,2048]{1,0:T(8,128)} copy-done((f32[256,2048]{1,0:T(8,128)}, f32[256,2048]{1,0:T(8,128)S(1)}, u32[]{:S(2)}) %copy-start.1) | copy-done | bytes 2097176
  83.4 1.0 ranks_and_pieces.1
  84.4 5.7 %all-to-all-start.3 = ((bf16[16,2,32,256]{3,2,1,0:T(8,128)(2,1)}), bf16[16,2,32,256]{3,2,1,0:T(8,128)(2,1)S(1)}, u32[]{:S(2)}, u32[]{:S(2)}) async-start(bf16[16,2,32,256]{3,2,1,0:T(8,128)(2,1)} %get-tuple-element.49), calls=%async_computation.3 | async-start | bytes 1048576 | tf_op jit(solution)/shard_map/all_to_all | solution.py:27
  90.6 2.4 %collective-permute-start.6 = (bf16[256,256]{1,0:T(8,128)(2,1)S(1)}, bf16[256,256]{1,0:T(8,128)(2,1)S(1)}, u32[]{:S(2)}, u32[]{:S(2)}) collective-permute-start(bf16[256,256]{1,0:T(8,128)(2,1)S(1)} %get-tuple-element.54), channel_id=1, source_target_pairs={{0,1},{1,2},{2,3},{3,0},{4,5},{5,6},{6,7},{7,4},{8,9},{9,10},{10,1... | collective-permute-start | bytes 393224 | tf_op jit(solution)/shard_map/ppermute | solution.py:451
  93.0 4.3 %collective-permute-start.7 = (bf16[256,256]{1,0:T(8,128)(2,1)S(1)}, bf16[256,256]{1,0:T(8,128)(2,1)S(1)}, u32[]{:S(2)}, u32[]{:S(2)}) collective-permute-start(bf16[256,256]{1,0:T(8,128)(2,1)S(1)} %get-tuple-element.55), channel_id=1, source_target_pairs={{0,2},{1,3},{2,0},{3,1},{4,6},{5,7},{6,4},{7,5},{8,10},{9,11},{10,... | collective-permute-start | bytes 393224 | tf_op jit(solution)/shard_map/ppermute | solution.py:451
  97.3 3.1 %collective-permute-start.8 = (bf16[256,256]{1,0:T(8,128)(2,1)S(1)}, bf16[256,256]{1,0:T(8,128)(2,1)S(1)}, u32[]{:S(2)}, u32[]{:S(2)}) collective-permute-start(bf16[256,256]{1,0:T(8,128)(2,1)S(1)} %get-tuple-element.56), channel_id=1, source_target_pairs={{0,3},{1,0},{2,1},{3,2},{4,7},{5,4},{6,5},{7,6},{8,11},{9,8},{10,9... | collective-permute-start | bytes 393224 | tf_op jit(solution)/shard_map/ppermute | solution.py:451
  101.0 2.9 %input_gradients.1 = bf16[2,128,2048]{2,1,0:T(8,128)(2,1)} custom-call(s32[2]{0:T(128)} %fusion.live_ref, bf16[2,64,128]{2,1,0:T(8,128)(2,1)} %get-tuple-element.65.ranks_ref, bf16[16,144,128]{2,1,0:T(8,128)(2,1)} %copy-done, f32[256,2048]{1,0:T(8,128)} %copy-done.1), custom_call_target="tpu_custom_call" | custom-call | flops 67108864 | bytes 3145728 | tf_op jit(solution)/shard_map/input_gradients/pallas_call | solution.py:277
  104.5 1.5 %layer_outputs.1 = bf16[2,128,256]{2,1,0:T(8,128)(2,1)} custom-call(s32[2]{0:T(128)S(1)} %copy-done.2, bf16[2,64,128]{2,1,0:T(8,128)(2,1)S(1)} %get-tuple-element.64.ranks_ref, f32[2,64,256]{2,1,0:T(8,128)S(1)} %get-tuple-element.52.up_ref, bf16[256,256]{1,0:T(8,128)(2,1)S(1)} %get-tuple-element.53.refs_0_, ...), custom_call_target="tpu_custom_call" | custom-call | tf_op jit(solution)/shard_map/layer_outputs/pallas_call | solution.py:307
  106.0 1.4 %all-to-all-done.3.pieces_ref = bf16[16,2,32,256]{3,2,1,0:T(8,128)(2,1)S(1)} async-done(((bf16[16,2,32,256]{3,2,1,0:T(8,128)(2,1)}), bf16[16,2,32,256]{3,2,1,0:T(8,128)(2,1)S(1)}, u32[]{:S(2)}, u32[]{:S(2)}) %all-to-all-start.3) | async-done | bytes 524320 | tf_op jit(solution)/shard_map/all_to_all | solution.py:27
  107.4 0.8 slot_sums.3
  108.2 1.9 %collective-permute-start.9 = (f32[2,2,32,256]{3,2,1,0:T(8,128)S(1)}, f32[2,2,32,256]{3,2,1,0:T(8,128)S(1)}, u32[]{:S(2)}, u32[]{:S(2)}) collective-permute-start(f32[2,2,32,256]{3,2,1,0:T(8,128)S(1)} %slot_sums.3), channel_id=1, source_target_pairs={{0,4},{4,0},{8,12},{12,8},{16,20},{20,16},{24,28},{28,24},{32,36},... | collective-permute-start | bytes 393224 | tf_op jit(solution)/shard_map/ppermute | solution.py:460
  110.2 0.8 slot_sums.2.own_ref
  111.5 0.7 placed_sums.1
  (26 shorter events, 3.5 us)
Async XLA Ops:
  7.2 18.5 %copy-start.5 = (bf16[1,2,128,256]{3,2,1,0:T(8,128)(2,1)S(1)}, bf16[1,2,128,256]{3,2,1,0:T(8,128)(2,1)}, u32[]{:S(2)}) copy-start(bf16[1,2,128,256]{3,2,1,0:T(8,128)(2,1)} %param.8) | copy-start | bytes 393220
  7.2 70.2 %all-gather.3.cloned.1.call-start = ((), (), s32[]{:S(2)}) async-start(), calls=%async_computation.4 | async-start | bytes 4456448 | tf_op jit(solution)/shard_map/all_gather | solution.py:431
  9.3 33.5 %all-to-all-start = ((bf16[16,152,128]{2,1,0:T(8,128)(2,1)}), bf16[16,152,128]{2,1,0:T(8,128)(2,1)S(1)}, u32[]{:S(2)}, u32[]{:S(2)}) async-start(bf16[16,152,128]{2,1,0:T(8,128)(2,1)} %packed_adapters.1), calls=%async_computation | async-start | bytes 1245184 | tf_op jit(solution)/shard_map/all_to_all | solution.py:27
  22.4 22.3 %collective-permute-start = (bf16[1,1,128,2048]{3,2,1,0:T(8,128)(2,1)S(1)}, bf16[1,1,128,2048]{3,2,1,0:T(8,128)(2,1)S(1)}, u32[]{:S(2)}, u32[]{:S(2)}) collective-permute-start(bf16[1,1,128,2048]{3,2,1,0:T(8,128)(2,1)S(1)} %get-tuple-element.63), channel_id=1, source_target_pairs={{0,64},{64,128},{128,192},{192,256},{256,320},{320,384},{384,448},... | collective-permute-start | bytes 1572872 | tf_op jit(solution)/shard_map/ppermute | solution.py:23
  25.7 6.6 %collective-permute-start.1 = (bf16[1,2,128,256]{3,2,1,0:T(8,128)(2,1)S(1)}, bf16[1,2,128,256]{3,2,1,0:T(8,128)(2,1)S(1)}, u32[]{:S(2)}, u32[]{:S(2)}) collective-permute-start(bf16[1,2,128,256]{3,2,1,0:T(8,128)(2,1)S(1)} %copy-done.5), channel_id=1, source_target_pairs={{0,448},{64,0},{128,64},{192,128},{256,192},{320,256},{384,320},{4... | collective-permute-start | bytes 393224 | tf_op jit(solution)/shard_map/ppermute | solution.py:23
  32.3 12.4 %collective-permute-start.2 = (bf16[256,256]{1,0:T(8,128)(2,1)S(1)}, bf16[256,256]{1,0:T(8,128)(2,1)S(1)}, u32[]{:S(2)}, u32[]{:S(2)}) collective-permute-start(bf16[256,256]{1,0:T(8,128)(2,1)S(1)} %bitcast.25), channel_id=1, source_target_pairs={{0,1},{1,2},{2,3},{3,0},{4,5},{5,6},{6,7},{7,4},{8,9},{9,10},{10,1... | collective-permute-start | bytes 393224 | tf_op jit(solution)/shard_map/ppermute | solution.py:424
  44.7 27.5 %all-to-all-start.1 = ((bf16[16,144,128]{2,1,0:T(8,128)(2,1)}), bf16[16,144,128]{2,1,0:T(8,128)(2,1)S(1)}, u32[]{:S(2)}, u32[]{:S(2)}) async-start(bf16[16,144,128]{2,1,0:T(8,128)(2,1)} %selected_pieces.1), calls=%async_computation.1 | async-start | bytes 1179648 | tf_op jit(solution)/shard_map/all_to_all | solution.py:27
  48.5 23.7 %collective-permute-start.5 = (bf16[1,1,128,2048]{3,2,1,0:T(8,128)(2,1)S(1)}, bf16[1,1,128,2048]{3,2,1,0:T(8,128)(2,1)S(1)}, u32[]{:S(2)}, u32[]{:S(2)}) collective-permute-start(bf16[1,1,128,2048]{3,2,1,0:T(8,128)(2,1)S(1)} %get-tuple-element.62), channel_id=1, source_target_pairs={{0,64},{64,128},{128,192},{192,256},{256,320},{320,384},{384,448},... | collective-permute-start | bytes 1572872 | tf_op jit(solution)/shard_map/ppermute | solution.py:23
  51.7 8.1 %collective-permute-start.3 = (bf16[256,256]{1,0:T(8,128)(2,1)S(1)}, bf16[256,256]{1,0:T(8,128)(2,1)S(1)}, u32[]{:S(2)}, u32[]{:S(2)}) collective-permute-start(bf16[256,256]{1,0:T(8,128)(2,1)S(1)} %bitcast.26), channel_id=1, source_target_pairs={{0,2},{1,3},{2,0},{3,1},{4,6},{5,7},{6,4},{7,5},{8,10},{9,11},{10,... | collective-permute-start | bytes 393224 | tf_op jit(solution)/shard_map/ppermute | solution.py:424
  56.4 6.4 %collective-permute-start.4 = (bf16[256,256]{1,0:T(8,128)(2,1)S(1)}, bf16[256,256]{1,0:T(8,128)(2,1)S(1)}, u32[]{:S(2)}, u32[]{:S(2)}) collective-permute-start(bf16[256,256]{1,0:T(8,128)(2,1)S(1)} %bitcast.27), channel_id=1, source_target_pairs={{0,3},{1,0},{2,1},{3,2},{4,7},{5,4},{6,5},{7,6},{8,11},{9,8},{10,9... | collective-permute-start | bytes 393224 | tf_op jit(solution)/shard_map/ppermute | solution.py:424
  72.2 9.9 %copy-start = (bf16[16,144,128]{2,1,0:T(8,128)(2,1)}, bf16[16,144,128]{2,1,0:T(8,128)(2,1)S(1)}, u32[]{:S(2)}) copy-start(bf16[16,144,128]{2,1,0:T(8,128)(2,1)S(1)} %all-to-all-done.1.second_ref.down_ref) | copy-start | bytes 1769476
  73.4 10.0 %all-to-all-start.2 = ((bf16[4,2,2,64,128]{4,3,2,1,0:T(8,128)(2,1)}), bf16[4,2,2,64,128]{4,3,2,1,0:T(8,128)(2,1)S(1)}, u32[]{:S(2)}, u32[]{:S(2)}) async-start(bf16[4,2,2,64,128]{4,3,2,1,0:T(8,128)(2,1)} %get-tuple-element.38), calls=%async_computation.2 | async-start | bytes 524288 | tf_op jit(solution)/shard_map/all_to_all | solution.py:27
  77.4 2.2 %copy-start.3 = (bf16[1024,2048]{1,0:T(8,128)(2,1)S(1)}, bf16[1024,2048]{1,0:T(8,128)(2,1)}, u32[]{:S(2)}) copy-start(bf16[1024,2048]{1,0:T(8,128)(2,1)} %all-gather.3.cloned.1.call-done) | copy-start | bytes 12582916
  79.6 10.4 %copy-start.4 = (s32[1,2,1]{1,2,0:T(1,128)S(1)}, s32[1,2,1]{1,2,0:T(1,128)}, u32[]{:S(2)}) copy-start(s32[1,2,1]{1,2,0:T(1,128)} %param.13) | copy-start | bytes 28
  82.0 1.4 %copy-start.1 = (f32[256,2048]{1,0:T(8,128)}, f32[256,2048]{1,0:T(8,128)S(1)}, u32[]{:S(2)}) copy-start(f32[256,2048]{1,0:T(8,128)S(1)} %get-tuple-element.51.product_ref) | copy-start | bytes 6291460
  84.4 23.0 %all-to-all-start.3 = ((bf16[16,2,32,256]{3,2,1,0:T(8,128)(2,1)}), bf16[16,2,32,256]{3,2,1,0:T(8,128)(2,1)S(1)}, u32[]{:S(2)}, u32[]{:S(2)}) async-start(bf16[16,2,32,256]{3,2,1,0:T(8,128)(2,1)} %get-tuple-element.49), calls=%async_computation.3 | async-start | bytes 1048576 | tf_op jit(solution)/shard_map/all_to_all | solution.py:27
  90.6 13.3 %collective-permute-start.6 = (bf16[256,256]{1,0:T(8,128)(2,1)S(1)}, bf16[256,256]{1,0:T(8,128)(2,1)S(1)}, u32[]{:S(2)}, u32[]{:S(2)}) collective-permute-start(bf16[256,256]{1,0:T(8,128)(2,1)S(1)} %get-tuple-element.54), channel_id=1, source_target_pairs={{0,1},{1,2},{2,3},{3,0},{4,5},{5,6},{6,7},{7,4},{8,9},{9,10},{10,1... | collective-permute-start | bytes 393224 | tf_op jit(solution)/shard_map/ppermute | solution.py:451
  93.0 10.9 %collective-permute-start.7 = (bf16[256,256]{1,0:T(8,128)(2,1)S(1)}, bf16[256,256]{1,0:T(8,128)(2,1)S(1)}, u32[]{:S(2)}, u32[]{:S(2)}) collective-permute-start(bf16[256,256]{1,0:T(8,128)(2,1)S(1)} %get-tuple-element.55), channel_id=1, source_target_pairs={{0,2},{1,3},{2,0},{3,1},{4,6},{5,7},{6,4},{7,5},{8,10},{9,11},{10,... | collective-permute-start | bytes 393224 | tf_op jit(solution)/shard_map/ppermute | solution.py:451
  97.3 6.6 %collective-permute-start.8 = (bf16[256,256]{1,0:T(8,128)(2,1)S(1)}, bf16[256,256]{1,0:T(8,128)(2,1)S(1)}, u32[]{:S(2)}, u32[]{:S(2)}) collective-permute-start(bf16[256,256]{1,0:T(8,128)(2,1)S(1)} %get-tuple-element.56), channel_id=1, source_target_pairs={{0,3},{1,0},{2,1},{3,2},{4,7},{5,4},{6,5},{7,6},{8,11},{9,8},{10,9... | collective-permute-start | bytes 393224 | tf_op jit(solution)/shard_map/ppermute | solution.py:451
  103.9 0.7 copy-start.2
  108.2 3.2 %collective-permute-start.9 = (f32[2,2,32,256]{3,2,1,0:T(8,128)S(1)}, f32[2,2,32,256]{3,2,1,0:T(8,128)S(1)}, u32[]{:S(2)}, u32[]{:S(2)}) collective-permute-start(f32[2,2,32,256]{3,2,1,0:T(8,128)S(1)} %slot_sums.3), channel_id=1, source_target_pairs={{0,4},{4,0},{8,12},{12,8},{16,20},{20,16},{24,28},{28,24},{32,36},... | collective-permute-start | bytes 393224 | tf_op jit(solution)/shard_map/ppermute | solution.py:460
Sparse Core Ops, SparseCore 0:
  10.1 66.1 all-gather.2

commit v6 on v4

--- a/solution.py
+++ b/solution.py
@@ -15,6 +15,7 @@
 bf16, f32 = jnp.bfloat16, jnp.float32
 VMEM_LIMIT = 24 * 1024 * 1024
 WIDE_LIMIT = 60 * 1024 * 1024
+PARTS = 4
 
 
 def passed_along(array, axis, by):
@@ -40,6 +41,12 @@
 
 def tn_dot(a, b):
     return lax.dot_general(a, b, (((0,), (0,)), ((), ())), preferred_element_type=f32)
+
+
+def started(source, target, sem):
+    copy = pltpu.make_async_copy(source, target, sem)
+    copy.start()
+    return copy
 
 
 def pack_kernel(halves, langs_ref, table_ref, down_ref, up_ref, out_ref):
@@ -170,32 +177,41 @@
     )(second, returned, *acts)
 
 
-def select_kernel(micro, own_slots, rank, slots_ref, first_ref, out_ref):
+def select_kernel(micro, own_slots, rank, slots_ref, first_ref, out, out_ref, sems):
     holders = out_ref.shape[0]
     group = out_ref.shape[1] // micro - rank
     low = own_slots * rank
-    for d in range(holders):
-        ups = []
-        for m in range(micro):
-            slot = jnp.minimum(slots_ref[d * micro + m], holders * own_slots - 1)
-            owner, k = slot // own_slots, slot % own_slots
-            rows = pl.ds(pl.multiple_of(k * rank, rank), rank)
-            out_ref[d, m * rank : (m + 1) * rank, :] = first_ref[owner, rows, :]
-            held = first_ref[owner, low : low + own_slots * group, :].astype(f32)
-            up = held[:group]
-            for j in range(1, own_slots):
-                up = jnp.where(k == j, held[j * group : (j + 1) * group], up)
-            ups.append(up)
-        out_ref[d, micro * rank :, :] = jnp.concatenate(ups, axis=0).astype(bf16)
+    chunk = holders // PARTS
+    sent = []
+    for i in range(PARTS):
+        for d in range(i * chunk, (i + 1) * chunk):
+            ups = []
+            for m in range(micro):
+                slot = jnp.minimum(slots_ref[d * micro + m], holders * own_slots - 1)
+                owner, k = lax.div(slot, own_slots), lax.rem(slot, own_slots)
+                rows = pl.ds(pl.multiple_of(k * rank, rank), rank)
+                out_ref[d, m * rank : (m + 1) * rank, :] = first_ref[owner, rows, :]
+                held = first_ref[owner, low : low + own_slots * group, :].astype(f32)
+                up = held[:group]
+                for j in range(1, own_slots):
+                    up = jnp.where(k == j, held[j * group : (j + 1) * group], up)
+                ups.append(up)
+            out_ref[d, micro * rank :, :] = jnp.concatenate(ups, axis=0).astype(bf16)
+        some = pl.ds(i * chunk, chunk)
+        sent.append(started(out_ref.at[some], out.at[some], sems.at[i]))
+    for copy in sent:
+        copy.wait()
 
 
 def selected(slots, first, micro, own_slots, rank, group):
     holders, _, lanes = first.shape
+    out = (holders, micro * (rank + group), lanes)
     return pl.pallas_call(
         functools.partial(select_kernel, micro, own_slots, rank),
-        out_shape=jax.ShapeDtypeStruct((holders, micro * (rank + group), lanes), bf16),
+        out_shape=jax.ShapeDtypeStruct(out, bf16),
         in_specs=[smem(), pl.BlockSpec(memory_space=pltpu.VMEM)],
-        out_specs=pl.BlockSpec(memory_space=pltpu.VMEM),
+        out_specs=pl.BlockSpec(memory_space=pl.ANY),
+        scratch_shapes=[pltpu.VMEM(out, bf16), pltpu.SemaphoreType.DMA((PARTS,))],
         compiler_params=params(),
         name="selected_pieces",
     )(slots, first)
@@ -292,19 +308,20 @@
 
 def slot_kernel(marks_ref, first_ref, pieces_ref, out_ref):
     holders, micro = pieces_ref.shape[:2]
-    for i in range(out_ref.shape[0]):
-        total, square = None, None
-        for d in range(holders):
-            partial = None
-            for m in range(micro):
-                hit = marks_ref[d * micro + m] == first_ref[0] + i
-                term = jnp.where(hit, pieces_ref[d, m].astype(f32), 0.0)
-                partial = term if partial is None else partial + term
-            total = partial if total is None else total + partial
-            squared = partial * partial
-            square = squared if square is None else square + squared
-        out_ref[i, 0] = total
-        out_ref[i, 1] = square
+    out_ref[...] = jnp.zeros_like(out_ref)
+    for d in range(holders):
+        marks = [marks_ref[d * micro + m] for m in range(micro)]
+        for i in range(out_ref.shape[0]):
+            hits = [mark == first_ref[0] + i for mark in marks]
+
+            @pl.when(functools.reduce(jnp.logical_or, hits))
+            def _():
+                partial = None
+                for m in range(micro):
+                    term = jnp.where(hits[m], pieces_ref[d, m].astype(f32), 0.0)
+                    partial = term if partial is None else partial + term
+                out_ref[i, 0] += partial
+                out_ref[i, 1] += partial * partial
 
 
 def slot_sums(marks, first_slot, pieces, own_slots):
@@ -363,7 +380,6 @@
     live = (langs < slot_table.shape[0]).astype(jnp.int32)
 
     weight = jnp.swapaxes(base_weight[0], 0, 1)
-    gathered = lax.all_gather(weight, "dp", axis=0)
     flat_cots = returned.reshape(rows, columns)
     cots = [flat_cots] + [
         lax.ppermute(flat_cots, "mp", [(i, (i + k) % quarters) for i in range(quarters)])
@@ -372,6 +388,8 @@
 
     down = jnp.swapaxes(adapter_down[0], 1, 2)
     first = packed(langs[None, :], slot_language, down, adapter_up[0], holders)
+    first, weight = lax.optimization_barrier((first, weight))
+    gathered = lax.all_gather(weight, "dp", axis=0)
     first = exchanged(first, "dp")
 
     marked = own_slots * (rank + up_rows)

time: 121 us -> 120 us (level)
  waiting for transfers between devices: 26.4 us -> 25.1 us
  transfers between devices with their start and end apart: 15 -> 15, of which waited for: 8 -> 7; matrix products, arithmetic and copies ran while one was open for 2% -> 2% of each run, Pallas kernels for 11% -> 9%
where the time goes in v6:
time: 120 us; the launch traced here: 119 us
  starting transfers between devices  57.8 us (48%)
  waiting for transfers between devices  25.1 us (21%)
  Pallas kernels  15 us (12%)
  between operations  14.2 us (12%)
  local copies, waits for them, and re-layouts  6.18 us (5%)
    all_to_all x4, starting transfers between devices, exchanged(): return lax.all_to_all(array, axis, split_axis=0, concat_axis=0, tiled=True)  25.3 us
    all_to_all x4, waiting for transfers between devices, exchanged(): return lax.all_to_all(array, axis, split_axis=0, concat_axis=0, tiled=True)  18.1 us
    ppermute x3, starting transfers between devices, shards(): lax.ppermute(flat_cots, 'mp', [(i, (i + k) % quarters) for i in range(qua...  10.5 us
    ppermute x3, starting transfers between devices, passed_along(): lax.ppermute(array, axis, [(i, (i + by) % devices) for i in range(devices)])  10.2 us
    ppermute x3, starting transfers between devices, shards(): lax.ppermute(base_parts[k], 'mp', [(i, (i + k) % quarters) for i in range...  9.78 us
    unnamed x12, local copies, waits for them, and re-layouts  4.2 us
    ppermute x3, waiting for transfers between devices, shards(): lax.ppermute(flat_cots, 'mp', [(i, (i + k) % quarters) for i in range(qua...  3.62 us
    pallas_call x1, Pallas kernels, input_gradients(): pl.pallas_call(functools.partial(gradient_kernel, micro), grid=(steps,),...  2.88 us
  transfers between devices with their start and end apart: 15, of which 7 were waited for; matrix products, arithmetic and copies ran while one was open for 2% of the time, Pallas kernels for 9%

profile of v6, /device:TPU:1, one launch (start us, length us, event | category | flops | bytes accessed | tf_op | source)
XLA Modules:
  0.0 119.2 jit_solution(886177095349590953)
XLA Ops:
  7.2 2.2 %packed_adapters.1 = bf16[16,152,128]{2,1,0:T(8,128)(2,1)} custom-call(s32[1,2]{1,0:T(1,128)} %bitcast.37, s32[1,32]{1,0:T(1,128)} %table_ref.1, bf16[2,64,2048]{2,1,0:T(8,128)(2,1)} %bitcast.33, bf16[2,64,256]{2,1,0:T(8,128)(2,1)} %bitcast.36), custom_call_target="tpu_custom_call" | custom-call | tf_op jit(solution)/shard_map/packed_adapters/pallas_call | solution.py:83
  9.4 11.9 %all-to-all-start = ((bf16[16,152,128]{2,1,0:T(8,128)(2,1)}), bf16[16,152,128]{2,1,0:T(8,128)(2,1)S(1)}, u32[]{:S(2)}, u32[]{:S(2)}) async-start(bf16[16,152,128]{2,1,0:T(8,128)(2,1)} %packed_adapters.1), calls=%async_computation | async-start | bytes 1245184 | tf_op jit(solution)/shard_map/all_to_all | solution.py:27
  21.3 1.3 %fusion.1 = (bf16[1,1,128,2048]{3,2,1,0:T(8,128)(2,1)S(1)}, bf16[1,1,128,2048]{3,2,1,0:T(8,128)(2,1)S(1)}) fusion(bf16[1,2,128,2048]{3,2,1,0:T(8,128)(2,1)} %param.7), kind=kLoop, calls=%fused_computation.5 | loop fusion | bytes 2097152 | tf_op jit(solution)/shard_map/slice | solution.py:376
  22.6 3.2 %collective-permute-start = (bf16[1,1,128,2048]{3,2,1,0:T(8,128)(2,1)S(1)}, bf16[1,1,128,2048]{3,2,1,0:T(8,128)(2,1)S(1)}, u32[]{:S(2)}, u32[]{:S(2)}) collective-permute-start(bf16[1,1,128,2048]{3,2,1,0:T(8,128)(2,1)S(1)} %get-tuple-element.63), channel_id=1, source_target_pairs={{0,64},{64,128},{128,192},{192,256},{256,320},{320,384},{384,448},... | collective-permute-start | bytes 1572872 | tf_op jit(solution)/shard_map/ppermute | solution.py:23
  25.8 3.8 %collective-permute-start.1 = (bf16[1,2,128,256]{3,2,1,0:T(8,128)(2,1)S(1)}, bf16[1,2,128,256]{3,2,1,0:T(8,128)(2,1)S(1)}, u32[]{:S(2)}, u32[]{:S(2)}) collective-permute-start(bf16[1,2,128,256]{3,2,1,0:T(8,128)(2,1)S(1)} %copy-done.5), channel_id=1, source_target_pairs={{0,448},{64,0},{128,64},{192,128},{256,192},{320,256},{384,320},{4... | collective-permute-start | bytes 393224 | tf_op jit(solution)/shard_map/ppermute | solution.py:23
  29.6 2.8 %collective-permute-done.1 = bf16[1,2,128,256]{3,2,1,0:T(8,128)(2,1)S(1)} collective-permute-done((bf16[1,2,128,256]{3,2,1,0:T(8,128)(2,1)S(1)}, bf16[1,2,128,256]{3,2,1,0:T(8,128)(2,1)S(1)}, u32[]{:S(2)}, u32[]{:S(2)}) %collective-permute-start.1) | collective-permute-done | bytes 131104 | tf_op jit(solution)/shard_map/ppermute | solution.py:23
  32.4 3.1 %collective-permute-start.2 = (bf16[256,256]{1,0:T(8,128)(2,1)S(1)}, bf16[256,256]{1,0:T(8,128)(2,1)S(1)}, u32[]{:S(2)}, u32[]{:S(2)}) collective-permute-start(bf16[256,256]{1,0:T(8,128)(2,1)S(1)} %bitcast.25), channel_id=1, source_target_pairs={{0,1},{1,2},{2,3},{3,0},{4,5},{5,6},{6,7},{7,4},{8,9},{9,10},{10,1... | collective-permute-start | bytes 393224 | tf_op jit(solution)/shard_map/ppermute | solution.py:385
  35.5 7.4 %all-to-all-done.first_ref = bf16[16,152,128]{2,1,0:T(8,128)(2,1)S(1)} async-done(((bf16[16,152,128]{2,1,0:T(8,128)(2,1)}), bf16[16,152,128]{2,1,0:T(8,128)(2,1)S(1)}, u32[]{:S(2)}, u32[]{:S(2)}) %all-to-all-start) | async-done | bytes 622624 | tf_op jit(solution)/shard_map/all_to_all | solution.py:27
  43.4 1.5 %selected_pieces.1 = bf16[16,144,128]{2,1,0:T(8,128)(2,1)} custom-call(s32[32]{0:T(128)S(1)} %reshape.32.slots_ref.marks_ref, bf16[16,152,128]{2,1,0:T(8,128)(2,1)S(1)} %all-to-all-done.first_ref), custom_call_target="tpu_custom_call" | custom-call | tf_op jit(solution)/shard_map/selected_pieces/pallas_call | solution.py:209
  44.8 3.8 %all-to-all-start.1 = ((bf16[16,144,128]{2,1,0:T(8,128)(2,1)}), bf16[16,144,128]{2,1,0:T(8,128)(2,1)S(1)}, u32[]{:S(2)}, u32[]{:S(2)}) async-start(bf16[16,144,128]{2,1,0:T(8,128)(2,1)} %selected_pieces.1), calls=%async_computation.1 | async-start | bytes 1179648 | tf_op jit(solution)/shard_map/all_to_all | solution.py:27
  48.6 3.2 %collective-permute-start.5 = (bf16[1,1,128,2048]{3,2,1,0:T(8,128)(2,1)S(1)}, bf16[1,1,128,2048]{3,2,1,0:T(8,128)(2,1)S(1)}, u32[]{:S(2)}, u32[]{:S(2)}) collective-permute-start(bf16[1,1,128,2048]{3,2,1,0:T(8,128)(2,1)S(1)} %get-tuple-element.62), channel_id=1, source_target_pairs={{0,64},{64,128},{128,192},{192,256},{256,320},{320,384},{384,448},... | collective-permute-start | bytes 1572872 | tf_op jit(solution)/shard_map/ppermute | solution.py:23
  51.8 4.7 %collective-permute-start.3 = (bf16[256,256]{1,0:T(8,128)(2,1)S(1)}, bf16[256,256]{1,0:T(8,128)(2,1)S(1)}, u32[]{:S(2)}, u32[]{:S(2)}) collective-permute-start(bf16[256,256]{1,0:T(8,128)(2,1)S(1)} %bitcast.26), channel_id=1, source_target_pairs={{0,2},{1,3},{2,0},{3,1},{4,6},{5,7},{6,4},{7,5},{8,10},{9,11},{10,... | collective-permute-start | bytes 393224 | tf_op jit(solution)/shard_map/ppermute | solution.py:385
  56.5 2.8 %collective-permute-start.4 = (bf16[256,256]{1,0:T(8,128)(2,1)S(1)}, bf16[256,256]{1,0:T(8,128)(2,1)S(1)}, u32[]{:S(2)}, u32[]{:S(2)}) collective-permute-start(bf16[256,256]{1,0:T(8,128)(2,1)S(1)} %bitcast.27), channel_id=1, source_target_pairs={{0,3},{1,0},{2,1},{3,2},{4,7},{5,4},{6,5},{7,6},{8,11},{9,8},{10,9... | collective-permute-start | bytes 393224 | tf_op jit(solution)/shard_map/ppermute | solution.py:385
  60.0 2.9 %collective-permute-done.4.refs_5_ = bf16[256,256]{1,0:T(8,128)(2,1)S(1)} collective-permute-done((bf16[256,256]{1,0:T(8,128)(2,1)S(1)}, bf16[256,256]{1,0:T(8,128)(2,1)S(1)}, u32[]{:S(2)}, u32[]{:S(2)}) %collective-permute-start.4) | collective-permute-done | bytes 131104 | tf_op jit(solution)/shard_map/ppermute | solution.py:385
  62.9 9.4 %all-to-all-done.1.second_ref.down_ref = bf16[16,144,128]{2,1,0:T(8,128)(2,1)S(1)} async-done(((bf16[16,144,128]{2,1,0:T(8,128)(2,1)}), bf16[16,144,128]{2,1,0:T(8,128)(2,1)S(1)}, u32[]{:S(2)}, u32[]{:S(2)}) %all-to-all-start.1) | async-done | bytes 589856 | tf_op jit(solution)/shard_map/all_to_all | solution.py:27
  72.3 1.2 %rank_parts.1 = (bf16[4,2,2,64,128]{4,3,2,1,0:T(8,128)(2,1)}, f32[2,64,256]{2,1,0:T(8,128)S(1)}) custom-call(bf16[16,144,128]{2,1,0:T(8,128)(2,1)S(1)} %all-to-all-done.1.second_ref.down_ref, bf16[2,128,256]{2,1,0:T(8,128)(2,1)S(1)} %bitcast.28, bf16[1,1,128,2048]{3,2,1,0:T(8,128)(2,1)S(1)} %collective-permute-done.refs_0_, ...), custom_call_target="tpu_custom_call" | custom-call | tf_op jit(solution)/shard_map/rank_parts/pallas_call | solution.py:167
  73.5 4.0 %all-to-all-start.2 = ((bf16[4,2,2,64,128]{4,3,2,1,0:T(8,128)(2,1)}), bf16[4,2,2,64,128]{4,3,2,1,0:T(8,128)(2,1)S(1)}, u32[]{:S(2)}, u32[]{:S(2)}) async-start(bf16[4,2,2,64,128]{4,3,2,1,0:T(8,128)(2,1)} %get-tuple-element.38), calls=%async_computation.2 | async-start | bytes 524288 | tf_op jit(solution)/shard_map/all_to_all | solution.py:27
  77.5 2.2 %copy-done.3 = bf16[1024,2048]{1,0:T(8,128)(2,1)S(1)} copy-done((bf16[1024,2048]{1,0:T(8,128)(2,1)S(1)}, bf16[1024,2048]{1,0:T(8,128)(2,1)}, u32[]{:S(2)}) %copy-start.3) | copy-done | bytes 4194328
  79.7 2.4 %weight_products.1 = (bf16[256,256]{1,0:T(8,128)(2,1)S(1)}, bf16[256,256]{1,0:T(8,128)(2,1)S(1)}, bf16[256,256]{1,0:T(8,128)(2,1)S(1)}, bf16[256,256]{1,0:T(8,128)(2,1)S(1)}, f32[256,2048]{1,0:T(8,128)S(1)}) custom-call(s32[1]{0:T(128)} %bitcast.8.first_ref, bf16[1,1,128,2048]{3,2,1,0:T(8,128)(2,1)S(1)} %collective-permute-done.refs_0_, ...), custom_call_target="tpu_custom_call" | custom-call | flops 2147483648 | bytes 7340032 | tf_op jit(solution)/shard_map/weight_products/pallas_call | solution.py:124
  82.1 1.3 %copy-done.1 = f32[256,2048]{1,0:T(8,128)} copy-done((f32[256,2048]{1,0:T(8,128)}, f32[256,2048]{1,0:T(8,128)S(1)}, u32[]{:S(2)}) %copy-start.1) | copy-done | bytes 2097176
  83.5 1.0 ranks_and_pieces.1
  84.5 5.7 %all-to-all-start.3 = ((bf16[16,2,32,256]{3,2,1,0:T(8,128)(2,1)}), bf16[16,2,32,256]{3,2,1,0:T(8,128)(2,1)S(1)}, u32[]{:S(2)}, u32[]{:S(2)}) async-start(bf16[16,2,32,256]{3,2,1,0:T(8,128)(2,1)} %get-tuple-element.49), calls=%async_computation.3 | async-start | bytes 1048576 | tf_op jit(solution)/shard_map/all_to_all | solution.py:27
  90.7 2.4 %collective-permute-start.6 = (bf16[256,256]{1,0:T(8,128)(2,1)S(1)}, bf16[256,256]{1,0:T(8,128)(2,1)S(1)}, u32[]{:S(2)}, u32[]{:S(2)}) collective-permute-start(bf16[256,256]{1,0:T(8,128)(2,1)S(1)} %get-tuple-element.54), channel_id=1, source_target_pairs={{0,1},{1,2},{2,3},{3,0},{4,5},{5,6},{6,7},{7,4},{8,9},{9,10},{10,1... | collective-permute-start | bytes 393224 | tf_op jit(solution)/shard_map/ppermute | solution.py:412
  93.1 4.3 %collective-permute-start.7 = (bf16[256,256]{1,0:T(8,128)(2,1)S(1)}, bf16[256,256]{1,0:T(8,128)(2,1)S(1)}, u32[]{:S(2)}, u32[]{:S(2)}) collective-permute-start(bf16[256,256]{1,0:T(8,128)(2,1)S(1)} %get-tuple-element.55), channel_id=1, source_target_pairs={{0,2},{1,3},{2,0},{3,1},{4,6},{5,7},{6,4},{7,5},{8,10},{9,11},{10,... | collective-permute-start | bytes 393224 | tf_op jit(solution)/shard_map/ppermute | solution.py:412
  97.4 3.1 %collective-permute-start.8 = (bf16[256,256]{1,0:T(8,128)(2,1)S(1)}, bf16[256,256]{1,0:T(8,128)(2,1)S(1)}, u32[]{:S(2)}, u32[]{:S(2)}) collective-permute-start(bf16[256,256]{1,0:T(8,128)(2,1)S(1)} %get-tuple-element.56), channel_id=1, source_target_pairs={{0,3},{1,0},{2,1},{3,2},{4,7},{5,4},{6,5},{7,6},{8,11},{9,8},{10,9... | collective-permute-start | bytes 393224 | tf_op jit(solution)/shard_map/ppermute | solution.py:412
  101.1 2.9 %input_gradients.1 = bf16[2,128,2048]{2,1,0:T(8,128)(2,1)} custom-call(s32[2]{0:T(128)} %fusion.live_ref, bf16[2,64,128]{2,1,0:T(8,128)(2,1)} %get-tuple-element.65.ranks_ref, bf16[16,144,128]{2,1,0:T(8,128)(2,1)} %copy-done, f32[256,2048]{1,0:T(8,128)} %copy-done.1), custom_call_target="tpu_custom_call" | custom-call | flops 67108864 | bytes 3145728 | tf_op jit(solution)/shard_map/input_gradients/pallas_call | solution.py:238
  104.6 1.5 %layer_outputs.1 = bf16[2,128,256]{2,1,0:T(8,128)(2,1)} custom-call(s32[2]{0:T(128)S(1)} %copy-done.2, bf16[2,64,128]{2,1,0:T(8,128)(2,1)S(1)} %get-tuple-element.64.ranks_ref, f32[2,64,256]{2,1,0:T(8,128)S(1)} %get-tuple-element.52.up_ref, bf16[256,256]{1,0:T(8,128)(2,1)S(1)} %get-tuple-element.53.refs_0_, ...), custom_call_target="tpu_custom_call" | custom-call | tf_op jit(solution)/shard_map/layer_outputs/pallas_call | solution.py:268
  106.1 1.4 %all-to-all-done.3.pieces_ref = bf16[16,2,32,256]{3,2,1,0:T(8,128)(2,1)S(1)} async-done(((bf16[16,2,32,256]{3,2,1,0:T(8,128)(2,1)}), bf16[16,2,32,256]{3,2,1,0:T(8,128)(2,1)S(1)}, u32[]{:S(2)}, u32[]{:S(2)}) %all-to-all-start.3) | async-done | bytes 524320 | tf_op jit(solution)/shard_map/all_to_all | solution.py:27
  107.5 0.9 slot_sums.3
  108.4 1.9 %collective-permute-start.9 = (f32[2,2,32,256]{3,2,1,0:T(8,128)S(1)}, f32[2,2,32,256]{3,2,1,0:T(8,128)S(1)}, u32[]{:S(2)}, u32[]{:S(2)}) collective-permute-start(f32[2,2,32,256]{3,2,1,0:T(8,128)S(1)} %slot_sums.3), channel_id=1, source_target_pairs={{0,4},{4,0},{8,12},{12,8},{16,20},{20,16},{24,28},{28,24},{32,36},... | collective-permute-start | bytes 393224 | tf_op jit(solution)/shard_map/ppermute | solution.py:421
  110.3 0.8 slot_sums.2.own_ref
  111.6 0.7 placed_sums.1
  (26 shorter events, 3.5 us)
Async XLA Ops:
  7.2 18.6 %copy-start.5 = (bf16[1,2,128,256]{3,2,1,0:T(8,128)(2,1)S(1)}, bf16[1,2,128,256]{3,2,1,0:T(8,128)(2,1)}, u32[]{:S(2)}) copy-start(bf16[1,2,128,256]{3,2,1,0:T(8,128)(2,1)} %param.8) | copy-start | bytes 393220
  7.2 70.3 %all-gather.3.cloned.1.call-start = ((), (), s32[]{:S(2)}) async-start(), calls=%async_computation.4 | async-start | bytes 4456448 | tf_op jit(solution)/shard_map/all_gather | solution.py:392
  9.4 33.5 %all-to-all-start = ((bf16[16,152,128]{2,1,0:T(8,128)(2,1)}), bf16[16,152,128]{2,1,0:T(8,128)(2,1)S(1)}, u32[]{:S(2)}, u32[]{:S(2)}) async-start(bf16[16,152,128]{2,1,0:T(8,128)(2,1)} %packed_adapters.1), calls=%async_computation | async-start | bytes 1245184 | tf_op jit(solution)/shard_map/all_to_all | solution.py:27
  22.6 22.3 %collective-permute-start = (bf16[1,1,128,2048]{3,2,1,0:T(8,128)(2,1)S(1)}, bf16[1,1,128,2048]{3,2,1,0:T(8,128)(2,1)S(1)}, u32[]{:S(2)}, u32[]{:S(2)}) collective-permute-start(bf16[1,1,128,2048]{3,2,1,0:T(8,128)(2,1)S(1)} %get-tuple-element.63), channel_id=1, source_target_pairs={{0,64},{64,128},{128,192},{192,256},{256,320},{320,384},{384,448},... | collective-permute-start | bytes 1572872 | tf_op jit(solution)/shard_map/ppermute | solution.py:23
  25.8 6.6 %collective-permute-start.1 = (bf16[1,2,128,256]{3,2,1,0:T(8,128)(2,1)S(1)}, bf16[1,2,128,256]{3,2,1,0:T(8,128)(2,1)S(1)}, u32[]{:S(2)}, u32[]{:S(2)}) collective-permute-start(bf16[1,2,128,256]{3,2,1,0:T(8,128)(2,1)S(1)} %copy-done.5), channel_id=1, source_target_pairs={{0,448},{64,0},{128,64},{192,128},{256,192},{320,256},{384,320},{4... | collective-permute-start | bytes 393224 | tf_op jit(solution)/shard_map/ppermute | solution.py:23
  32.4 12.4 %collective-permute-start.2 = (bf16[256,256]{1,0:T(8,128)(2,1)S(1)}, bf16[256,256]{1,0:T(8,128)(2,1)S(1)}, u32[]{:S(2)}, u32[]{:S(2)}) collective-permute-start(bf16[256,256]{1,0:T(8,128)(2,1)S(1)} %bitcast.25), channel_id=1, source_target_pairs={{0,1},{1,2},{2,3},{3,0},{4,5},{5,6},{6,7},{7,4},{8,9},{9,10},{10,1... | collective-permute-start | bytes 393224 | tf_op jit(solution)/shard_map/ppermute | solution.py:385
  44.8 27.4 %all-to-all-start.1 = ((bf16[16,144,128]{2,1,0:T(8,128)(2,1)}), bf16[16,144,128]{2,1,0:T(8,128)(2,1)S(1)}, u32[]{:S(2)}, u32[]{:S(2)}) async-start(bf16[16,144,128]{2,1,0:T(8,128)(2,1)} %selected_pieces.1), calls=%async_computation.1 | async-start | bytes 1179648 | tf_op jit(solution)/shard_map/all_to_all | solution.py:27
  48.6 23.6 %collective-permute-start.5 = (bf16[1,1,128,2048]{3,2,1,0:T(8,128)(2,1)S(1)}, bf16[1,1,128,2048]{3,2,1,0:T(8,128)(2,1)S(1)}, u32[]{:S(2)}, u32[]{:S(2)}) collective-permute-start(bf16[1,1,128,2048]{3,2,1,0:T(8,128)(2,1)S(1)} %get-tuple-element.62), channel_id=1, source_target_pairs={{0,64},{64,128},{128,192},{192,256},{256,320},{320,384},{384,448},... | collective-permute-start | bytes 1572872 | tf_op jit(solution)/shard_map/ppermute | solution.py:23
  51.8 8.1 %collective-permute-start.3 = (bf16[256,256]{1,0:T(8,128)(2,1)S(1)}, bf16[256,256]{1,0:T(8,128)(2,1)S(1)}, u32[]{:S(2)}, u32[]{:S(2)}) collective-permute-start(bf16[256,256]{1,0:T(8,128)(2,1)S(1)} %bitcast.26), channel_id=1, source_target_pairs={{0,2},{1,3},{2,0},{3,1},{4,6},{5,7},{6,4},{7,5},{8,10},{9,11},{10,... | collective-permute-start | bytes 393224 | tf_op jit(solution)/shard_map/ppermute | solution.py:385
  56.5 6.4 %collective-permute-start.4 = (bf16[256,256]{1,0:T(8,128)(2,1)S(1)}, bf16[256,256]{1,0:T(8,128)(2,1)S(1)}, u32[]{:S(2)}, u32[]{:S(2)}) collective-permute-start(bf16[256,256]{1,0:T(8,128)(2,1)S(1)} %bitcast.27), channel_id=1, source_target_pairs={{0,3},{1,0},{2,1},{3,2},{4,7},{5,4},{6,5},{7,6},{8,11},{9,8},{10,9... | collective-permute-start | bytes 393224 | tf_op jit(solution)/shard_map/ppermute | solution.py:385
  72.3 9.8 %copy-start = (bf16[16,144,128]{2,1,0:T(8,128)(2,1)}, bf16[16,144,128]{2,1,0:T(8,128)(2,1)S(1)}, u32[]{:S(2)}) copy-start(bf16[16,144,128]{2,1,0:T(8,128)(2,1)S(1)} %all-to-all-done.1.second_ref.down_ref) | copy-start | bytes 1769476
  73.5 10.0 %all-to-all-start.2 = ((bf16[4,2,2,64,128]{4,3,2,1,0:T(8,128)(2,1)}), bf16[4,2,2,64,128]{4,3,2,1,0:T(8,128)(2,1)S(1)}, u32[]{:S(2)}, u32[]{:S(2)}) async-start(bf16[4,2,2,64,128]{4,3,2,1,0:T(8,128)(2,1)} %get-tuple-element.38), calls=%async_computation.2 | async-start | bytes 524288 | tf_op jit(solution)/shard_map/all_to_all | solution.py:27
  77.5 2.2 %copy-start.3 = (bf16[1024,2048]{1,0:T(8,128)(2,1)S(1)}, bf16[1024,2048]{1,0:T(8,128)(2,1)}, u32[]{:S(2)}) copy-start(bf16[1024,2048]{1,0:T(8,128)(2,1)} %all-gather.3.cloned.1.call-done) | copy-start | bytes 12582916
  79.7 10.5 %copy-start.4 = (s32[1,2,1]{1,2,0:T(1,128)S(1)}, s32[1,2,1]{1,2,0:T(1,128)}, u32[]{:S(2)}) copy-start(s32[1,2,1]{1,2,0:T(1,128)} %param.13) | copy-start | bytes 28
  82.1 1.4 %copy-start.1 = (f32[256,2048]{1,0:T(8,128)}, f32[256,2048]{1,0:T(8,128)S(1)}, u32[]{:S(2)}) copy-start(f32[256,2048]{1,0:T(8,128)S(1)} %get-tuple-element.51.product_ref) | copy-start | bytes 6291460
  84.5 23.0 %all-to-all-start.3 = ((bf16[16,2,32,256]{3,2,1,0:T(8,128)(2,1)}), bf16[16,2,32,256]{3,2,1,0:T(8,128)(2,1)S(1)}, u32[]{:S(2)}, u32[]{:S(2)}) async-start(bf16[16,2,32,256]{3,2,1,0:T(8,128)(2,1)} %get-tuple-element.49), calls=%async_computation.3 | async-start | bytes 1048576 | tf_op jit(solution)/shard_map/all_to_all | solution.py:27
  90.7 13.3 %collective-permute-start.6 = (bf16[256,256]{1,0:T(8,128)(2,1)S(1)}, bf16[256,256]{1,0:T(8,128)(2,1)S(1)}, u32[]{:S(2)}, u32[]{:S(2)}) collective-permute-start(bf16[256,256]{1,0:T(8,128)(2,1)S(1)} %get-tuple-element.54), channel_id=1, source_target_pairs={{0,1},{1,2},{2,3},{3,0},{4,5},{5,6},{6,7},{7,4},{8,9},{9,10},{10,1... | collective-permute-start | bytes 393224 | tf_op jit(solution)/shard_map/ppermute | solution.py:412
  93.1 10.9 %collective-permute-start.7 = (bf16[256,256]{1,0:T(8,128)(2,1)S(1)}, bf16[256,256]{1,0:T(8,128)(2,1)S(1)}, u32[]{:S(2)}, u32[]{:S(2)}) collective-permute-start(bf16[256,256]{1,0:T(8,128)(2,1)S(1)} %get-tuple-element.55), channel_id=1, source_target_pairs={{0,2},{1,3},{2,0},{3,1},{4,6},{5,7},{6,4},{7,5},{8,10},{9,11},{10,... | collective-permute-start | bytes 393224 | tf_op jit(solution)/shard_map/ppermute | solution.py:412
  97.4 6.6 %collective-permute-start.8 = (bf16[256,256]{1,0:T(8,128)(2,1)S(1)}, bf16[256,256]{1,0:T(8,128)(2,1)S(1)}, u32[]{:S(2)}, u32[]{:S(2)}) collective-permute-start(bf16[256,256]{1,0:T(8,128)(2,1)S(1)} %get-tuple-element.56), channel_id=1, source_target_pairs={{0,3},{1,0},{2,1},{3,2},{4,7},{5,4},{6,5},{7,6},{8,11},{9,8},{10,9... | collective-permute-start | bytes 393224 | tf_op jit(solution)/shard_map/ppermute | solution.py:412
  104.0 0.7 copy-start.2
  108.4 3.2 %collective-permute-start.9 = (f32[2,2,32,256]{3,2,1,0:T(8,128)S(1)}, f32[2,2,32,256]{3,2,1,0:T(8,128)S(1)}, u32[]{:S(2)}, u32[]{:S(2)}) collective-permute-start(f32[2,2,32,256]{3,2,1,0:T(8,128)S(1)} %slot_sums.3), channel_id=1, source_target_pairs={{0,4},{4,0},{8,12},{12,8},{16,20},{20,16},{24,28},{28,24},{32,36},... | collective-permute-start | bytes 393224 | tf_op jit(solution)/shard_map/ppermute | solution.py:421
Sparse Core Ops, SparseCore 0:
  10.1 66.2 all-gather.2

commit v7 on v6

--- a/solution.py
+++ b/solution.py
@@ -101,19 +101,27 @@
 def weight_kernel(micro, quarters, first_ref, *refs):
     acts, cots = refs[:micro], refs[micro : micro + quarters]
     gathered_ref = refs[micro + quarters]
-    outs, back_ref = refs[micro + quarters + 1 : -1], refs[-1]
+    outs, back_out = refs[micro + quarters + 1 : -3], refs[-3]
+    back_ref, sem = refs[-2], refs[-1]
     holders, _, width = gathered_ref.shape
     group = holders // quarters
-    rows = jnp.concatenate([ref[0, 0] for ref in acts], axis=0)
+
+    def weight(k):
+        quarter = lax.rem(first_ref[0] + k, quarters)
+        return gathered_ref[pl.ds(quarter * group, group)].reshape(-1, width)
+
     for k in range(quarters):
-        quarter = lax.rem(first_ref[0] + k, quarters)
-        weight = gathered_ref[pl.ds(quarter * group, group)].reshape(-1, width)
-        outs[k][...] = nt_dot(rows, weight).astype(bf16)
-        back = jnp.dot(cots[(quarters - k) % quarters][...], weight, preferred_element_type=f32)
+        part = cots[(quarters - k) % quarters][...]
+        back = jnp.dot(part, weight(k), preferred_element_type=f32)
         if k == 0:
             back_ref[...] = back
         else:
             back_ref[...] += back
+    copy = started(back_ref, back_out, sem)
+    rows = jnp.concatenate([ref[0, 0] for ref in acts], axis=0)
+    for k in range(quarters):
+        outs[k][...] = nt_dot(rows, weight(k)).astype(bf16)
+    copy.wait()
 
 
 def weight_products(first, acts, cots, gathered):
@@ -126,7 +134,9 @@
         out_shape=(jax.ShapeDtypeStruct((rows, group * cols), bf16),) * quarters
         + (jax.ShapeDtypeStruct((rows, width), f32),),
         in_specs=[smem()] + [pl.BlockSpec(memory_space=pltpu.VMEM)] * (micro + quarters + 1),
-        out_specs=(pl.BlockSpec(memory_space=pltpu.VMEM),) * (quarters + 1),
+        out_specs=(pl.BlockSpec(memory_space=pltpu.VMEM),) * quarters
+        + (pl.BlockSpec(memory_space=pl.ANY),),
+        scratch_shapes=[pltpu.VMEM((rows, width), f32), pltpu.SemaphoreType.DMA],
         compiler_params=pltpu.CompilerParams(vmem_limit_bytes=VMEM_LIMIT),
         cost_estimate=pl.CostEstimate(
             flops=4 * rows * width * cols * holders,

time: 120 us -> 120 us (level)
  no operation moved by 1% of the time
where the time goes in v7:
time: 120 us; the launch traced here: 119 us
  starting transfers between devices  57.9 us (48%)
  waiting for transfers between devices  24.6 us (20%)
  Pallas kernels  15.3 us (13%)
  between operations  14.2 us (12%)
  local copies, waits for them, and re-layouts  6.18 us (5%)
    all_to_all x4, starting transfers between devices, exchanged(): return lax.all_to_all(array, axis, split_axis=0, concat_axis=0, tiled=True)  25 us
    all_to_all x4, waiting for transfers between devices, exchanged(): return lax.all_to_all(array, axis, split_axis=0, concat_axis=0, tiled=True)  17.8 us
    ppermute x3, starting transfers between devices, shards(): lax.ppermute(flat_cots, 'mp', [(i, (i + k) % quarters) for i in range(qua...  10.5 us
    ppermute x3, starting transfers between devices, passed_along(): lax.ppermute(array, axis, [(i, (i + by) % devices) for i in range(devices)])  10.2 us
    ppermute x3, starting transfers between devices, shards(): lax.ppermute(base_parts[k], 'mp', [(i, (i + k) % quarters) for i in range...  10.1 us
    unnamed x12, local copies, waits for them, and re-layouts  4.2 us
    ppermute x3, waiting for transfers between devices, shards(): lax.ppermute(flat_cots, 'mp', [(i, (i + k) % quarters) for i in range(qua...  3.62 us
    pallas_call x1, Pallas kernels, input_gradients(): pl.pallas_call(functools.partial(gradient_kernel, micro), grid=(steps,),...  2.88 us
  transfers between devices with their start and end apart: 15, of which 7 were waited for; matrix products, arithmetic and copies ran while one was open for 2% of the time, Pallas kernels for 9%

profile of v7, /device:TPU:1, one launch (start us, length us, event | category | flops | bytes accessed | tf_op | source)
XLA Modules:
  0.0 119.1 jit_solution(5673154097818726876)
XLA Ops:
  7.2 2.2 %packed_adapters.1 = bf16[16,152,128]{2,1,0:T(8,128)(2,1)} custom-call(s32[1,2]{1,0:T(1,128)} %bitcast.37, s32[1,32]{1,0:T(1,128)} %table_ref.1, bf16[2,64,2048]{2,1,0:T(8,128)(2,1)} %bitcast.33, bf16[2,64,256]{2,1,0:T(8,128)(2,1)} %bitcast.36), custom_call_target="tpu_custom_call" | custom-call | tf_op jit(solution)/shard_map/packed_adapters/pallas_call | solution.py:83
  9.4 11.9 %all-to-all-start = ((bf16[16,152,128]{2,1,0:T(8,128)(2,1)}), bf16[16,152,128]{2,1,0:T(8,128)(2,1)S(1)}, u32[]{:S(2)}, u32[]{:S(2)}) async-start(bf16[16,152,128]{2,1,0:T(8,128)(2,1)} %packed_adapters.1), calls=%async_computation | async-start | bytes 1245184 | tf_op jit(solution)/shard_map/all_to_all | solution.py:27
  21.3 1.3 %fusion.1 = (bf16[1,1,128,2048]{3,2,1,0:T(8,128)(2,1)S(1)}, bf16[1,1,128,2048]{3,2,1,0:T(8,128)(2,1)S(1)}) fusion(bf16[1,2,128,2048]{3,2,1,0:T(8,128)(2,1)} %param.7), kind=kLoop, calls=%fused_computation.5 | loop fusion | bytes 2097152 | tf_op jit(solution)/shard_map/slice | solution.py:386
  22.6 3.2 %collective-permute-start = (bf16[1,1,128,2048]{3,2,1,0:T(8,128)(2,1)S(1)}, bf16[1,1,128,2048]{3,2,1,0:T(8,128)(2,1)S(1)}, u32[]{:S(2)}, u32[]{:S(2)}) collective-permute-start(bf16[1,1,128,2048]{3,2,1,0:T(8,128)(2,1)S(1)} %get-tuple-element.63), channel_id=1, source_target_pairs={{0,64},{64,128},{128,192},{192,256},{256,320},{320,384},{384,448},... | collective-permute-start | bytes 1572872 | tf_op jit(solution)/shard_map/ppermute | solution.py:23
  25.8 3.8 %collective-permute-start.1 = (bf16[1,2,128,256]{3,2,1,0:T(8,128)(2,1)S(1)}, bf16[1,2,128,256]{3,2,1,0:T(8,128)(2,1)S(1)}, u32[]{:S(2)}, u32[]{:S(2)}) collective-permute-start(bf16[1,2,128,256]{3,2,1,0:T(8,128)(2,1)S(1)} %copy-done.5), channel_id=1, source_target_pairs={{0,448},{64,0},{128,64},{192,128},{256,192},{320,256},{384,320},{4... | collective-permute-start | bytes 393224 | tf_op jit(solution)/shard_map/ppermute | solution.py:23
  29.6 2.8 %collective-permute-done.1 = bf16[1,2,128,256]{3,2,1,0:T(8,128)(2,1)S(1)} collective-permute-done((bf16[1,2,128,256]{3,2,1,0:T(8,128)(2,1)S(1)}, bf16[1,2,128,256]{3,2,1,0:T(8,128)(2,1)S(1)}, u32[]{:S(2)}, u32[]{:S(2)}) %collective-permute-start.1) | collective-permute-done | bytes 131104 | tf_op jit(solution)/shard_map/ppermute | solution.py:23
  32.4 3.1 %collective-permute-start.2 = (bf16[256,256]{1,0:T(8,128)(2,1)S(1)}, bf16[256,256]{1,0:T(8,128)(2,1)S(1)}, u32[]{:S(2)}, u32[]{:S(2)}) collective-permute-start(bf16[256,256]{1,0:T(8,128)(2,1)S(1)} %bitcast.25), channel_id=1, source_target_pairs={{0,1},{1,2},{2,3},{3,0},{4,5},{5,6},{6,7},{7,4},{8,9},{9,10},{10,1... | collective-permute-start | bytes 393224 | tf_op jit(solution)/shard_map/ppermute | solution.py:395
  35.5 7.4 %all-to-all-done.first_ref = bf16[16,152,128]{2,1,0:T(8,128)(2,1)S(1)} async-done(((bf16[16,152,128]{2,1,0:T(8,128)(2,1)}), bf16[16,152,128]{2,1,0:T(8,128)(2,1)S(1)}, u32[]{:S(2)}, u32[]{:S(2)}) %all-to-all-start) | async-done | bytes 622624 | tf_op jit(solution)/shard_map/all_to_all | solution.py:27
  43.4 1.5 %selected_pieces.1 = bf16[16,144,128]{2,1,0:T(8,128)(2,1)} custom-call(s32[32]{0:T(128)S(1)} %reshape.32.slots_ref.marks_ref, bf16[16,152,128]{2,1,0:T(8,128)(2,1)S(1)} %all-to-all-done.first_ref), custom_call_target="tpu_custom_call" | custom-call | tf_op jit(solution)/shard_map/selected_pieces/pallas_call | solution.py:219
  44.8 3.8 %all-to-all-start.1 = ((bf16[16,144,128]{2,1,0:T(8,128)(2,1)}), bf16[16,144,128]{2,1,0:T(8,128)(2,1)S(1)}, u32[]{:S(2)}, u32[]{:S(2)}) async-start(bf16[16,144,128]{2,1,0:T(8,128)(2,1)} %selected_pieces.1), calls=%async_computation.1 | async-start | bytes 1179648 | tf_op jit(solution)/shard_map/all_to_all | solution.py:27
  48.6 3.2 %collective-permute-start.5 = (bf16[1,1,128,2048]{3,2,1,0:T(8,128)(2,1)S(1)}, bf16[1,1,128,2048]{3,2,1,0:T(8,128)(2,1)S(1)}, u32[]{:S(2)}, u32[]{:S(2)}) collective-permute-start(bf16[1,1,128,2048]{3,2,1,0:T(8,128)(2,1)S(1)} %get-tuple-element.62), channel_id=1, source_target_pairs={{0,64},{64,128},{128,192},{192,256},{256,320},{320,384},{384,448},... | collective-permute-start | bytes 1572872 | tf_op jit(solution)/shard_map/ppermute | solution.py:23
  51.8 4.7 %collective-permute-start.3 = (bf16[256,256]{1,0:T(8,128)(2,1)S(1)}, bf16[256,256]{1,0:T(8,128)(2,1)S(1)}, u32[]{:S(2)}, u32[]{:S(2)}) collective-permute-start(bf16[256,256]{1,0:T(8,128)(2,1)S(1)} %bitcast.26), channel_id=1, source_target_pairs={{0,2},{1,3},{2,0},{3,1},{4,6},{5,7},{6,4},{7,5},{8,10},{9,11},{10,... | collective-permute-start | bytes 393224 | tf_op jit(solution)/shard_map/ppermute | solution.py:395
  56.5 2.8 %collective-permute-start.4 = (bf16[256,256]{1,0:T(8,128)(2,1)S(1)}, bf16[256,256]{1,0:T(8,128)(2,1)S(1)}, u32[]{:S(2)}, u32[]{:S(2)}) collective-permute-start(bf16[256,256]{1,0:T(8,128)(2,1)S(1)} %bitcast.27), channel_id=1, source_target_pairs={{0,3},{1,0},{2,1},{3,2},{4,7},{5,4},{6,5},{7,6},{8,11},{9,8},{10,9... | collective-permute-start | bytes 393224 | tf_op jit(solution)/shard_map/ppermute | solution.py:395
  60.0 2.9 %collective-permute-done.4.refs_5_ = bf16[256,256]{1,0:T(8,128)(2,1)S(1)} collective-permute-done((bf16[256,256]{1,0:T(8,128)(2,1)S(1)}, bf16[256,256]{1,0:T(8,128)(2,1)S(1)}, u32[]{:S(2)}, u32[]{:S(2)}) %collective-permute-start.4) | collective-permute-done | bytes 131104 | tf_op jit(solution)/shard_map/ppermute | solution.py:395
  62.9 9.4 %all-to-all-done.1.second_ref.down_ref = bf16[16,144,128]{2,1,0:T(8,128)(2,1)S(1)} async-done(((bf16[16,144,128]{2,1,0:T(8,128)(2,1)}), bf16[16,144,128]{2,1,0:T(8,128)(2,1)S(1)}, u32[]{:S(2)}, u32[]{:S(2)}) %all-to-all-start.1) | async-done | bytes 589856 | tf_op jit(solution)/shard_map/all_to_all | solution.py:27
  72.3 1.2 %rank_parts.1 = (bf16[4,2,2,64,128]{4,3,2,1,0:T(8,128)(2,1)}, f32[2,64,256]{2,1,0:T(8,128)S(1)}) custom-call(bf16[16,144,128]{2,1,0:T(8,128)(2,1)S(1)} %all-to-all-done.1.second_ref.down_ref, bf16[2,128,256]{2,1,0:T(8,128)(2,1)S(1)} %bitcast.28, bf16[1,1,128,2048]{3,2,1,0:T(8,128)(2,1)S(1)} %collective-permute-done.refs_0_, ...), custom_call_target="tpu_custom_call" | custom-call | tf_op jit(solution)/shard_map/rank_parts/pallas_call | solution.py:177
  73.5 4.0 %all-to-all-start.2 = ((bf16[4,2,2,64,128]{4,3,2,1,0:T(8,128)(2,1)}), bf16[4,2,2,64,128]{4,3,2,1,0:T(8,128)(2,1)S(1)}, u32[]{:S(2)}, u32[]{:S(2)}) async-start(bf16[4,2,2,64,128]{4,3,2,1,0:T(8,128)(2,1)} %get-tuple-element.38), calls=%async_computation.2 | async-start | bytes 524288 | tf_op jit(solution)/shard_map/all_to_all | solution.py:27
  77.5 2.2 %copy-done.3 = bf16[1024,2048]{1,0:T(8,128)(2,1)S(1)} copy-done((bf16[1024,2048]{1,0:T(8,128)(2,1)S(1)}, bf16[1024,2048]{1,0:T(8,128)(2,1)}, u32[]{:S(2)}) %copy-start.3) | copy-done | bytes 4194328
  79.7 2.7 %weight_products.1 = (bf16[256,256]{1,0:T(8,128)(2,1)S(1)}, bf16[256,256]{1,0:T(8,128)(2,1)S(1)}, bf16[256,256]{1,0:T(8,128)(2,1)S(1)}, bf16[256,256]{1,0:T(8,128)(2,1)S(1)}, f32[256,2048]{1,0:T(8,128)S(1)}) custom-call(s32[1]{0:T(128)} %bitcast.8.first_ref, bf16[1,1,128,2048]{3,2,1,0:T(8,128)(2,1)S(1)} %collective-permute-done.refs_0_, ...), custom_call_target="tpu_custom_call" | custom-call | flops 2147483648 | bytes 7340032 | tf_op jit(solution)/shard_map/weight_products/pallas_call | solution.py:132
  82.4 1.3 %copy-done.1 = f32[256,2048]{1,0:T(8,128)} copy-done((f32[256,2048]{1,0:T(8,128)}, f32[256,2048]{1,0:T(8,128)S(1)}, u32[]{:S(2)}) %copy-start.1) | copy-done | bytes 2097176
  83.8 1.0 ranks_and_pieces.1
  84.8 5.3 %all-to-all-start.3 = ((bf16[16,2,32,256]{3,2,1,0:T(8,128)(2,1)}), bf16[16,2,32,256]{3,2,1,0:T(8,128)(2,1)S(1)}, u32[]{:S(2)}, u32[]{:S(2)}) async-start(bf16[16,2,32,256]{3,2,1,0:T(8,128)(2,1)} %get-tuple-element.49), calls=%async_computation.3 | async-start | bytes 1048576 | tf_op jit(solution)/shard_map/all_to_all | solution.py:27
  90.7 2.7 %collective-permute-start.6 = (bf16[256,256]{1,0:T(8,128)(2,1)S(1)}, bf16[256,256]{1,0:T(8,128)(2,1)S(1)}, u32[]{:S(2)}, u32[]{:S(2)}) collective-permute-start(bf16[256,256]{1,0:T(8,128)(2,1)S(1)} %get-tuple-element.54), channel_id=1, source_target_pairs={{0,1},{1,2},{2,3},{3,0},{4,5},{5,6},{6,7},{7,4},{8,9},{9,10},{10,1... | collective-permute-start | bytes 393224 | tf_op jit(solution)/shard_map/ppermute | solution.py:422
  93.4 4.3 %collective-permute-start.7 = (bf16[256,256]{1,0:T(8,128)(2,1)S(1)}, bf16[256,256]{1,0:T(8,128)(2,1)S(1)}, u32[]{:S(2)}, u32[]{:S(2)}) collective-permute-start(bf16[256,256]{1,0:T(8,128)(2,1)S(1)} %get-tuple-element.55), channel_id=1, source_target_pairs={{0,2},{1,3},{2,0},{3,1},{4,6},{5,7},{6,4},{7,5},{8,10},{9,11},{10,... | collective-permute-start | bytes 393224 | tf_op jit(solution)/shard_map/ppermute | solution.py:422
  97.7 3.1 %collective-permute-start.8 = (bf16[256,256]{1,0:T(8,128)(2,1)S(1)}, bf16[256,256]{1,0:T(8,128)(2,1)S(1)}, u32[]{:S(2)}, u32[]{:S(2)}) collective-permute-start(bf16[256,256]{1,0:T(8,128)(2,1)S(1)} %get-tuple-element.56), channel_id=1, source_target_pairs={{0,3},{1,0},{2,1},{3,2},{4,7},{5,4},{6,5},{7,6},{8,11},{9,8},{10,9... | collective-permute-start | bytes 393224 | tf_op jit(solution)/shard_map/ppermute | solution.py:422
  101.4 2.9 %input_gradients.1 = bf16[2,128,2048]{2,1,0:T(8,128)(2,1)} custom-call(s32[2]{0:T(128)} %fusion.live_ref, bf16[2,64,128]{2,1,0:T(8,128)(2,1)} %get-tuple-element.65.ranks_ref, bf16[16,144,128]{2,1,0:T(8,128)(2,1)} %copy-done, f32[256,2048]{1,0:T(8,128)} %copy-done.1), custom_call_target="tpu_custom_call" | custom-call | flops 67108864 | bytes 3145728 | tf_op jit(solution)/shard_map/input_gradients/pallas_call | solution.py:248
  105.0 1.5 %layer_outputs.1 = bf16[2,128,256]{2,1,0:T(8,128)(2,1)} custom-call(s32[2]{0:T(128)S(1)} %copy-done.2, bf16[2,64,128]{2,1,0:T(8,128)(2,1)S(1)} %get-tuple-element.64.ranks_ref, f32[2,64,256]{2,1,0:T(8,128)S(1)} %get-tuple-element.52.up_ref, bf16[256,256]{1,0:T(8,128)(2,1)S(1)} %get-tuple-element.53.refs_0_, ...), custom_call_target="tpu_custom_call" | custom-call | tf_op jit(solution)/shard_map/layer_outputs/pallas_call | solution.py:278
  106.4 1.0 all-to-all-done.3.pieces_ref
  107.5 0.8 slot_sums.3
  108.3 2.1 %collective-permute-start.9 = (f32[2,2,32,256]{3,2,1,0:T(8,128)S(1)}, f32[2,2,32,256]{3,2,1,0:T(8,128)S(1)}, u32[]{:S(2)}, u32[]{:S(2)}) collective-permute-start(f32[2,2,32,256]{3,2,1,0:T(8,128)S(1)} %slot_sums.3), channel_id=1, source_target_pairs={{0,4},{4,0},{8,12},{12,8},{16,20},{20,16},{24,28},{28,24},{32,36},... | collective-permute-start | bytes 393224 | tf_op jit(solution)/shard_map/ppermute | solution.py:431
  110.4 0.8 slot_sums.2.own_ref
  111.6 0.7 placed_sums.1
  (26 shorter events, 3.3 us)
Async XLA Ops:
  7.2 18.6 %copy-start.5 = (bf16[1,2,128,256]{3,2,1,0:T(8,128)(2,1)S(1)}, bf16[1,2,128,256]{3,2,1,0:T(8,128)(2,1)}, u32[]{:S(2)}) copy-start(bf16[1,2,128,256]{3,2,1,0:T(8,128)(2,1)} %param.8) | copy-start | bytes 393220
  7.2 70.3 %all-gather.3.cloned.1.call-start = ((), (), s32[]{:S(2)}) async-start(), calls=%async_computation.4 | async-start | bytes 4456448 | tf_op jit(solution)/shard_map/all_gather | solution.py:402
  9.4 33.5 %all-to-all-start = ((bf16[16,152,128]{2,1,0:T(8,128)(2,1)}), bf16[16,152,128]{2,1,0:T(8,128)(2,1)S(1)}, u32[]{:S(2)}, u32[]{:S(2)}) async-start(bf16[16,152,128]{2,1,0:T(8,128)(2,1)} %packed_adapters.1), calls=%async_computation | async-start | bytes 1245184 | tf_op jit(solution)/shard_map/all_to_all | solution.py:27
  22.6 22.3 %collective-permute-start = (bf16[1,1,128,2048]{3,2,1,0:T(8,128)(2,1)S(1)}, bf16[1,1,128,2048]{3,2,1,0:T(8,128)(2,1)S(1)}, u32[]{:S(2)}, u32[]{:S(2)}) collective-permute-start(bf16[1,1,128,2048]{3,2,1,0:T(8,128)(2,1)S(1)} %get-tuple-element.63), channel_id=1, source_target_pairs={{0,64},{64,128},{128,192},{192,256},{256,320},{320,384},{384,448},... | collective-permute-start | bytes 1572872 | tf_op jit(solution)/shard_map/ppermute | solution.py:23
  25.8 6.6 %collective-permute-start.1 = (bf16[1,2,128,256]{3,2,1,0:T(8,128)(2,1)S(1)}, bf16[1,2,128,256]{3,2,1,0:T(8,128)(2,1)S(1)}, u32[]{:S(2)}, u32[]{:S(2)}) collective-permute-start(bf16[1,2,128,256]{3,2,1,0:T(8,128)(2,1)S(1)} %copy-done.5), channel_id=1, source_target_pairs={{0,448},{64,0},{128,64},{192,128},{256,192},{320,256},{384,320},{4... | collective-permute-start | bytes 393224 | tf_op jit(solution)/shard_map/ppermute | solution.py:23
  32.4 12.4 %collective-permute-start.2 = (bf16[256,256]{1,0:T(8,128)(2,1)S(1)}, bf16[256,256]{1,0:T(8,128)(2,1)S(1)}, u32[]{:S(2)}, u32[]{:S(2)}) collective-permute-start(bf16[256,256]{1,0:T(8,128)(2,1)S(1)} %bitcast.25), channel_id=1, source_target_pairs={{0,1},{1,2},{2,3},{3,0},{4,5},{5,6},{6,7},{7,4},{8,9},{9,10},{10,1... | collective-permute-start | bytes 393224 | tf_op jit(solution)/shard_map/ppermute | solution.py:395
  44.8 27.4 %all-to-all-start.1 = ((bf16[16,144,128]{2,1,0:T(8,128)(2,1)}), bf16[16,144,128]{2,1,0:T(8,128)(2,1)S(1)}, u32[]{:S(2)}, u32[]{:S(2)}) async-start(bf16[16,144,128]{2,1,0:T(8,128)(2,1)} %selected_pieces.1), calls=%async_computation.1 | async-start | bytes 1179648 | tf_op jit(solution)/shard_map/all_to_all | solution.py:27
  48.6 23.6 %collective-permute-start.5 = (bf16[1,1,128,2048]{3,2,1,0:T(8,128)(2,1)S(1)}, bf16[1,1,128,2048]{3,2,1,0:T(8,128)(2,1)S(1)}, u32[]{:S(2)}, u32[]{:S(2)}) collective-permute-start(bf16[1,1,128,2048]{3,2,1,0:T(8,128)(2,1)S(1)} %get-tuple-element.62), channel_id=1, source_target_pairs={{0,64},{64,128},{128,192},{192,256},{256,320},{320,384},{384,448},... | collective-permute-start | bytes 1572872 | tf_op jit(solution)/shard_map/ppermute | solution.py:23
  51.8 8.1 %collective-permute-start.3 = (bf16[256,256]{1,0:T(8,128)(2,1)S(1)}, bf16[256,256]{1,0:T(8,128)(2,1)S(1)}, u32[]{:S(2)}, u32[]{:S(2)}) collective-permute-start(bf16[256,256]{1,0:T(8,128)(2,1)S(1)} %bitcast.26), channel_id=1, source_target_pairs={{0,2},{1,3},{2,0},{3,1},{4,6},{5,7},{6,4},{7,5},{8,10},{9,11},{10,... | collective-permute-start | bytes 393224 | tf_op jit(solution)/shard_map/ppermute | solution.py:395
  56.5 6.4 %collective-permute-start.4 = (bf16[256,256]{1,0:T(8,128)(2,1)S(1)}, bf16[256,256]{1,0:T(8,128)(2,1)S(1)}, u32[]{:S(2)}, u32[]{:S(2)}) collective-permute-start(bf16[256,256]{1,0:T(8,128)(2,1)S(1)} %bitcast.27), channel_id=1, source_target_pairs={{0,3},{1,0},{2,1},{3,2},{4,7},{5,4},{6,5},{7,6},{8,11},{9,8},{10,9... | collective-permute-start | bytes 393224 | tf_op jit(solution)/shard_map/ppermute | solution.py:395
  72.3 10.1 %copy-start = (bf16[16,144,128]{2,1,0:T(8,128)(2,1)}, bf16[16,144,128]{2,1,0:T(8,128)(2,1)S(1)}, u32[]{:S(2)}) copy-start(bf16[16,144,128]{2,1,0:T(8,128)(2,1)S(1)} %all-to-all-done.1.second_ref.down_ref) | copy-start | bytes 1769476
  73.5 10.3 %all-to-all-start.2 = ((bf16[4,2,2,64,128]{4,3,2,1,0:T(8,128)(2,1)}), bf16[4,2,2,64,128]{4,3,2,1,0:T(8,128)(2,1)S(1)}, u32[]{:S(2)}, u32[]{:S(2)}) async-start(bf16[4,2,2,64,128]{4,3,2,1,0:T(8,128)(2,1)} %get-tuple-element.38), calls=%async_computation.2 | async-start | bytes 524288 | tf_op jit(solution)/shard_map/all_to_all | solution.py:27
  77.5 2.2 %copy-start.3 = (bf16[1024,2048]{1,0:T(8,128)(2,1)S(1)}, bf16[1024,2048]{1,0:T(8,128)(2,1)}, u32[]{:S(2)}) copy-start(bf16[1024,2048]{1,0:T(8,128)(2,1)} %all-gather.3.cloned.1.call-done) | copy-start | bytes 12582916
  79.7 10.5 %copy-start.4 = (s32[1,2,1]{1,2,0:T(1,128)S(1)}, s32[1,2,1]{1,2,0:T(1,128)}, u32[]{:S(2)}) copy-start(s32[1,2,1]{1,2,0:T(1,128)} %param.13) | copy-start | bytes 28
  82.4 1.4 %copy-start.1 = (f32[256,2048]{1,0:T(8,128)}, f32[256,2048]{1,0:T(8,128)S(1)}, u32[]{:S(2)}) copy-start(f32[256,2048]{1,0:T(8,128)S(1)} %get-tuple-element.51.product_ref) | copy-start | bytes 6291460
  84.8 22.7 %all-to-all-start.3 = ((bf16[16,2,32,256]{3,2,1,0:T(8,128)(2,1)}), bf16[16,2,32,256]{3,2,1,0:T(8,128)(2,1)S(1)}, u32[]{:S(2)}, u32[]{:S(2)}) async-start(bf16[16,2,32,256]{3,2,1,0:T(8,128)(2,1)} %get-tuple-element.49), calls=%async_computation.3 | async-start | bytes 1048576 | tf_op jit(solution)/shard_map/all_to_all | solution.py:27
  90.7 13.6 %collective-permute-start.6 = (bf16[256,256]{1,0:T(8,128)(2,1)S(1)}, bf16[256,256]{1,0:T(8,128)(2,1)S(1)}, u32[]{:S(2)}, u32[]{:S(2)}) collective-permute-start(bf16[256,256]{1,0:T(8,128)(2,1)S(1)} %get-tuple-element.54), channel_id=1, source_target_pairs={{0,1},{1,2},{2,3},{3,0},{4,5},{5,6},{6,7},{7,4},{8,9},{9,10},{10,1... | collective-permute-start | bytes 393224 | tf_op jit(solution)/shard_map/ppermute | solution.py:422
  93.4 10.9 %collective-permute-start.7 = (bf16[256,256]{1,0:T(8,128)(2,1)S(1)}, bf16[256,256]{1,0:T(8,128)(2,1)S(1)}, u32[]{:S(2)}, u32[]{:S(2)}) collective-permute-start(bf16[256,256]{1,0:T(8,128)(2,1)S(1)} %get-tuple-element.55), channel_id=1, source_target_pairs={{0,2},{1,3},{2,0},{3,1},{4,6},{5,7},{6,4},{7,5},{8,10},{9,11},{10,... | collective-permute-start | bytes 393224 | tf_op jit(solution)/shard_map/ppermute | solution.py:422
  97.7 6.6 %collective-permute-start.8 = (bf16[256,256]{1,0:T(8,128)(2,1)S(1)}, bf16[256,256]{1,0:T(8,128)(2,1)S(1)}, u32[]{:S(2)}, u32[]{:S(2)}) collective-permute-start(bf16[256,256]{1,0:T(8,128)(2,1)S(1)} %get-tuple-element.56), channel_id=1, source_target_pairs={{0,3},{1,0},{2,1},{3,2},{4,7},{5,4},{6,5},{7,6},{8,11},{9,8},{10,9... | collective-permute-start | bytes 393224 | tf_op jit(solution)/shard_map/ppermute | solution.py:422
  104.3 0.7 copy-start.2
  108.3 3.2 %collective-permute-start.9 = (f32[2,2,32,256]{3,2,1,0:T(8,128)S(1)}, f32[2,2,32,256]{3,2,1,0:T(8,128)S(1)}, u32[]{:S(2)}, u32[]{:S(2)}) collective-permute-start(f32[2,2,32,256]{3,2,1,0:T(8,128)S(1)} %slot_sums.3), channel_id=1, source_target_pairs={{0,4},{4,0},{8,12},{12,8},{16,20},{20,16},{24,28},{28,24},{32,36},... | collective-permute-start | bytes 393224 | tf_op jit(solution)/shard_map/ppermute | solution.py:431
Sparse Core Ops, SparseCore 0:
  10.1 66.2 all-gather.2

commit v8 on v7

--- a/solution.py
+++ b/solution.py
@@ -227,7 +227,7 @@
     )(slots, first)
 
 
-def gradient_kernel(micro, live_ref, ranks_ref, down_ref, product_ref, out_ref):
+def gradient_kernel(micro, count, marks_ref, me_ref, ranks_ref, down_ref, product_ref, out_ref):
     rank = ranks_ref.shape[1]
     pieces = down_ref.shape[0]
     for m in range(micro):
@@ -237,19 +237,21 @@
         )
         lora = jnp.dot(back, down, preferred_element_type=f32).astype(bf16).astype(f32)
         part = product_ref[m * BLOCK_ROWS : (m + 1) * BLOCK_ROWS] + lora
-        out_ref[m] = jnp.where(live_ref[m] > 0, part, 0.0).astype(bf16)
-
-
-def input_gradients(live, ranks, second, product):
+        live = marks_ref[me_ref[0] * micro + m] < count
+        out_ref[m] = jnp.where(live, part, 0.0).astype(bf16)
+
+
+def input_gradients(marks, me, count, ranks, second, product):
     micro, rank = ranks.shape[:2]
     rows, width = product.shape
     pieces, _, piece = second.shape
     steps = 2
     return pl.pallas_call(
-        functools.partial(gradient_kernel, micro),
+        functools.partial(gradient_kernel, micro, count),
         grid=(steps,),
         out_shape=jax.ShapeDtypeStruct((micro, BLOCK_ROWS, width), bf16),
         in_specs=[
+            smem(),
             smem(),
             pl.BlockSpec(ranks.shape, lambda i: (0, 0, 0)),
             pl.BlockSpec((pieces // steps, micro * rank, piece), lambda i: (i, 0, 0)),
@@ -261,28 +263,29 @@
             flops=2 * rows * width * rank, bytes_accessed=6 * rows * width, transcendentals=0
         ),
         name="input_gradients",
-    )(live, ranks, second, product)
-
-
-def layer_kernel(micro, live_ref, ranks_ref, up_ref, *refs):
+    )(marks, me, ranks, second, product)
+
+
+def layer_kernel(micro, count, marks_ref, me_ref, ranks_ref, up_ref, *refs):
     out_ref = refs[-1]
     for m in range(micro):
         total = adapter_scale * tn_dot(ranks_ref[m], up_ref[m].astype(bf16))
         for part_ref in refs[:-1]:
             total += part_ref[m * BLOCK_ROWS : (m + 1) * BLOCK_ROWS, :].astype(f32)
-        out_ref[m] = jnp.where(live_ref[m] > 0, total, 0.0).astype(bf16)
-
-
-def layer_outputs(live, ranks, up, parts):
+        live = marks_ref[me_ref[0] * micro + m] < count
+        out_ref[m] = jnp.where(live, total, 0.0).astype(bf16)
+
+
+def layer_outputs(marks, me, count, ranks, up, parts):
     micro, _, columns = up.shape
     return pl.pallas_call(
-        functools.partial(layer_kernel, micro),
+        functools.partial(layer_kernel, micro, count),
         out_shape=jax.ShapeDtypeStruct((micro, BLOCK_ROWS, columns), bf16),
-        in_specs=[smem()] + [pl.BlockSpec(memory_space=pltpu.VMEM)] * (2 + len(parts)),
+        in_specs=[smem(), smem()] + [pl.BlockSpec(memory_space=pltpu.VMEM)] * (2 + len(parts)),
         out_specs=pl.BlockSpec(memory_space=pltpu.VMEM),
         compiler_params=params(),
         name="layer_outputs",
-    )(live, ranks, up, *parts)
+    )(marks, me, ranks, up, *parts)
 
 
 def rank_kernel(parts_ref, incoming_ref, ranks_ref, pieces_ref):
@@ -387,7 +390,6 @@
 
     slot_table = slot_language[0]
     langs = block_language[0, :, 0]
-    live = (langs < slot_table.shape[0]).astype(jnp.int32)
 
     weight = jnp.swapaxes(base_weight[0], 0, 1)
     flat_cots = returned.reshape(rows, columns)
@@ -422,8 +424,9 @@
         lax.ppermute(base_parts[k], "mp", [(i, (i + k) % quarters) for i in range(quarters)])
         for k in range(1, quarters)
     ]
-    layer_out = layer_outputs(live, rank_in, up, base_parts)[None]
-    input_gradient = input_gradients(live, rank_back, second, back)[None]
+    place, count = me.astype(jnp.int32).reshape(1), slot_table.shape[0]
+    layer_out = layer_outputs(slots, place, count, rank_in, up, base_parts)[None]
+    input_gradient = input_gradients(slots, place, count, rank_back, second, back)[None]
     pieces, input_gradient, layer_out = lax.optimization_barrier(
         (pieces, input_gradient, layer_out)
     )

time: 120 us -> 120 us (level)
  waiting for transfers between devices: 24.6 us -> 25.9 us
where the time goes in v8:
time: 120 us; the launch traced here: 119 us
  starting transfers between devices  57.8 us (48%)
  waiting for transfers between devices  25.9 us (22%)
  Pallas kernels  15.4 us (13%)
  between operations  14.3 us (12%)
  local copies, waits for them, and re-layouts  5.53 us (5%)
    all_to_all x4, starting transfers between devices, exchanged(): return lax.all_to_all(array, axis, split_axis=0, concat_axis=0, tiled=True)  25 us
    all_to_all x4, waiting for transfers between devices, exchanged(): return lax.all_to_all(array, axis, split_axis=0, concat_axis=0, tiled=True)  18.9 us
    ppermute x3, starting transfers between devices, shards(): lax.ppermute(flat_cots, 'mp', [(i, (i + k) % quarters) for i in range(qua...  10.5 us
    ppermute x3, starting transfers between devices, passed_along(): lax.ppermute(array, axis, [(i, (i + by) % devices) for i in range(devices)])  10.2 us
    ppermute x3, starting transfers between devices, shards(): lax.ppermute(base_parts[k], 'mp', [(i, (i + k) % quarters) for i in range...  10.1 us
    ppermute x3, waiting for transfers between devices, shards(): lax.ppermute(flat_cots, 'mp', [(i, (i + k) % quarters) for i in range(qua...  3.62 us
    unnamed x12, local copies, waits for them, and re-layouts  3.55 us
    pallas_call x1, Pallas kernels, input_gradients(): pl.pallas_call(functools.partial(gradient_kernel, micro, count), grid=(st...  2.87 us
  transfers between devices with their start and end apart: 15, of which 7 were waited for; matrix products, arithmetic and copies ran while one was open for 2% of the time, Pallas kernels for 9%

profile of v8, /device:TPU:1, one launch (start us, length us, event | category | flops | bytes accessed | tf_op | source)
XLA Modules:
  0.0 119.1 jit_solution(6859828975490259780)
XLA Ops:
  7.2 2.2 %packed_adapters.1 = bf16[16,152,128]{2,1,0:T(8,128)(2,1)} custom-call(s32[1,2]{1,0:T(1,128)} %bitcast.36, s32[1,32]{1,0:T(1,128)} %table_ref.1, bf16[2,64,2048]{2,1,0:T(8,128)(2,1)} %bitcast.32, bf16[2,64,256]{2,1,0:T(8,128)(2,1)} %bitcast.35), custom_call_target="tpu_custom_call" | custom-call | tf_op jit(solution)/shard_map/packed_adapters/pallas_call | solution.py:83
  9.4 11.9 %all-to-all-start = ((bf16[16,152,128]{2,1,0:T(8,128)(2,1)}), bf16[16,152,128]{2,1,0:T(8,128)(2,1)S(1)}, u32[]{:S(2)}, u32[]{:S(2)}) async-start(bf16[16,152,128]{2,1,0:T(8,128)(2,1)} %packed_adapters.1), calls=%async_computation | async-start | bytes 1245184 | tf_op jit(solution)/shard_map/all_to_all | solution.py:27
  21.3 1.3 %fusion = (bf16[1,1,128,2048]{3,2,1,0:T(8,128)(2,1)S(1)}, bf16[1,1,128,2048]{3,2,1,0:T(8,128)(2,1)S(1)}) fusion(bf16[1,2,128,2048]{3,2,1,0:T(8,128)(2,1)} %param.7), kind=kLoop, calls=%fused_computation.3 | loop fusion | bytes 2097152 | tf_op jit(solution)/shard_map/slice | solution.py:389
  22.6 3.2 %collective-permute-start = (bf16[1,1,128,2048]{3,2,1,0:T(8,128)(2,1)S(1)}, bf16[1,1,128,2048]{3,2,1,0:T(8,128)(2,1)S(1)}, u32[]{:S(2)}, u32[]{:S(2)}) collective-permute-start(bf16[1,1,128,2048]{3,2,1,0:T(8,128)(2,1)S(1)} %get-tuple-element.63), channel_id=1, source_target_pairs={{0,64},{64,128},{128,192},{192,256},{256,320},{320,384},{384,448},... | collective-permute-start | bytes 1572872 | tf_op jit(solution)/shard_map/ppermute | solution.py:23
  25.8 3.8 %collective-permute-start.1 = (bf16[1,2,128,256]{3,2,1,0:T(8,128)(2,1)S(1)}, bf16[1,2,128,256]{3,2,1,0:T(8,128)(2,1)S(1)}, u32[]{:S(2)}, u32[]{:S(2)}) collective-permute-start(bf16[1,2,128,256]{3,2,1,0:T(8,128)(2,1)S(1)} %copy-done.5), channel_id=1, source_target_pairs={{0,448},{64,0},{128,64},{192,128},{256,192},{320,256},{384,320},{4... | collective-permute-start | bytes 393224 | tf_op jit(solution)/shard_map/ppermute | solution.py:23
  29.6 2.8 %collective-permute-done.1 = bf16[1,2,128,256]{3,2,1,0:T(8,128)(2,1)S(1)} collective-permute-done((bf16[1,2,128,256]{3,2,1,0:T(8,128)(2,1)S(1)}, bf16[1,2,128,256]{3,2,1,0:T(8,128)(2,1)S(1)}, u32[]{:S(2)}, u32[]{:S(2)}) %collective-permute-start.1) | collective-permute-done | bytes 131104 | tf_op jit(solution)/shard_map/ppermute | solution.py:23
  32.4 3.1 %collective-permute-start.2 = (bf16[256,256]{1,0:T(8,128)(2,1)S(1)}, bf16[256,256]{1,0:T(8,128)(2,1)S(1)}, u32[]{:S(2)}, u32[]{:S(2)}) collective-permute-start(bf16[256,256]{1,0:T(8,128)(2,1)S(1)} %bitcast.24), channel_id=1, source_target_pairs={{0,1},{1,2},{2,3},{3,0},{4,5},{5,6},{6,7},{7,4},{8,9},{9,10},{10,1... | collective-permute-start | bytes 393224 | tf_op jit(solution)/shard_map/ppermute | solution.py:397
  35.5 7.4 %all-to-all-done.first_ref = bf16[16,152,128]{2,1,0:T(8,128)(2,1)S(1)} async-done(((bf16[16,152,128]{2,1,0:T(8,128)(2,1)}), bf16[16,152,128]{2,1,0:T(8,128)(2,1)S(1)}, u32[]{:S(2)}, u32[]{:S(2)}) %all-to-all-start) | async-done | bytes 622624 | tf_op jit(solution)/shard_map/all_to_all | solution.py:27
  43.4 1.4 %selected_pieces.1 = bf16[16,144,128]{2,1,0:T(8,128)(2,1)} custom-call(s32[32]{0:T(128)S(1)} %reshape.32.slots_ref.marks_ref, bf16[16,152,128]{2,1,0:T(8,128)(2,1)S(1)} %all-to-all-done.first_ref), custom_call_target="tpu_custom_call" | custom-call | tf_op jit(solution)/shard_map/selected_pieces/pallas_call | solution.py:219
  44.9 3.8 %all-to-all-start.1 = ((bf16[16,144,128]{2,1,0:T(8,128)(2,1)}), bf16[16,144,128]{2,1,0:T(8,128)(2,1)S(1)}, u32[]{:S(2)}, u32[]{:S(2)}) async-start(bf16[16,144,128]{2,1,0:T(8,128)(2,1)} %selected_pieces.1), calls=%async_computation.1 | async-start | bytes 1179648 | tf_op jit(solution)/shard_map/all_to_all | solution.py:27
  48.7 3.2 %collective-permute-start.5 = (bf16[1,1,128,2048]{3,2,1,0:T(8,128)(2,1)S(1)}, bf16[1,1,128,2048]{3,2,1,0:T(8,128)(2,1)S(1)}, u32[]{:S(2)}, u32[]{:S(2)}) collective-permute-start(bf16[1,1,128,2048]{3,2,1,0:T(8,128)(2,1)S(1)} %get-tuple-element.62), channel_id=1, source_target_pairs={{0,64},{64,128},{128,192},{192,256},{256,320},{320,384},{384,448},... | collective-permute-start | bytes 1572872 | tf_op jit(solution)/shard_map/ppermute | solution.py:23
  51.9 4.7 %collective-permute-start.3 = (bf16[256,256]{1,0:T(8,128)(2,1)S(1)}, bf16[256,256]{1,0:T(8,128)(2,1)S(1)}, u32[]{:S(2)}, u32[]{:S(2)}) collective-permute-start(bf16[256,256]{1,0:T(8,128)(2,1)S(1)} %bitcast.25), channel_id=1, source_target_pairs={{0,2},{1,3},{2,0},{3,1},{4,6},{5,7},{6,4},{7,5},{8,10},{9,11},{10,... | collective-permute-start | bytes 393224 | tf_op jit(solution)/shard_map/ppermute | solution.py:397
  56.5 2.8 %collective-permute-start.4 = (bf16[256,256]{1,0:T(8,128)(2,1)S(1)}, bf16[256,256]{1,0:T(8,128)(2,1)S(1)}, u32[]{:S(2)}, u32[]{:S(2)}) collective-permute-start(bf16[256,256]{1,0:T(8,128)(2,1)S(1)} %bitcast.26), channel_id=1, source_target_pairs={{0,3},{1,0},{2,1},{3,2},{4,7},{5,4},{6,5},{7,6},{8,11},{9,8},{10,9... | collective-permute-start | bytes 393224 | tf_op jit(solution)/shard_map/ppermute | solution.py:397
  60.0 2.9 %collective-permute-done.4.refs_5_ = bf16[256,256]{1,0:T(8,128)(2,1)S(1)} collective-permute-done((bf16[256,256]{1,0:T(8,128)(2,1)S(1)}, bf16[256,256]{1,0:T(8,128)(2,1)S(1)}, u32[]{:S(2)}, u32[]{:S(2)}) %collective-permute-start.4) | collective-permute-done | bytes 131104 | tf_op jit(solution)/shard_map/ppermute | solution.py:397
  62.9 9.4 %all-to-all-done.1.second_ref.down_ref = bf16[16,144,128]{2,1,0:T(8,128)(2,1)S(1)} async-done(((bf16[16,144,128]{2,1,0:T(8,128)(2,1)}), bf16[16,144,128]{2,1,0:T(8,128)(2,1)S(1)}, u32[]{:S(2)}, u32[]{:S(2)}) %all-to-all-start.1) | async-done | bytes 589856 | tf_op jit(solution)/shard_map/all_to_all | solution.py:27
  72.3 1.2 %rank_parts.1 = (bf16[4,2,2,64,128]{4,3,2,1,0:T(8,128)(2,1)}, f32[2,64,256]{2,1,0:T(8,128)S(1)}) custom-call(bf16[16,144,128]{2,1,0:T(8,128)(2,1)S(1)} %all-to-all-done.1.second_ref.down_ref, bf16[2,128,256]{2,1,0:T(8,128)(2,1)S(1)} %bitcast.27, bf16[1,1,128,2048]{3,2,1,0:T(8,128)(2,1)S(1)} %collective-permute-done.refs_0_, ...), custom_call_target="tpu_custom_call" | custom-call | tf_op jit(solution)/shard_map/rank_parts/pallas_call | solution.py:177
  73.5 4.0 %all-to-all-start.2 = ((bf16[4,2,2,64,128]{4,3,2,1,0:T(8,128)(2,1)}), bf16[4,2,2,64,128]{4,3,2,1,0:T(8,128)(2,1)S(1)}, u32[]{:S(2)}, u32[]{:S(2)}) async-start(bf16[4,2,2,64,128]{4,3,2,1,0:T(8,128)(2,1)} %get-tuple-element.38), calls=%async_computation.2 | async-start | bytes 524288 | tf_op jit(solution)/shard_map/all_to_all | solution.py:27
  77.5 2.2 %copy-done.4 = bf16[1024,2048]{1,0:T(8,128)(2,1)S(1)} copy-done((bf16[1024,2048]{1,0:T(8,128)(2,1)S(1)}, bf16[1024,2048]{1,0:T(8,128)(2,1)}, u32[]{:S(2)}) %copy-start.4) | copy-done | bytes 4194328
  79.7 2.7 %weight_products.1 = (bf16[256,256]{1,0:T(8,128)(2,1)S(1)}, bf16[256,256]{1,0:T(8,128)(2,1)S(1)}, bf16[256,256]{1,0:T(8,128)(2,1)S(1)}, bf16[256,256]{1,0:T(8,128)(2,1)S(1)}, f32[256,2048]{1,0:T(8,128)S(1)}) custom-call(s32[1]{0:T(128)} %bitcast.8.first_ref, bf16[1,1,128,2048]{3,2,1,0:T(8,128)(2,1)S(1)} %collective-permute-done.refs_0_, ...), custom_call_target="tpu_custom_call" | custom-call | flops 2147483648 | bytes 7340032 | tf_op jit(solution)/shard_map/weight_products/pallas_call | solution.py:132
  82.5 1.3 %copy-done.1 = f32[256,2048]{1,0:T(8,128)} copy-done((f32[256,2048]{1,0:T(8,128)}, f32[256,2048]{1,0:T(8,128)S(1)}, u32[]{:S(2)}) %copy-start.1) | copy-done | bytes 2097176
  83.8 1.0 ranks_and_pieces.1
  84.8 5.3 %all-to-all-start.3 = ((bf16[16,2,32,256]{3,2,1,0:T(8,128)(2,1)}), bf16[16,2,32,256]{3,2,1,0:T(8,128)(2,1)S(1)}, u32[]{:S(2)}, u32[]{:S(2)}) async-start(bf16[16,2,32,256]{3,2,1,0:T(8,128)(2,1)} %get-tuple-element.49), calls=%async_computation.3 | async-start | bytes 1048576 | tf_op jit(solution)/shard_map/all_to_all | solution.py:27
  90.1 2.8 %collective-permute-start.6 = (bf16[256,256]{1,0:T(8,128)(2,1)S(1)}, bf16[256,256]{1,0:T(8,128)(2,1)S(1)}, u32[]{:S(2)}, u32[]{:S(2)}) collective-permute-start(bf16[256,256]{1,0:T(8,128)(2,1)S(1)} %get-tuple-element.54), channel_id=1, source_target_pairs={{0,1},{1,2},{2,3},{3,0},{4,5},{5,6},{6,7},{7,4},{8,9},{9,10},{10,1... | collective-permute-start | bytes 393224 | tf_op jit(solution)/shard_map/ppermute | solution.py:424
  92.9 4.3 %collective-permute-start.7 = (bf16[256,256]{1,0:T(8,128)(2,1)S(1)}, bf16[256,256]{1,0:T(8,128)(2,1)S(1)}, u32[]{:S(2)}, u32[]{:S(2)}) collective-permute-start(bf16[256,256]{1,0:T(8,128)(2,1)S(1)} %get-tuple-element.55), channel_id=1, source_target_pairs={{0,2},{1,3},{2,0},{3,1},{4,6},{5,7},{6,4},{7,5},{8,10},{9,11},{10,... | collective-permute-start | bytes 393224 | tf_op jit(solution)/shard_map/ppermute | solution.py:424
  97.2 3.1 %collective-permute-start.8 = (bf16[256,256]{1,0:T(8,128)(2,1)S(1)}, bf16[256,256]{1,0:T(8,128)(2,1)S(1)}, u32[]{:S(2)}, u32[]{:S(2)}) collective-permute-start(bf16[256,256]{1,0:T(8,128)(2,1)S(1)} %get-tuple-element.56), channel_id=1, source_target_pairs={{0,3},{1,0},{2,1},{3,2},{4,7},{5,4},{6,5},{7,6},{8,11},{9,8},{10,9... | collective-permute-start | bytes 393224 | tf_op jit(solution)/shard_map/ppermute | solution.py:424
  100.9 2.9 %input_gradients.1 = bf16[2,128,2048]{2,1,0:T(8,128)(2,1)} custom-call(s32[32]{0:T(128)} %copy-done.2, s32[1]{0:T(128)} %bitcast.10.me_ref, bf16[2,64,128]{2,1,0:T(8,128)(2,1)} %get-tuple-element.65.ranks_ref, bf16[16,144,128]{2,1,0:T(8,128)(2,1)} %copy-done, f32[256,2048]{1,0:T(8,128)} %copy-done.1), custom_call_target="tpu_custom_call" | custom-call | flops 67108864 | bytes 3145728 | tf_op jit(solution)/shard_map/input_gradients/pallas_call | solution.py:249
  103.8 1.5 %layer_outputs.1 = bf16[2,128,256]{2,1,0:T(8,128)(2,1)} custom-call(s32[32]{0:T(128)S(1)} %copy-done.3, s32[1]{0:T(128)} %bitcast.10.me_ref, bf16[2,64,128]{2,1,0:T(8,128)(2,1)S(1)} %get-tuple-element.64.ranks_ref, f32[2,64,256]{2,1,0:T(8,128)S(1)} %get-tuple-element.52.up_ref, bf16[256,256]{1,0:T(8,128)(2,1)S(1)} %get-tuple-element.53.refs_0_, ...), custom_call_target="tpu_custom_call" | custom-call | tf_op jit(solution)/shard_map/layer_outputs/pallas_call | solution.py:281
  105.3 2.2 %all-to-all-done.3.pieces_ref = bf16[16,2,32,256]{3,2,1,0:T(8,128)(2,1)S(1)} async-done(((bf16[16,2,32,256]{3,2,1,0:T(8,128)(2,1)}), bf16[16,2,32,256]{3,2,1,0:T(8,128)(2,1)S(1)}, u32[]{:S(2)}, u32[]{:S(2)}) %all-to-all-start.3) | async-done | bytes 524320 | tf_op jit(solution)/shard_map/all_to_all | solution.py:27
  107.5 0.8 slot_sums.3
  108.3 1.9 %collective-permute-start.9 = (f32[2,2,32,256]{3,2,1,0:T(8,128)S(1)}, f32[2,2,32,256]{3,2,1,0:T(8,128)S(1)}, u32[]{:S(2)}, u32[]{:S(2)}) collective-permute-start(f32[2,2,32,256]{3,2,1,0:T(8,128)S(1)} %slot_sums.3), channel_id=1, source_target_pairs={{0,4},{4,0},{8,12},{12,8},{16,20},{20,16},{24,28},{28,24},{32,36},... | collective-permute-start | bytes 393224 | tf_op jit(solution)/shard_map/ppermute | solution.py:434
  110.3 0.8 slot_sums.2.own_ref
  111.6 0.7 placed_sums.1
  (25 shorter events, 2.3 us)
Async XLA Ops:
  7.2 18.6 %copy-start.5 = (bf16[1,2,128,256]{3,2,1,0:T(8,128)(2,1)S(1)}, bf16[1,2,128,256]{3,2,1,0:T(8,128)(2,1)}, u32[]{:S(2)}) copy-start(bf16[1,2,128,256]{3,2,1,0:T(8,128)(2,1)} %param.8) | copy-start | bytes 393220
  7.2 70.3 %all-gather.3.cloned.1.call-start = ((), (), s32[]{:S(2)}) async-start(), calls=%async_computation.4 | async-start | bytes 4456448 | tf_op jit(solution)/shard_map/all_gather | solution.py:404
  9.4 33.5 %all-to-all-start = ((bf16[16,152,128]{2,1,0:T(8,128)(2,1)}), bf16[16,152,128]{2,1,0:T(8,128)(2,1)S(1)}, u32[]{:S(2)}, u32[]{:S(2)}) async-start(bf16[16,152,128]{2,1,0:T(8,128)(2,1)} %packed_adapters.1), calls=%async_computation | async-start | bytes 1245184 | tf_op jit(solution)/shard_map/all_to_all | solution.py:27
  22.6 22.3 %collective-permute-start = (bf16[1,1,128,2048]{3,2,1,0:T(8,128)(2,1)S(1)}, bf16[1,1,128,2048]{3,2,1,0:T(8,128)(2,1)S(1)}, u32[]{:S(2)}, u32[]{:S(2)}) collective-permute-start(bf16[1,1,128,2048]{3,2,1,0:T(8,128)(2,1)S(1)} %get-tuple-element.63), channel_id=1, source_target_pairs={{0,64},{64,128},{128,192},{192,256},{256,320},{320,384},{384,448},... | collective-permute-start | bytes 1572872 | tf_op jit(solution)/shard_map/ppermute | solution.py:23
  25.8 6.6 %collective-permute-start.1 = (bf16[1,2,128,256]{3,2,1,0:T(8,128)(2,1)S(1)}, bf16[1,2,128,256]{3,2,1,0:T(8,128)(2,1)S(1)}, u32[]{:S(2)}, u32[]{:S(2)}) collective-permute-start(bf16[1,2,128,256]{3,2,1,0:T(8,128)(2,1)S(1)} %copy-done.5), channel_id=1, source_target_pairs={{0,448},{64,0},{128,64},{192,128},{256,192},{320,256},{384,320},{4... | collective-permute-start | bytes 393224 | tf_op jit(solution)/shard_map/ppermute | solution.py:23
  32.4 12.4 %collective-permute-start.2 = (bf16[256,256]{1,0:T(8,128)(2,1)S(1)}, bf16[256,256]{1,0:T(8,128)(2,1)S(1)}, u32[]{:S(2)}, u32[]{:S(2)}) collective-permute-start(bf16[256,256]{1,0:T(8,128)(2,1)S(1)} %bitcast.24), channel_id=1, source_target_pairs={{0,1},{1,2},{2,3},{3,0},{4,5},{5,6},{6,7},{7,4},{8,9},{9,10},{10,1... | collective-permute-start | bytes 393224 | tf_op jit(solution)/shard_map/ppermute | solution.py:397
  43.4 39.1 %copy-start.2 = (s32[32]{0:T(128)}, s32[32]{0:T(128)S(1)}, u32[]{:S(2)}) copy-start(s32[32]{0:T(128)S(1)} %reshape.32.slots_ref.marks_ref) | copy-start | bytes 388
  44.9 27.4 %all-to-all-start.1 = ((bf16[16,144,128]{2,1,0:T(8,128)(2,1)}), bf16[16,144,128]{2,1,0:T(8,128)(2,1)S(1)}, u32[]{:S(2)}, u32[]{:S(2)}) async-start(bf16[16,144,128]{2,1,0:T(8,128)(2,1)} %selected_pieces.1), calls=%async_computation.1 | async-start | bytes 1179648 | tf_op jit(solution)/shard_map/all_to_all | solution.py:27
  48.7 23.7 %collective-permute-start.5 = (bf16[1,1,128,2048]{3,2,1,0:T(8,128)(2,1)S(1)}, bf16[1,1,128,2048]{3,2,1,0:T(8,128)(2,1)S(1)}, u32[]{:S(2)}, u32[]{:S(2)}) collective-permute-start(bf16[1,1,128,2048]{3,2,1,0:T(8,128)(2,1)S(1)} %get-tuple-element.62), channel_id=1, source_target_pairs={{0,64},{64,128},{128,192},{192,256},{256,320},{320,384},{384,448},... | collective-permute-start | bytes 1572872 | tf_op jit(solution)/shard_map/ppermute | solution.py:23
  51.9 8.1 %collective-permute-start.3 = (bf16[256,256]{1,0:T(8,128)(2,1)S(1)}, bf16[256,256]{1,0:T(8,128)(2,1)S(1)}, u32[]{:S(2)}, u32[]{:S(2)}) collective-permute-start(bf16[256,256]{1,0:T(8,128)(2,1)S(1)} %bitcast.25), channel_id=1, source_target_pairs={{0,2},{1,3},{2,0},{3,1},{4,6},{5,7},{6,4},{7,5},{8,10},{9,11},{10,... | collective-permute-start | bytes 393224 | tf_op jit(solution)/shard_map/ppermute | solution.py:397
  56.5 6.4 %collective-permute-start.4 = (bf16[256,256]{1,0:T(8,128)(2,1)S(1)}, bf16[256,256]{1,0:T(8,128)(2,1)S(1)}, u32[]{:S(2)}, u32[]{:S(2)}) collective-permute-start(bf16[256,256]{1,0:T(8,128)(2,1)S(1)} %bitcast.26), channel_id=1, source_target_pairs={{0,3},{1,0},{2,1},{3,2},{4,7},{5,4},{6,5},{7,6},{8,11},{9,8},{10,9... | collective-permute-start | bytes 393224 | tf_op jit(solution)/shard_map/ppermute | solution.py:397
  72.3 10.1 %copy-start = (bf16[16,144,128]{2,1,0:T(8,128)(2,1)}, bf16[16,144,128]{2,1,0:T(8,128)(2,1)S(1)}, u32[]{:S(2)}) copy-start(bf16[16,144,128]{2,1,0:T(8,128)(2,1)S(1)} %all-to-all-done.1.second_ref.down_ref) | copy-start | bytes 1769476
  73.5 10.3 %all-to-all-start.2 = ((bf16[4,2,2,64,128]{4,3,2,1,0:T(8,128)(2,1)}), bf16[4,2,2,64,128]{4,3,2,1,0:T(8,128)(2,1)S(1)}, u32[]{:S(2)}, u32[]{:S(2)}) async-start(bf16[4,2,2,64,128]{4,3,2,1,0:T(8,128)(2,1)} %get-tuple-element.38), calls=%async_computation.2 | async-start | bytes 524288 | tf_op jit(solution)/shard_map/all_to_all | solution.py:27
  77.5 2.2 %copy-start.4 = (bf16[1024,2048]{1,0:T(8,128)(2,1)S(1)}, bf16[1024,2048]{1,0:T(8,128)(2,1)}, u32[]{:S(2)}) copy-start(bf16[1024,2048]{1,0:T(8,128)(2,1)} %all-gather.3.cloned.1.call-done) | copy-start | bytes 12582916
  82.4 1.4 %copy-start.1 = (f32[256,2048]{1,0:T(8,128)}, f32[256,2048]{1,0:T(8,128)S(1)}, u32[]{:S(2)}) copy-start(f32[256,2048]{1,0:T(8,128)S(1)} %get-tuple-element.51.product_ref) | copy-start | bytes 6291460
  83.8 20.0 %copy-start.3 = (s32[32]{0:T(128)S(1)}, s32[32]{0:T(128)}, u32[]{:S(2)}) copy-start(s32[32]{0:T(128)} %copy-done.2) | copy-start | bytes 388
  84.8 22.7 %all-to-all-start.3 = ((bf16[16,2,32,256]{3,2,1,0:T(8,128)(2,1)}), bf16[16,2,32,256]{3,2,1,0:T(8,128)(2,1)S(1)}, u32[]{:S(2)}, u32[]{:S(2)}) async-start(bf16[16,2,32,256]{3,2,1,0:T(8,128)(2,1)} %get-tuple-element.49), calls=%async_computation.3 | async-start | bytes 1048576 | tf_op jit(solution)/shard_map/all_to_all | solution.py:27
  90.1 13.7 %collective-permute-start.6 = (bf16[256,256]{1,0:T(8,128)(2,1)S(1)}, bf16[256,256]{1,0:T(8,128)(2,1)S(1)}, u32[]{:S(2)}, u32[]{:S(2)}) collective-permute-start(bf16[256,256]{1,0:T(8,128)(2,1)S(1)} %get-tuple-element.54), channel_id=1, source_target_pairs={{0,1},{1,2},{2,3},{3,0},{4,5},{5,6},{6,7},{7,4},{8,9},{9,10},{10,1... | collective-permute-start | bytes 393224 | tf_op jit(solution)/shard_map/ppermute | solution.py:424
  92.9 10.9 %collective-permute-start.7 = (bf16[256,256]{1,0:T(8,128)(2,1)S(1)}, bf16[256,256]{1,0:T(8,128)(2,1)S(1)}, u32[]{:S(2)}, u32[]{:S(2)}) collective-permute-start(bf16[256,256]{1,0:T(8,128)(2,1)S(1)} %get-tuple-element.55), channel_id=1, source_target_pairs={{0,2},{1,3},{2,0},{3,1},{4,6},{5,7},{6,4},{7,5},{8,10},{9,11},{10,... | collective-permute-start | bytes 393224 | tf_op jit(solution)/shard_map/ppermute | solution.py:424
  97.2 6.6 %collective-permute-start.8 = (bf16[256,256]{1,0:T(8,128)(2,1)S(1)}, bf16[256,256]{1,0:T(8,128)(2,1)S(1)}, u32[]{:S(2)}, u32[]{:S(2)}) collective-permute-start(bf16[256,256]{1,0:T(8,128)(2,1)S(1)} %get-tuple-element.56), channel_id=1, source_target_pairs={{0,3},{1,0},{2,1},{3,2},{4,7},{5,4},{6,5},{7,6},{8,11},{9,8},{10,9... | collective-permute-start | bytes 393224 | tf_op jit(solution)/shard_map/ppermute | solution.py:424
  108.3 3.2 %collective-permute-start.9 = (f32[2,2,32,256]{3,2,1,0:T(8,128)S(1)}, f32[2,2,32,256]{3,2,1,0:T(8,128)S(1)}, u32[]{:S(2)}, u32[]{:S(2)}) collective-permute-start(f32[2,2,32,256]{3,2,1,0:T(8,128)S(1)} %slot_sums.3), channel_id=1, source_target_pairs={{0,4},{4,0},{8,12},{12,8},{16,20},{20,16},{24,28},{28,24},{32,36},... | collective-permute-start | bytes 393224 | tf_op jit(solution)/shard_map/ppermute | solution.py:434
Sparse Core Ops, SparseCore 0:
  10.1 66.2 all-gather.2
